TPU v7x, 32 devices: a whole 2x2x4 slice. The times are simulated.
32 devices in a mesh: wide: 16 (over z, y, x), narrow: 2 (over core).
Axes of the slice: x: 2, y: 2, z: 4, core: 2. Of those that a mesh axis runs over, the one named last changes fastest.
Arguments:
- incoming_activations: bfloat16 [32768, 768], P(('wide', 'narrow')), may hold values from -6 to 6
- span_identifiers: int32 [64, 512], P(('wide', 'narrow')), may hold values from 0 to 7, never falling along the last dimension, each value on 1 to 128 neighbouring positions
- partner_global_index: int32 [512], replicated, may hold values from 0 to 511, as said below
- softmax_coolness: float32 [1], replicated, may hold values from 0.03 to 0.06
- triple_kernel_panel: bfloat16 [768, 2304], replicated, may hold values from -0.21875 to 0.21875
- asking_shift: float32 [768], replicated, may hold values from -0.6 to 0.6
- content_shift: float32 [768], replicated, may hold values from -0.6 to 0.6
- mixer_result_kernel: bfloat16 [768, 768], replicated, may hold values from -1.75 to 1.75
- mixer_result_shift: float32 [768], replicated, may hold values from -0.6 to 0.6
- initial_standardize_scale: float32 [768], replicated, may hold values from 0.5 to 1.5
- initial_standardize_shift: float32 [768], replicated, may hold values from -0.6 to 0.6
- perceptron_entry_kernel: bfloat16 [768, 3072], replicated, may hold values from -0.21875 to 0.21875
- perceptron_entry_shift: float32 [3072], replicated, may hold values from -0.6 to 0.6
- perceptron_result_kernel: bfloat16 [3072, 768], replicated, may hold values from -0.109375 to 0.109375
- perceptron_result_shift: float32 [768], replicated, may hold values from -0.6 to 0.6
- later_standardize_scale: float32 [768], replicated, may hold values from 0.5 to 1.5
- later_standardize_shift: float32 [768], replicated, may hold values from -0.6 to 0.6
Outputs:
- loss: float32 [1], replicated
- layer_out: bfloat16 [32768, 768], P(('wide', 'narrow'))
- input_grad: float32 [32768, 768], P(('wide', 'narrow'))
- attn_weight_grad: float32 [768, 2304], replicated
- query_bias_grad: float32 [768], replicated
- value_bias_grad: float32 [768], replicated
- merge_weight_grad: float32 [768, 768], replicated
- merge_bias_grad: float32 [768], replicated
- first_gain_grad: float32 [768], replicated
- first_shift_grad: float32 [768], replicated
- inner_weight_grad: float32 [768, 3072], replicated
- inner_bias_grad: float32 [3072], replicated
- outer_weight_grad: float32 [3072, 768], replicated
- outer_bias_grad: float32 [768], replicated
- second_gain_grad: float32 [768], replicated
- second_shift_grad: float32 [768], replicated
Inputs may be any that keep to these rules, and one draw needn't show every extreme that they name: `span_identifiers`: in each packed row the segment numbers never fall and every number below 8 occurs, none on more than 128 tokens. `partner_global_index`: a permutation of the segments with no segment its own partner.
All inputs are finite; a program needn't handle non-finite values.
Results may differ from a plain program's by a relative error of at most 0.008.
Values may be sent and summed in bfloat16 or wider, within the bound.
No kernel may reach another device: no remote copies, remote signals or barrier semaphores. Data moves between devices by JAX's collectives and lax.ppermute only.
A program may use at most 192 MiB of HBM per device.

v0:
```python
from functools import partial

import jax
import jax.numpy as jnp
from jax import lax
from jax.experimental import pallas as pl
from jax.experimental.pallas import tpu as pltpu
from jax.sharding import PartitionSpec as P

HEADS = 12
S_ROW = 8
BOTH = ("wide", "narrow")
BF = jnp.bfloat16
F32 = jnp.float32


def tie(values, *others):
    return lax.optimization_barrier((values, others))[0]


class Place:
    def __init__(self):
        self.wide, self.narrow = lax.axis_size("wide"), lax.axis_size("narrow")
        self.count = self.wide * self.narrow
        self.core = lax.axis_index("narrow")
        self.me = lax.axis_index("wide") * self.narrow + self.core
        bits = [self.narrow << i for i in range(self.wide.bit_length() - 1)]
        self.own = [(1, 1)]
        self.pairs = [bits[i : i + 2] for i in range(0, len(bits), 2)]
        first, second = bits[0], bits[1]
        self.stages = [[(first, second)], [(second, first)]]
        self.stages += [self.combine(pair) for pair in self.pairs[1:]]
        self.spread = [self.combine(pair) for pair in self.pairs[::-1]] + [self.own]

    def combine(self, bits):
        if len(bits) == 1:
            return [(bits[0],) * 2]
        return [(m, m) for m in (bits[0], bits[1], bits[0] | bits[1])]

    def exchange(self, value, masks):
        pairs = [(i, i ^ masks[i % 2]) for i in range(self.count)]
        return lax.ppermute(value, BOTH, pairs)

    def index(self, stage):
        bit = lambda mask: (self.me // mask) % 2
        if len(stage) == 1:
            one, other = stage[0]
            return bit(one) if one == other else jnp.where(self.core == 0, bit(one), bit(other))
        return bit(stage[0][0]) + 2 * bit(stage[1][0])


class Sum:
    def __init__(self, place, send):
        self.place = place
        self.down, self.up = list(place.stages), list(place.stages[::-1]) + [place.own]
        self.sent = [send]
        self.got = [place.exchange(send, place.own[0])]
        self.stage = None

    def receive(self, order):
        got = [order.after(g) for g in self.got]
        if self.stage is None:
            return [self.kept] + got
        index = self.place.index(self.stage)
        parts = [self.kept] + got
        if len(parts) == 2:
            return [jnp.where(index == 0, jnp.concatenate(parts), jnp.concatenate(parts[::-1]))]
        ordered = []
        for at in range(len(parts)):
            value = parts[0]
            for i in range(1, len(parts)):
                value = jnp.where(index == at ^ i, parts[i], value)
            ordered.append(value)
        return [jnp.concatenate(ordered)]

    def advance(self, order):
        if not self.up:
            return
        terms = self.receive(order)
        if self.down:
            stage = self.down.pop(0)
            parts = len(stage) + 1
            index = self.place.index(stage)
            size = terms[0].shape[0] // parts
            cut = lambda at: sum(
                lax.dynamic_slice_in_dim(t, at * size, size).astype(F32) for t in terms
            )
            self.sent = [cut(index ^ (i + 1)).astype(BF) for i in range(len(stage))]
            self.kept = cut(index)
        else:
            self.stage = stage = self.up.pop(0)
            self.kept = sum(t.astype(F32) for t in terms).astype(BF) if len(terms) > 1 else terms[0]
            self.sent = [self.kept] * len(stage)
        self.got = [self.place.exchange(s, m) for s, m in zip(self.sent, stage)]
        order.done(*self.sent)


class Order:
    def __init__(self):
        self.last = ()

    def after(self, value):
        return tie(value, *self.last)

    def done(self, *values):
        self.last = values


def add_everywhere(total, place, order):
    for stage in [place.own] + place.spread[:-1]:
        got = [place.exchange(total, masks) for masks in stage]
        order.done(total)
        yield
        for part in got:
            total = total + order.after(part)
    order.done(total)
    yield total


def nt_dot(left, right):
    return lax.dot_general(left, right, (((1,), (1,)), ((), ())), preferred_element_type=F32)


def tn_dot(left, right):
    return lax.dot_general(left, right, (((0,), (0,)), ((), ())), preferred_element_type=F32)


def thirds(value):
    top = value.astype(BF)
    rest = value - top.astype(F32)
    middle = rest.astype(BF)
    return top, middle, (rest - middle.astype(F32)).astype(BF)


def column_sum(value):
    return jnp.sum(value, axis=0, keepdims=True)


def contrast_into(block, masks, me, cool_ref, pick_ref, there_ref, own_ref, partner_ref, loss_ref, grad_ref,
                  all_ref, sums_ref, rnorm_ref):
    count, width_all = all_ref.shape
    owned = own_ref.shape[0]
    for position, mask in enumerate(masks):
        at = pl.multiple_of((me ^ mask) * owned, owned)
        all_ref[pl.ds(at, owned), :] = there_ref[position * owned : (position + 1) * owned, :]
    widths = [width_all * f // 12 for f in (1, 2, 4, 8, 12)]
    warm = 1.0 / cool_ref[0]
    lane = lax.broadcasted_iota(jnp.int32, (1, 128), 1)
    first_mask = (lane < widths[0]).astype(F32)
    spans = [(0, 128, True), (0, 128, False), (128, widths[2], False), (widths[2], widths[3], False),
             (widths[3], widths[4], False)]
    partner = partner_ref[...][None, :]

    squares = jnp.zeros((8, count), F32)
    for index, (lo, hi, masked) in enumerate(spans):
        part = all_ref[:, lo:hi].astype(F32)
        if masked:
            part = part * first_mask
        term = sum(nt_dot(jnp.ones((8, hi - lo), BF), p) for p in thirds(part * part))
        squares = term if index <= 1 else squares + term
        rnorm_ref[index] = lax.rsqrt(squares[:1] + 1e-06)
    sums_ref[...] = jnp.zeros_like(sums_ref)
    hits = jnp.zeros((1, count), F32)
    for b in range(count // block):
        rows = pl.ds(b * block, block)
        row = lax.broadcasted_iota(jnp.int32, (block, count), 0) + b * block
        diagonal = row == lax.broadcasted_iota(jnp.int32, (block, count), 1)
        positive = row == partner
        gram = norms = None
        for index, (lo, hi, masked) in enumerate(spans):
            mine = all_ref[rows, lo:hi]
            if masked:
                mine = mine * first_mask.astype(BF)
            wide = mine.astype(F32)
            term = nt_dot(mine, all_ref[:, lo:hi])
            square = jnp.sum(wide * wide, axis=1, keepdims=True)
            gram, norms = (term, square) if index <= 1 else (gram + term, norms + square)
            scores = gram * (lax.rsqrt(norms + 1e-06) * warm) * rnorm_ref[index]
            sums_ref[index] += column_sum(jnp.where(diagonal, 0.0, jnp.exp(scores)))
            hits += column_sum(jnp.where(positive, scores, 0.0))
    logs = -hits
    for index in range(5):
        logs += jnp.log(sums_ref[index])
    loss_ref[...] = jnp.sum(logs, axis=1, keepdims=True)

    first = me * owned
    col = lax.broadcasted_iota(jnp.int32, (owned, count), 1)
    line = lax.broadcasted_iota(jnp.int32, (owned, count), 0)
    chosen = jnp.zeros((owned, count), jnp.int32)
    for i in range(owned):
        chosen = jnp.where(line == i, pick_ref[first + i], chosen)
    diagonal = line + first == col
    picks = (chosen == col).astype(F32) + (partner == line + first).astype(F32)
    gram = norms = None
    weights, inverses = [], []
    for index, (lo, hi, masked) in enumerate(spans):
        mine = own_ref[:, lo:hi]
        if masked:
            mine = mine * first_mask.astype(BF)
        wide = mine.astype(F32)
        term = nt_dot(mine, all_ref[:, lo:hi])
        square = jnp.sum(wide * wide, axis=1, keepdims=True)
        gram, norms = (term, square) if index <= 1 else (gram + term, norms + square)
        inverse = lax.rsqrt(norms + 1e-06)
        raised = jnp.where(diagonal, 0.0, jnp.exp(gram * (inverse * warm) * rnorm_ref[index]))
        own_sum = jnp.sum(raised, axis=1, keepdims=True)
        pull = raised * (1.0 / own_sum + 1.0 / sums_ref[index]) - picks
        weights.append(pull * (rnorm_ref[index] * warm))
        inverses.append(inverse)
    parts = jnp.dot(
        jnp.concatenate(thirds(jnp.concatenate(weights, axis=0)), axis=0), all_ref[...],
        preferred_element_type=F32,
    )
    unit_grads = parts[: 5 * owned] + parts[5 * owned : 10 * owned] + parts[10 * owned :]
    total = jnp.zeros((owned, width_all), F32)
    column = lax.broadcasted_iota(jnp.int32, (owned, width_all), 1)
    embed = own_ref[...].astype(F32)
    for index in range(5):
        inside = column < widths[index]
        mine = jnp.where(inside, embed, 0.0)
        grad = jnp.where(inside, unit_grads[index * owned : (index + 1) * owned], 0.0)
        along = jnp.sum(mine * grad, axis=1, keepdims=True)
        inverse = inverses[index]
        total += inverse * grad - (inverse * inverse * inverse * along) * mine
    grad_ref[...] = total


SEQUENCE = (
    "A0", "A", "I", "A", "B0", "B", "A", "T", "A", "B", "C0", "A", "C", "B", "A", "C", "B", "A",
    "C", "B", "C", "B", "X", "C", "S0", "B", "C", "S", "A", "BF", "S", "AF", "C", "SF", "C", "CF",
)

VMEM_LIMIT = 58 * 1024 * 1024


def kernel_call(body, name, flops, nbytes, **options):
    return pl.pallas_call(
        body,
        compiler_params=pltpu.CompilerParams(vmem_limit_bytes=VMEM_LIMIT),
        cost_estimate=pl.CostEstimate(flops=flops, bytes_accessed=nbytes, transcendentals=0),
        name=name,
        **options,
    )


def fixed(shape):
    return pl.BlockSpec(shape, lambda *_: (0,) * len(shape))


def windows(length, step=128):
    return [(at, max(0, at - step), min(length, at + 2 * step)) for at in range(0, length, step)]


def segment_row(seg_ref):
    return seg_ref[pl.ds(pl.program_id(0), 1), :].astype(F32)


def segment_column(seg):
    return jnp.broadcast_to(seg, (128, seg.shape[1])).T


def masks_into(bias_ref, seg_ref):
    seg = segment_row(seg_ref)
    column = segment_column(seg)
    for index, (at, lo, hi) in enumerate(windows(seg.shape[1])):
        same = column[lo:hi, :] == seg[:, at : at + 128]
        bias = jnp.where(same, 0.0, -1e9)
        bias_ref[index, : hi - lo, :] = jnp.concatenate([bias, bias], axis=1)


def pair_stack(two):
    lane = lax.broadcasted_iota(jnp.int32, two.shape, 1)
    nought = jnp.zeros_like(two)
    half = two.shape[1] // 2
    return jnp.concatenate(
        [jnp.where(lane < half, two, nought), jnp.where(lane < half, nought, two)], axis=0
    )


def pair_merge(both):
    size = both.shape[1] // 2
    row = lax.broadcasted_iota(jnp.int32, (both.shape[0], size), 0)
    return jnp.where(row < both.shape[0] // 2, both[:, :size], both[:, size:])


def attend_kernel(x_ref, seg_ref, w_ref, bq_ref, bv_ref, wo_ref, bo_ref, gain_ref,
                  shift_ref, q_ref, k_ref, v_ref, mixed_t_ref, lse_ref, hat_ref, rstd_ref, low_ref,
                  x_t_ref, low_t_ref, bias_ref, mixed_ref):
    length, width = x_ref.shape
    x = x_ref[...]
    masks_into(bias_ref, seg_ref)
    q = jnp.dot(x, w_ref[:, :width], preferred_element_type=F32) + bq_ref[...][None, :]
    q_ref[...] = (q.astype(BF).astype(F32) * (width // HEADS) ** -0.5).astype(BF)
    k_ref[...] = jnp.dot(x, w_ref[:, width : 2 * width], preferred_element_type=F32).astype(BF)
    v_ref[...] = (jnp.dot(x, w_ref[:, 2 * width :], preferred_element_type=F32) + bv_ref[...][None, :]).astype(BF)
    jobs = [(pair, index) + win for pair in range(HEADS // 2) for index, win in enumerate(windows(length))]

    def scores(job):
        pair, index, at, lo, hi = job
        lanes = slice(pair * 128, pair * 128 + 128)
        stacked = pair_stack(q_ref[at : at + 128, lanes])
        return nt_dot(k_ref[lo:hi, lanes], stacked)

    ahead = scores(jobs[0])
    for number, job in enumerate(jobs):
        pair, index, at, lo, hi = job
        lanes = slice(pair * 128, pair * 128 + 128)
        raw = ahead
        if number + 1 < len(jobs):
            ahead = scores(jobs[number + 1])
        masked = raw + bias_ref[index, : hi - lo, :]
        top = jnp.max(masked, axis=0, keepdims=True)
        raised = jnp.exp(masked - top)
        total = jnp.sum(raised, axis=0, keepdims=True)
        log_total = top + jnp.log(total)
        for side in (0, 1):
            head = 2 * pair + side
            lse_ref[head // 4, head % 4 : head % 4 + 1, at : at + 128] = log_total[:, side * 128 : side * 128 + 128]
        both = tn_dot((raised * (1.0 / total)).astype(BF), v_ref[lo:hi, lanes])
        lane = lax.broadcasted_iota(jnp.int32, (128, 128), 1)
        merged = jnp.where(lane < 64, both[:128], both[128:])
        mixed_ref[at : at + 128, lanes] = merged.astype(BF)
        mixed_t_ref[lanes, at : at + 128] = merged.T.astype(BF)
    attn = jnp.dot(mixed_ref[...], wo_ref[...], preferred_element_type=F32) + bo_ref[...][None, :]
    total = x.astype(F32) + attn
    center = total - jnp.mean(total, axis=1, keepdims=True)
    rstd = lax.rsqrt(jnp.mean(center * center, axis=1, keepdims=True) + 1e-05)
    hat = center * rstd
    hat_ref[...] = hat
    rstd_ref[...] = rstd
    low = (hat * gain_ref[...][None, :] + shift_ref[...][None, :]).astype(BF)
    low_ref[...] = low
    low_t_ref[...] = low.T
    x_t_ref[...] = x.T


def attend(x, seg, w, bq, bv, wo, bo, gain, shift):
    tokens, width = x.shape
    rows, length = seg.shape
    row_block = lambda *tail: pl.BlockSpec((length,) + tail, lambda r: (r, 0))
    return kernel_call(
        attend_kernel, "attend", 2 * tokens * width * width * 4 + 4 * tokens * 384 * width * 2, 20 << 20,
        grid=(rows,),
        in_specs=[
            row_block(width), fixed(seg.shape), fixed(w.shape), fixed(bq.shape), fixed(bv.shape), fixed(wo.shape), fixed(bo.shape),
            fixed(gain.shape), fixed(shift.shape),
        ],
        out_specs=(
            row_block(width), row_block(width), row_block(width),
            pl.BlockSpec((width, length), lambda r: (0, r)),
            pl.BlockSpec((HEADS // 4, 4, length), lambda r: (r, 0, 0)),
            row_block(width), row_block(1), row_block(width),
            pl.BlockSpec((width, length), lambda r: (0, r)), pl.BlockSpec((width, length), lambda r: (0, r)),
        ),
        out_shape=(
            jax.ShapeDtypeStruct((tokens, width), BF), jax.ShapeDtypeStruct((tokens, width), BF),
            jax.ShapeDtypeStruct((tokens, width), BF), jax.ShapeDtypeStruct((width, tokens), BF),
            jax.ShapeDtypeStruct((rows * HEADS // 4, 4, length), F32), jax.ShapeDtypeStruct((tokens, width), F32),
            jax.ShapeDtypeStruct((tokens, 1), F32), jax.ShapeDtypeStruct((tokens, width), BF),
            jax.ShapeDtypeStruct((width, tokens), BF), jax.ShapeDtypeStruct((width, tokens), BF),
        ),
        scratch_shapes=[
            pltpu.VMEM((length // 128, 384, 256), F32), pltpu.VMEM((length, width), BF),
        ],
    )(x, seg, w, bq, bv, wo, bo, gain, shift)


def gelu_parts(v):
    bell = jnp.exp(v * v * -0.5)
    t = 1.0 / (1.0 + (0.3275911 * 0.5 ** 0.5) * jnp.abs(v))
    poly = ((((0.5 * 1.061405429 * t - 0.5 * 1.453152027) * t + 0.5 * 1.421413741) * t
             - 0.5 * 0.284496736) * t + 0.5 * 0.254829592) * t
    tail = poly * bell
    share = jnp.where(v >= 0.0, 1.0 - tail, tail)
    return v * share, share + v * bell * 0.3989422804014327


def feed_kernel(chunk, hat_ref, low_ref, seg_ref, gain1_ref, shift1_ref, w1_ref, b1_ref, w2_ref, b2_ref,
                gain_ref, shift_ref, act_t_ref, slope_ref, hat2_ref, rstd2_ref, out_ref, embed_ref,
                pooled_ref, value_ref):
    length, width = hat_ref.shape
    hidden = w1_ref.shape[1]
    low = low_ref[...]
    count = hidden // chunk

    def entry(i):
        return jnp.dot(low, w1_ref[:, i * chunk : (i + 1) * chunk], preferred_element_type=F32)

    total = hat_ref[...] * gain1_ref[...][None, :] + shift1_ref[...][None, :] + b2_ref[...][None, :]
    ahead = entry(0)
    for i in range(count):
        cols = slice(i * chunk, (i + 1) * chunk)
        inner = ahead + b1_ref[cols][None, :]
        if i + 1 < count:
            ahead = entry(i + 1)
        value, slope = gelu_parts(inner)
        value = value.astype(BF)
        act_t_ref[cols, :] = value.T
        slope_ref[:, cols] = slope.astype(BF)
        value_ref[:, cols] = value
    total += jnp.dot(value_ref[...], w2_ref[...], preferred_element_type=F32)
    center = total - jnp.mean(total, axis=1, keepdims=True)
    rstd = lax.rsqrt(jnp.mean(center * center, axis=1, keepdims=True) + 1e-05)
    hat = center * rstd
    hat2_ref[...] = hat
    rstd2_ref[...] = rstd
    out = hat * gain_ref[...][None, :] + shift_ref[...][None, :]
    out_ref[...] = out.astype(BF)
    number = lax.broadcasted_iota(jnp.int32, (S_ROW, length), 0)
    onehot = (segment_row(seg_ref) == number.astype(F32)).astype(F32)
    tokens_in = jnp.sum(onehot, axis=1, keepdims=True)
    onehot = onehot.astype(BF)
    sums = jnp.zeros((S_ROW, width), F32)
    for part in thirds(out):
        sums += jnp.dot(onehot, part, preferred_element_type=F32)
    row = pl.program_id(0)
    pooled_ref[pl.ds(row * S_ROW, S_ROW), :] = sums / tokens_in

    @pl.when(row == pl.num_programs(0) - 1)
    def _():
        embed_ref[...] = pooled_ref[...].astype(BF)


def feed(hat, low, seg, gain1, shift1, w1, b1, w2, b2, gain, shift):
    tokens, width = hat.shape
    rows, length = seg.shape
    hidden = w1.shape[1]
    row_block = lambda *tail: pl.BlockSpec((length,) + tail, lambda r: (r, 0))
    return kernel_call(
        partial(feed_kernel, 1024), "feed", 4 * tokens * width * hidden, 30 << 20,
        grid=(rows,),
        in_specs=[
            row_block(width), row_block(width), fixed(seg.shape),
        ] + [fixed(a.shape) for a in (gain1, shift1, w1, b1, w2, b2, gain, shift)],
        out_specs=(
            pl.BlockSpec((hidden, length), lambda r: (0, r)), row_block(hidden), row_block(width), row_block(1),
            row_block(width),
            fixed((rows * S_ROW, width)),
        ),
        out_shape=(
            jax.ShapeDtypeStruct((hidden, tokens), BF), jax.ShapeDtypeStruct((tokens, hidden), BF),
            jax.ShapeDtypeStruct((tokens, width), F32), jax.ShapeDtypeStruct((tokens, 1), F32),
            jax.ShapeDtypeStruct((tokens, width), BF), jax.ShapeDtypeStruct((rows * S_ROW, width), BF),
        ),
        scratch_shapes=[pltpu.VMEM((rows * S_ROW, width), F32), pltpu.VMEM((length, hidden), BF)],
    )(hat, low, seg, gain1, shift1, w1, b1, w2, b2, gain, shift)


def norm_back(grad, hat, rstd, gain):
    inside = grad * gain
    first = jnp.mean(inside, axis=1, keepdims=True)
    second = jnp.mean(inside * hat, axis=1, keepdims=True)
    return (inside - first - hat * second) * rstd


def line_into(ref, vectors):
    ref[...] = jnp.zeros_like(ref)
    at = 0
    for vector in vectors:
        ref[:, at : at + vector.shape[1]] = vector
        at += vector.shape[1]


def copies(pairs, sems):
    return [pltpu.make_async_copy(src, dst, sems.at[i]) for i, (src, dst) in enumerate(pairs)]


def outer_back_kernel(block, masks, info_ref, pick_ref, cool_ref, there_ref, own_ref, partner_ref, seg_ref, rstd_ref,
                      gain_ref, act_t_ref, hat_hbm, loss_ref, line_ref, send_ref,
                      keep_ref, second_hbm, outer_hbm, embed_grad_ref, all_ref, sums_ref, rnorm_ref,
                      hat_ref, second_ref, outer_ref, sems):
    step = pl.program_id(0)
    rows, length = seg_ref.shape
    width = gain_ref.shape[0]
    load, *store = copies([(hat_hbm, hat_ref), (second_ref, second_hbm), (outer_ref, outer_hbm)], sems)

    @pl.when(step == 0)
    def _():
        load.start()
        contrast_into(block, masks, info_ref[0], cool_ref, pick_ref, there_ref, own_ref, partner_ref,
                      loss_ref, embed_grad_ref, all_ref, sums_ref, rnorm_ref)
        load.wait()
        gains, shifts, biases = [], [], []
        for row in range(rows):
            span = slice(row * length, (row + 1) * length)
            seg = seg_ref[row : row + 1, :].astype(F32)
            number = lax.broadcasted_iota(jnp.int32, (S_ROW, length), 0).astype(F32)
            tokens_in = jnp.sum((seg == number).astype(F32), axis=1, keepdims=True)
            each = embed_grad_ref[row * S_ROW : (row + 1) * S_ROW, :] / tokens_in
            stack = [p.astype(F32) for p in thirds(each)] + [jnp.zeros((128 - 3 * S_ROW, width), F32)]
            lane = lax.broadcasted_iota(jnp.int32, (length, 128), 1)
            pick = (lane < 3 * S_ROW) & ((lane % S_ROW).astype(F32) == segment_column(seg))
            grad = jnp.dot(
                pick.astype(BF), jnp.concatenate(stack).astype(BF), preferred_element_type=F32
            )
            hat = hat_ref[span, :]
            second = norm_back(grad, hat, rstd_ref[span, :], gain_ref[...][None, :])
            low = second.astype(BF)
            second_ref[span, :] = second
            outer_ref[span, :] = low
            gains.append(column_sum(grad * hat))
            shifts.append(column_sum(grad))
            biases.append(column_sum(low.astype(F32)))
        line_into(line_ref, [sum(biases), sum(gains), sum(shifts)])
        for copy in store:
            copy.start()

    weight = jnp.dot(act_t_ref[...], outer_ref[...], preferred_element_type=F32).astype(BF)
    half = pl.num_programs(0) // 2

    @pl.when(step < half)
    def _():
        send_ref[...] = weight

    @pl.when(step >= half)
    def _():
        keep_ref[...] = weight

    @pl.when(step == pl.num_programs(0) - 1)
    def _():
        for copy in store:
            copy.wait()


def gather_embeds(own, place):
    there, masks = own, [0]
    for stage in place.spread:
        there = jnp.concatenate([there] + [place.exchange(there, pair) for pair in stage])
        masks = masks + [m ^ pair[0] for pair in stage for m in masks]
    return there, masks


def outer_back(own, partner, coolness, seg, hat, rstd, gain, act_t, place, chunk=768):
    there, masks = gather_embeds(own, place)
    owned, width = own.shape
    count = owned * len(masks)
    tokens = hat.shape[0]
    hidden = act_t.shape[0]
    steps = hidden // chunk
    half = steps // 2
    whole = lambda shape: pl.BlockSpec(shape, lambda i, *_: (0,) * len(shape))
    smem, hbm = pl.BlockSpec(memory_space=pltpu.SMEM), pl.BlockSpec(memory_space=pl.ANY)
    vmem = pl.BlockSpec(memory_space=pltpu.VMEM)
    turn = lambda i, info: (lax.rem(i + half * (1 - info[1]), steps), 0)
    return kernel_call(
        partial(outer_back_kernel, min(count, 256), masks), "outer_back", 2 * tokens * hidden * width, 20 << 20,
        grid_spec=pltpu.PrefetchScalarGridSpec(
            num_scalar_prefetch=1,
            grid=(steps,),
            in_specs=[smem, smem, vmem, vmem, whole(partner.shape), whole(seg.shape),
                      whole(rstd.shape), whole(gain.shape), pl.BlockSpec((chunk, tokens), turn), hbm],
            out_specs=(
                whole((1, 1)), whole((1, hidden)),
                pl.BlockSpec((chunk, width), lambda i, info: (jnp.minimum(i, half - 1), 0)),
                pl.BlockSpec((chunk, width), lambda i, info: (jnp.maximum(i - half, 0), 0)), hbm, hbm,
            ),
            scratch_shapes=[
                pltpu.VMEM((owned, width), F32), pltpu.VMEM((count, width), BF), pltpu.VMEM((5, 1, count), F32),
                pltpu.VMEM((5, 1, count), F32), pltpu.VMEM((tokens, width), F32),
                pltpu.VMEM((tokens, width), F32), pltpu.VMEM((tokens, width), BF), pltpu.SemaphoreType.DMA((3,)),
            ],
        ),
        out_shape=(
            jax.ShapeDtypeStruct((1, 1), F32), jax.ShapeDtypeStruct((1, hidden), F32),
            jax.ShapeDtypeStruct((hidden // 2, width), BF), jax.ShapeDtypeStruct((hidden // 2, width), BF),
            jax.ShapeDtypeStruct((tokens, width), F32), jax.ShapeDtypeStruct((tokens, width), BF),
        ),
    )(jnp.stack([place.me, place.core]), partner, coolness, there, own, partner, seg, rstd, gain, act_t, hat)


def inner_back_kernel(rows, info_ref, outer_ref, low_t_ref, slope_ref, w2_ref, w1_ref, rstd_ref, gain_ref, second_hbm,
                      hat_hbm, mixed_t_hbm, wo_hbm, send_ref, keep_ref, bias_ref, mixed_grad_ref, merge_ref, line_ref,
                      first_hbm,
                      normed_ref, second_ref, hat_ref, mixed_t_ref, wo_ref, sems, out_sems):
    step, last = pl.program_id(0), pl.num_programs(0) - 1
    length = outer_ref.shape[0] // rows
    loads = copies([(second_hbm, second_ref), (hat_hbm, hat_ref), (mixed_t_hbm, mixed_t_ref), (wo_hbm, wo_ref)], sems)

    @pl.when(step == 0)
    def _():
        for copy in loads:
            copy.start()

    active = nt_dot(outer_ref[...], w2_ref[...])
    inner = (active * slope_ref[...].astype(F32)).astype(BF)
    bias_ref[...] = column_sum(inner.astype(F32))
    weight = jnp.dot(low_t_ref[...], inner, preferred_element_type=F32).astype(BF)
    normed = nt_dot(inner, w1_ref[...])

    @pl.when(step <= last // 2)
    def _():
        send_ref[...] = weight

    @pl.when(step > last // 2)
    def _():
        keep_ref[...] = weight

    @pl.when(step == 0)
    def _():
        normed_ref[...] = normed

    @pl.when(step > 0)
    def _():
        normed_ref[...] += normed

    @pl.when(step == last)
    def _():
        for copy in loads:
            copy.wait()
        gains, shifts, biases, merges, stores = [], [], [], [], []
        for row in range(rows):
            span = slice(row * length, (row + 1) * length)
            hat = hat_ref[span, :]
            grad = normed_ref[span, :] + second_ref[span, :]
            first = norm_back(grad, hat, rstd_ref[span, :], gain_ref[...][None, :])
            normed_ref[span, :] = first
            store = pltpu.make_async_copy(normed_ref.at[span, :], first_hbm.at[span, :], out_sems.at[row])
            store.start()
            stores.append(store)
            low = first.astype(BF)
            gains.append(column_sum(grad * hat))
            shifts.append(column_sum(grad))
            biases.append(column_sum(low.astype(F32)))
            mixed_grad_ref[span, :] = nt_dot(low, wo_ref[...]).astype(BF)
            merges.append(jnp.dot(mixed_t_ref[:, span], low, preferred_element_type=F32))
        merge_ref[...] = sum(merges).astype(BF)
        line_into(line_ref, [sum(biases), sum(gains), sum(shifts)])
        for store in stores:
            store.wait()


def inner_back(outer, second, low_t, slope, w2, w1, hat, rstd, gain, mixed_t, wo, rows, place, chunk=512):
    tokens, width = outer.shape
    hidden = slope.shape[1]
    steps = hidden // chunk
    half = steps // 2
    whole = lambda shape: pl.BlockSpec(shape, lambda i, *_: (0,) * len(shape))
    hbm = pl.BlockSpec(memory_space=pl.ANY)
    turn = lambda i, info: lax.rem(i + half * (1 - info[1]), steps)
    early = lambda i: jnp.minimum(i, half - 1)
    late = lambda i: jnp.maximum(i - half, 0)
    line = jax.ShapeDtypeStruct((1, hidden), F32)
    part = jax.ShapeDtypeStruct((half * width, chunk), BF)
    return kernel_call(
        partial(inner_back_kernel, rows), "inner_back", 6 * tokens * hidden * width, 40 << 20,
        grid_spec=pltpu.PrefetchScalarGridSpec(
            num_scalar_prefetch=1,
            grid=(steps,),
            in_specs=[
                whole(outer.shape), whole(low_t.shape),
                pl.BlockSpec((tokens, chunk), lambda i, info: (0, turn(i, info))),
                pl.BlockSpec((chunk, width), lambda i, info: (turn(i, info), 0)),
                pl.BlockSpec((width, chunk), lambda i, info: (0, turn(i, info))),
                whole(rstd.shape), whole(gain.shape), hbm, hbm, hbm, hbm,
            ],
            out_specs=(
                pl.BlockSpec((width, chunk), lambda i, info: (early(i), 0)),
                pl.BlockSpec((width, chunk), lambda i, info: (late(i), 0)),
                pl.BlockSpec((1, chunk), lambda i, info: (0, turn(i, info))),
                whole((tokens, width)), whole((width, width)), whole((1, hidden)), hbm,
            ),
            scratch_shapes=[
                pltpu.VMEM((tokens, width), F32), pltpu.VMEM((tokens, width), F32), pltpu.VMEM((tokens, width), F32),
                pltpu.VMEM(mixed_t.shape, BF), pltpu.VMEM(wo.shape, BF), pltpu.SemaphoreType.DMA((4,)),
                pltpu.SemaphoreType.DMA((rows,)),
            ],
        ),
        out_shape=(
            part, part, line, jax.ShapeDtypeStruct((tokens, width), BF),
            jax.ShapeDtypeStruct((width, width), BF), line,
            jax.ShapeDtypeStruct((tokens, width), F32),
        ),
    )(jnp.stack([place.me, place.core]), outer, low_t, slope, w2, w1, rstd, gain, second, hat, mixed_t, wo)


def attend_back_kernel(pairs, core_ref, x_t_ref, merge_ref, seg_ref, lse_ref, q_ref, k_ref, v_ref, grad_ref,
                       dq_ref, dk_ref, dv_ref, send_ref, keep_ref, line_ref,
                       bias_ref, k_sum_ref, v_sum_ref, weight_ref):
    row = pl.program_id(0)
    length = q_ref.shape[0]
    masks_into(bias_ref, seg_ref)
    k_sum_ref[...] = jnp.zeros_like(k_sum_ref)
    v_sum_ref[...] = jnp.zeros_like(v_sum_ref)
    jobs = [(pair, index) + win for pair in range(pairs) for index, win in enumerate(windows(length))]

    def begin(job):
        pair, index, at, lo, hi = job
        lanes = slice(pair * 128, pair * 128 + 128)
        query = pair_stack(q_ref[at : at + 128, lanes])
        grad = pair_stack(grad_ref[at : at + 128, lanes])
        return query, grad, nt_dot(k_ref[lo:hi, lanes], query), nt_dot(v_ref[lo:hi, lanes], grad)

    ahead = begin(jobs[0])
    for number, job in enumerate(jobs):
        pair, index, at, lo, hi = job
        lanes = slice(pair * 128, pair * 128 + 128)
        query, grad, raw, prob_grad = ahead
        if number + 1 < len(jobs):
            ahead = begin(jobs[number + 1])
        log_total = jnp.concatenate(
            [lse_ref[head // 4, head % 4 : head % 4 + 1, at : at + 128] for head in (2 * pair, 2 * pair + 1)],
            axis=1
        )
        probs = jnp.exp(raw + bias_ref[index, : hi - lo, :] - log_total)
        weighed = probs * prob_grad
        raw_grad = (weighed - probs * jnp.sum(weighed, axis=0, keepdims=True)).astype(BF)
        v_sum_ref[lo:hi, lanes] += jnp.dot(probs.astype(BF), grad, preferred_element_type=F32)
        k_sum_ref[lo:hi, lanes] += jnp.dot(raw_grad, query, preferred_element_type=F32)
        if index == 0:
            keys_t = k_ref[:, lanes].T
        both = jnp.dot(keys_t[:, lo:hi], raw_grad, preferred_element_type=F32)
        merged = pair_merge(both) * 0.125
        dq_ref[at : at + 128, lanes] = merged.T.astype(BF)
    dk_ref[...] = k_sum_ref[...].astype(BF)
    dv_ref[...] = v_sum_ref[...].astype(BF)

    @pl.when(row == 0)
    def _():
        for ref in (weight_ref, line_ref):
            ref[...] = jnp.zeros_like(ref)

    width = dq_ref.shape[1]
    line_ref[:, :width] += column_sum(dq_ref[...].astype(F32))
    line_ref[:, width : 2 * width] += column_sum(dv_ref[...].astype(F32))
    for index, ref in enumerate((dq_ref, dk_ref, dv_ref)):
        weight_ref[index] += jnp.dot(x_t_ref[...], ref[...], preferred_element_type=F32)

    @pl.when(row == pl.num_programs(0) - 1)
    def _():
        for mine, first, second in ((0, keep_ref, send_ref), (1, send_ref, keep_ref)):
            @pl.when(core_ref[0] == mine)
            def _(first=first, second=second):
                first[...] = weight_ref[:2].astype(BF)
                second[0] = weight_ref[2].astype(BF)
                second[1] = merge_ref[...]


def attend_back(x_t, merge, seg, lse, q, k, v, grad, place):
    tokens, width = q.shape
    rows, length = seg.shape
    part = pl.BlockSpec((length, width), lambda r, core: (r, 0))
    whole = lambda shape: pl.BlockSpec(shape, lambda i, *_: (0,) * len(shape))
    groups = HEADS // 4
    half = jax.ShapeDtypeStruct((2, width, width), BF)
    return kernel_call(
        partial(attend_back_kernel, HEADS // 2), "attend_back",
        10 * tokens * 384 * width * 2 + 6 * tokens * width * width, 30 << 20,
        grid_spec=pltpu.PrefetchScalarGridSpec(
            num_scalar_prefetch=1,
            grid=(rows,),
            in_specs=[
                pl.BlockSpec((width, length), lambda r, core: (0, r)), whole(merge.shape), whole(seg.shape),
                pl.BlockSpec((groups, 4, length), lambda r, core: (r, 0, 0)), part, part, part, part,
            ],
            out_specs=(part, part, part, whole(half.shape), whole(half.shape), whole((1, 4 * width))),
            scratch_shapes=[
                pltpu.VMEM((length // 128, 384, 256), F32), pltpu.VMEM((length, width), F32),
                pltpu.VMEM((length, width), F32), pltpu.VMEM((3, width, width), F32),
            ],
        ),
        out_shape=(jax.ShapeDtypeStruct((tokens, width), BF),) * 3
        + (half, half, jax.ShapeDtypeStruct((1, 4 * width), F32)),
    )(place.core.reshape(1), x_t, merge, seg, lse, q, k, v, grad)


def input_back_kernel(first_ref, *refs):
    *grads, w_ref, out_ref = refs
    width = first_ref.shape[1]
    total = first_ref[...]
    for index, ref in enumerate(grads):
        total += nt_dot(ref[...], w_ref[:, index * width : (index + 1) * width])
    out_ref[...] = total


def input_back(first, grads, w, block=512):
    tokens, width = first.shape
    rows = lambda cols: pl.BlockSpec((block, cols), lambda i: (i, 0))
    return kernel_call(
        input_back_kernel, "input_back", 6 * tokens * width * width, 15 << 20,
        grid=(tokens // block,),
        in_specs=[rows(width)] + [rows(g.shape[1]) for g in grads] + [fixed(w.shape)],
        out_specs=rows(width),
        out_shape=jax.ShapeDtypeStruct((tokens, width), F32),
    )(first, *grads, w)


def finish_kernel(plan, core_ref, kept_ref, got_ref, *refs):
    *outs, out_ref, out_sems = refs
    core = core_ref[0]
    rows = out_ref.shape[1]
    stores = []
    for index, (kind, at, target) in enumerate(plan):
        span = slice(at * rows, (at + 1) * rows)
        kept, got = kept_ref[span, :].astype(F32), got_ref[span, :].astype(F32)
        own = core == (0 if kind == "low" else 1)
        out_ref[index] = kept if kind == "kept" else got if kind == "got" else jnp.where(own, kept, got)
        stores.append(pltpu.make_async_copy(out_ref.at[index], target(outs, core), out_sems.at[index]))
        stores[-1].start()
    for store in stores:
        store.wait()


def finish(one, order, place, rows, plan, shapes):
    while one.up:
        one.advance(order)
    kept, got = one.kept, order.after(one.got[0])
    half, cols = kept.shape
    hbm = pl.BlockSpec(memory_space=pl.ANY)
    result = kernel_call(
        partial(finish_kernel, plan), "finish", 0, half * cols * 12,
        in_specs=[pl.BlockSpec(memory_space=pltpu.SMEM)] + [pl.BlockSpec(memory_space=pltpu.VMEM)] * 2,
        out_specs=[hbm] * len(shapes),
        out_shape=[jax.ShapeDtypeStruct(shape, F32) for shape in shapes],
        scratch_shapes=[
            pltpu.VMEM((len(plan), rows, cols), F32), pltpu.SemaphoreType.DMA((len(plan),)),
        ],
    )(place.core.reshape(1), kept, got)
    order.done(*result)
    return result


def on_device(
    incoming_activations,
    span_identifiers,
    partner_global_index,
    softmax_coolness,
    triple_kernel_panel,
    asking_shift,
    content_shift,
    mixer_result_kernel,
    mixer_result_shift,
    initial_standardize_scale,
    initial_standardize_shift,
    perceptron_entry_kernel,
    perceptron_entry_shift,
    perceptron_result_kernel,
    perceptron_result_shift,
    later_standardize_scale,
    later_standardize_shift,
):
    rows, length = span_identifiers.shape
    width = incoming_activations.shape[1]
    hidden = perceptron_entry_kernel.shape[1]
    place, order = Place(), Order()
    seg = span_identifiers
    q, k, v, mixed_t, lse, hat1, rstd1, low, x_t, low_t = attend(
        incoming_activations, seg, triple_kernel_panel, asking_shift, content_shift, mixer_result_kernel,
        mixer_result_shift, initial_standardize_scale, initial_standardize_shift,
    )
    act_t, slope, hat2, rstd2, layer_out, embed = feed(
        hat1, low, seg, initial_standardize_scale, initial_standardize_shift, perceptron_entry_kernel,
        perceptron_entry_shift, perceptron_result_kernel, perceptron_result_shift, later_standardize_scale,
        later_standardize_shift,
    )
    (
        loss, second_line, outer_send, outer_keep, second, outer,
    ) = outer_back(
        embed, partner_global_index, softmax_coolness, seg, hat2, rstd2, later_standardize_scale, act_t, place
    )
    order.done(outer)
    got, sums, blocks = {}, {}, hidden // 512 // 2

    def inner():
        (
            got["inner_send"], got["inner_keep"], got["inner_line"], got["mixed_grad"], got["merge"],
            got["first_line"], got["first"],
        ) = inner_back(
            order.after(outer), second, low_t, slope, perceptron_result_kernel, perceptron_entry_kernel, hat1,
            rstd1, initial_standardize_scale, mixed_t, mixer_result_kernel, rows, place,
        )
        order.done(got["mixed_grad"])

    def attention():
        *got["grads"], got["rest_send"], got["rest_keep"], got["rest_line"] = attend_back(
            x_t, got["merge"], seg, lse, q, k, v, order.after(got["mixed_grad"]), place
        )
        order.done(got["rest_send"])

    def inputs():
        got["input_grad"] = input_back(order.after(got["first"]), got["grads"], triple_kernel_panel)
        order.done(got["input_grad"])

    def start(name, send, keep):
        sums[name] = Sum(place, order.after(send))
        sums[name].kept = keep
        order.done(*sums[name].sent)

    def start_outer():
        start("A", outer_send, outer_keep)

    def start_inner():
        start("B", got["inner_send"], got["inner_keep"])

    def start_rest():
        start("C", got["rest_send"].reshape(2 * width, width), got["rest_keep"].reshape(2 * width, width))

    def start_small():
        lines = [second_line, got["inner_line"], got["first_line"], got["rest_line"]]
        small = jnp.concatenate(lines, axis=0)
        sums["S"] = add_everywhere(order.after(small), place, order)
        next(sums["S"])

    def small_step():
        got["small"] = next(sums["S"])

    def finish_small():
        while got.get("small") is None:
            small_step()

    def finish_outer():
        def lines(at, upper):
            def target(outs, core):
                half = core if upper else 1 - core
                return outs[0].at[pl.ds(pl.multiple_of((half * 4 + at) * (hidden // 8), hidden // 8), hidden // 8), :]
            return target
        plan = [("kept", i, lines(i, True)) for i in range(4)] + [("got", i, lines(i, False)) for i in range(4)]
        got["outer_grad"], = finish(sums["A"], order, place, hidden // 8, plan, [(hidden, width)])

    def finish_inner():
        def columns(at, upper):
            def target(outs, core):
                half = core if upper else 1 - core
                return outs[0].at[:, pl.ds(pl.multiple_of((half * blocks + at) * 512, 512), 512)]
            return target
        plan = [("kept", i, columns(i, True)) for i in range(blocks)]
        plan += [("got", i, columns(i, False)) for i in range(blocks)]
        got["inner_grad"], = finish(sums["B"], order, place, width, plan, [(width, hidden)])

    def finish_rest():
        whole = lambda outs, core: outs[1]
        column = lambda at: lambda outs, core: outs[0].at[:, pl.ds(pl.multiple_of(at(core) * width, width), width)]
        plan = [
            ("kept", 0, column(lambda core: 2 * core)), ("got", 0, column(lambda core: 2 - 2 * core)),
            ("low", 1, column(lambda core: 1)), ("high", 1, whole),
        ]
        got["panel_grad"], got["merge_grad"] = finish(
            sums["C"], order, place, width, plan, [(width, 3 * width), (width, width)]
        )

    actions = dict(
        I=inner, T=attention, X=inputs, A0=start_outer, B0=start_inner,
        C0=start_rest, S0=start_small, S=small_step, SF=finish_small, A=lambda: sums["A"].advance(order),
        B=lambda: sums["B"].advance(order), C=lambda: sums["C"].advance(order),
        AF=finish_outer, BF=finish_inner, CF=finish_rest,
    )
    for action in SEQUENCE:
        actions[action]()
    small = got["small"]
    cut = lambda row, at: small[row, at * width : (at + 1) * width]
    outer_bias_grad, gain2_grad, shift2_grad = cut(0, 0), cut(0, 1), cut(0, 2)
    inner_bias_grad = small[1]
    merge_bias_grad, gain1_grad, shift1_grad = cut(2, 0), cut(2, 1), cut(2, 2)
    query_bias_grad, value_bias_grad = cut(3, 0), cut(3, 1)
    return (
        loss.reshape(1),
        layer_out,
        got["input_grad"],
        got["panel_grad"],
        query_bias_grad,
        value_bias_grad,
        got["merge_grad"],
        merge_bias_grad,
        gain1_grad,
        shift1_grad,
        got["inner_grad"],
        inner_bias_grad,
        got["outer_grad"],
        outer_bias_grad,
        gain2_grad,
        shift2_grad,
    )


def solution(mesh):
    return jax.shard_map(
        on_device,
        mesh=mesh,
        in_specs=(
            P(("wide", "narrow"), None),
            P(("wide", "narrow"), None),
            P(),
            P(),
            P(),
            P(),
            P(),
            P(),
            P(),
            P(),
            P(),
            P(),
            P(),
            P(),
            P(),
            P(),
            P(),
        ),
        out_specs=(
            P(),
            P(("wide", "narrow"), None),
            P(("wide", "narrow"), None),
            P(),
            P(),
            P(),
            P(),
            P(),
            P(),
            P(),
            P(),
            P(),
            P(),
            P(),
            P(),
            P(),
        ),
        check_vma=False,
    )
```

profile of v0, /device:TPU:0, one launch (start us, length us, event | category | flops | bytes accessed | tf_op | source)
XLA Modules:
  0.0 325.7 jit_solution(4078766735496869265)
XLA Ops:
  0.6 20.1 %attend.1 = (bf16[1024,768]{1,0:T(8,128)(2,1)}, bf16[1024,768]{1,0:T(8,128)(2,1)}, bf16[1024,768]{1,0:T(8,128)(2,1)}, bf16[768,1024]{1,0:T(8,128)(2,1)}, f32[6,4...) custom-call(bf16[1024,768]{1,0:T(8,128)(2,1)} %x_ref.1, ...), custom_call_target="tpu_custom_call" | custom-call | flops 7247757312 | bytes 20971520 | tf_op jit(solution)/shard_map/attend/pallas_call | solution.py:341
  20.7 27.2 %feed.1 = (bf16[3072,1024]{1,0:T(8,128)(2,1)}, bf16[1024,3072]{1,0:T(8,128)(2,1)}, f32[1024,768]{1,0:T(8,128)}, f32[1024,1]{1,0:T(8,128)}, bf16[1024,768]{1,0:T(8,128)(2,1)}, /*index=5*/bf16[16,768]{1,0:T(8,128)(2,1)}) custom-call(f32[1024,768]{1,0:T(8,128)} %get-tuple-element.103.hat_ref.hat_hbm, bf16[1024,768]{1,0:T(8,128)(2,1)} %get-tuple-element.104.low_ref, ...), custom_call_target="tpu_custom_call" | custom-call | flops 9663676416 | bytes 31457280 | tf_op jit(solution)/shard_map/feed/pallas_call | solution.py:429
  47.9 3.1 collective-permute-start
  51.0 2.6 collective-permute-start.1
  54.4 1.9 collective-permute-done.1
  56.3 3.1 collective-permute-done.2
  59.4 1.5 collective-permute-start.3
  60.9 1.5 collective-permute-start.4
  62.9 1.8 collective-permute-done.3
  66.0 2.0 collective-permute-done.5
  70.7 17.6 %outer_back.1 = (f32[1,1]{1,0:T(1,128)}, f32[1,3072]{1,0:T(1,128)}, bf16[1536,768]{1,0:T(8,128)(2,1)}, bf16[1536,768]{1,0:T(8,128)(2,1)}, f32[1024,768]{1,0:T(8,128)}, /*index=5*/bf16[1024,768]{1,0:T(8,128)(2,1)}) custom-call(s32[2]{0:T(128)} %pad_add_fusion.info_ref, s32[512]{0:T(512)} %partner_ref.1, f32[1]{0:T(128)S(6)} %copy.73.cool_ref, ...), custom_call_target="tpu_custom_call" | custom-call | flops 4831838208 | bytes 20971520 | tf_op jit(solution)/shard_map/outer_back/pallas_call | solution.py:545
  88.5 4.6 %collective-permute-done.7 = bf16[1536,768]{1,0:T(8,128)(2,1)S(1)} collective-permute-done((bf16[1536,768]{1,0:T(8,128)(2,1)}, bf16[1536,768]{1,0:T(8,128)(2,1)S(1)}, u32[]{:S(2)}, u32[]{:S(2)}) %collective-permute-start.7) | collective-permute-done | bytes 2359328 | tf_op jit(solution)/shard_map/ppermute | solution.py:42
  93.1 2.1 convert_add_fusion.2
  95.9 28.8 %inner_back.1 = (bf16[2304,512]{1,0:T(8,128)(2,1)}, bf16[2304,512]{1,0:T(8,128)(2,1)}, f32[1,3072]{1,0:T(1,128)}, bf16[1024,768]{1,0:T(8,128)(2,1)}, bf16[768,76...) custom-call(s32[2]{0:T(128)} %pad_add_fusion.info_ref, bf16[1024,768]{1,0:T(8,128)(2,1)} %get-tuple-element.116.outer_ref, ...), custom_call_target="tpu_custom_call" | custom-call | flops 14495514624 | bytes 41943040 | tf_op jit(solution)/shard_map/inner_back/pallas_call | solution.py:644
  124.7 2.4 convert_add_fusion.5
  127.2 1.3 collective-permute-start.11
  128.5 3.5 %collective-permute-done.9 = bf16[2304,512]{1,0:T(8,128)(2,1)} collective-permute-done((bf16[2304,512]{1,0:T(8,128)(2,1)}, bf16[2304,512]{1,0:T(8,128)(2,1)}, u32[]{:S(2)}, u32[]{:S(2)}) %collective-permute-start.9) | collective-permute-done | bytes 2359328 | tf_op jit(solution)/shard_map/ppermute | solution.py:42
  132.0 3.3 %add_convert_fusion.1 = (bf16[1152,512]{1,0:T(8,128)(2,1)}, f32[1152,512]{1,0:T(8,128)S(1)}) fusion(bf16[2304,512]{1,0:T(8,128)(2,1)} %collective-permute-done.9, s32[]{:T(128)S(6)} %select_n.445, bf16[2304,512]{1,0:T(8,128)(2,1)S(1)} %copy-done.4, s32[]{:T(128)S(6)} %select_n.441), kind=kLoop, calls=%fused_computation.5 | loop fusion | flops 4128768 | bytes 8257544 | tf_op jit(solution)/shard_map/convert_element_type | solution.py:88
  135.3 1.5 collective-permute-start.10
  139.4 3.6 %collective-permute-start.14 = (bf16[96,768]{1,0:T(8,128)(2,1)S(1)}, bf16[96,768]{1,0:T(8,128)(2,1)S(1)}, u32[]{:S(2)}, u32[]{:S(2)}) collective-permute-start(bf16[96,768]{1,0:T(8,128)(2,1)S(1)} %get-tuple-element.241), channel_id=1, source_target_pairs={{0,24},{1,25},{2,26},{3,27},{4,28},{5,29},{6,30},{7,31},{8,16},{9,... | collective-permute-start | bytes 442376 | tf_op jit(solution)/shard_map/ppermute | solution.py:42
  142.9 27.1 %attend_back.1 = (bf16[1024,768]{1,0:T(8,128)(2,1)}, bf16[1024,768]{1,0:T(8,128)(2,1)}, bf16[1024,768]{1,0:T(8,128)(2,1)}, bf16[2,768,768]{2,1,0:T(8,128)(2,1)},...) custom-call(s32[1]{0:T(128)} %bitcast.1.core_ref, bf16[768,1024]{1,0:T(8,128)(2,1)} %get-tuple-element.130.x_t_ref, ...), custom_call_target="tpu_custom_call" | custom-call | flops 9663676416 | bytes 31457280 | tf_op jit(solution)/shard_map/attend_back/pallas_call | solution.py:745
  173.2 3.6 %collective-permute-start.17 = (bf16[96,768]{1,0:T(8,128)(2,1)S(1)}, bf16[96,768]{1,0:T(8,128)(2,1)S(1)}, u32[]{:S(2)}, u32[]{:S(2)}) collective-permute-start(bf16[96,768]{1,0:T(8,128)(2,1)S(1)} %add_convert_fusion.14), channel_id=1, source_target_pairs={{0,24},{1,25},{2,26},{3,27},{4,28},{5,29},{6,30},{7,31},{8,16},{9,... | collective-permute-start | bytes 442376 | tf_op jit(solution)/shard_map/ppermute | solution.py:42
  176.7 1.4 collective-permute-start.15
  178.1 1.8 collective-permute-done.19
  179.9 6.4 %collective-permute-done.18 = bf16[96,768]{1,0:T(8,128)(2,1)S(1)} collective-permute-done((bf16[96,768]{1,0:T(8,128)(2,1)S(1)}, bf16[96,768]{1,0:T(8,128)(2,1)S(1)}, u32[]{:S(2)}, u32[]{:S(2)}) %collective-permute-start.18) | collective-permute-done | bytes 147488 | tf_op jit(solution)/shard_map/ppermute | solution.py:42
  187.1 1.4 collective-permute-start.22
  188.5 2.8 convert_add_fusion
  192.0 1.9 add_convert_fusion.12
  193.9 6.9 %collective-permute-done.22 = bf16[384,768]{1,0:T(8,128)(2,1)} collective-permute-done((bf16[384,768]{1,0:T(8,128)(2,1)S(1)}, bf16[384,768]{1,0:T(8,128)(2,1)}, u32[]{:S(2)}, u32[]{:S(2)}) %collective-permute-start.22) | collective-permute-done | bytes 589856 | tf_op jit(solution)/shard_map/ppermute | solution.py:42
  203.1 1.4 broadcast_select_fusion.1
  204.5 2.5 collective-permute-start.27
  207.0 3.0 collective-permute-start.20
  209.9 2.4 collective-permute-start.24
  213.4 2.0 collective-permute-done.20
  215.4 4.7 %collective-permute-done.23 = bf16[144,512]{1,0:T(8,128)(2,1)} collective-permute-done((bf16[144,512]{1,0:T(8,128)(2,1)}, bf16[144,512]{1,0:T(8,128)(2,1)}, u32[]{:S(2)}, u32[]{:S(2)}) %collective-permute-start.23) | collective-permute-done | bytes 147488 | tf_op jit(solution)/shard_map/ppermute | solution.py:42
  221.3 2.2 collective-permute-start.29
  223.6 2.4 collective-permute-start.25
  226.0 1.6 collective-permute-done.27
  227.6 2.0 maximum_select_fusion.kept_ref
  229.6 1.7 add_convert_fusion.7
  231.3 3.7 %collective-permute-done.28 = bf16[144,512]{1,0:T(8,128)(2,1)S(1)} collective-permute-done((bf16[144,512]{1,0:T(8,128)(2,1)S(1)}, bf16[144,512]{1,0:T(8,128)(2,1)S(1)}, u32[]{:S(2)}, u32[]{:S(2)}) %collective-permute-start.28) | collective-permute-done | bytes 147488 | tf_op jit(solution)/shard_map/ppermute | solution.py:42
  235.4 1.3 collective-permute-start.30
  236.7 2.9 collective-permute-start.31
  239.6 2.4 collective-permute-start.33
  242.0 1.7 collective-permute-done.31
  243.8 7.7 %collective-permute-done.32 = bf16[96,768]{1,0:T(8,128)(2,1)S(1)} collective-permute-done((bf16[96,768]{1,0:T(8,128)(2,1)S(1)}, bf16[96,768]{1,0:T(8,128)(2,1)S(1)}, u32[]{:S(2)}, u32[]{:S(2)}) %collective-permute-start.32) | collective-permute-done | bytes 147488 | tf_op jit(solution)/shard_map/ppermute | solution.py:42
  252.5 2.3 collective-permute-start.36
  255.0 2.2 collective-permute-start.34
  258.7 8.7 %input_back.1 = f32[1024,768]{1,0:T(8,128)} custom-call(f32[1024,768]{1,0:T(8,128)} %get-tuple-element.163.first_ref, bf16[1024,768]{1,0:T(8,128)(2,1)} %get-tuple-element.164.refs_0_, bf16[1024,768]{1,0:T(8,128)(2,1)} %get-tuple-element.165.refs_1_, bf16[1024,768]{1,0:T(8,128)(2,1)} %get-tuple-element.166.refs_2_, bf16[768,2304]{1,0:T(8,128)(2,1)} %refs_3_.1), custom_call_target="tpu_custom_call" | custom-call | flops 3623878656 | bytes 15728640 | tf_op jit(solution)/shard_map/input_back/pallas_call | solution.py:778
  267.9 5.9 %collective-permute-done.38 = bf16[1152,512]{1,0:T(8,128)(2,1)S(1)} collective-permute-done((bf16[1152,512]{1,0:T(8,128)(2,1)S(1)}, bf16[1152,512]{1,0:T(8,128)(2,1)S(1)}, u32[]{:S(2)}, u32[]{:S(2)}) %collective-permute-start.38) | collective-permute-done | bytes 1179680 | tf_op jit(solution)/shard_map/ppermute | solution.py:42
  274.6 1.6 collective-permute-start.37
  276.2 8.4 %collective-permute-done.37 = bf16[384,768]{1,0:T(8,128)(2,1)S(1)} collective-permute-done((bf16[384,768]{1,0:T(8,128)(2,1)S(1)}, bf16[384,768]{1,0:T(8,128)(2,1)S(1)}, u32[]{:S(2)}, u32[]{:S(2)}) %collective-permute-start.37) | collective-permute-done | bytes 589856 | tf_op jit(solution)/shard_map/ppermute | solution.py:42
  284.9 1.4 collective-permute-start.39
  289.5 1.4 copy-done.6
  290.9 2.4 collective-permute-start.45
  293.4 6.2 %finish.3 = f32[768,3072]{1,0:T(8,128)} custom-call(s32[1]{0:T(128)} %bitcast.1.core_ref, bf16[2304,512]{1,0:T(8,128)(2,1)} %copy-done.2, bf16[2304,512]{1,0:T(8,128)(2,1)} %copy-done.6), custom_call_target="tpu_custom_call" | custom-call | bytes 14155776 | tf_op jit(solution)/shard_map/finish/pallas_call | solution.py:809
  299.6 1.4 copy-done.5
  301.0 6.2 %finish.4 = f32[3072,768]{1,0:T(8,128)} custom-call(s32[1]{0:T(128)} %bitcast.1.core_ref, bf16[1536,768]{1,0:T(8,128)(2,1)} %copy-done.1, bf16[1536,768]{1,0:T(8,128)(2,1)} %copy-done.5), custom_call_target="tpu_custom_call" | custom-call | bytes 14155776 | tf_op jit(solution)/shard_map/finish/pallas_call | solution.py:809
  307.2 1.9 maximum_select_fusion.2.kept_ref
  310.3 1.3 collective-permute-start.48
  311.5 1.3 collective-permute-start.49
  314.3 2.2 collective-permute-done.49
  317.8 1.4 copy-done.3
  319.2 6.2 %finish.5 = (f32[768,2304]{1,0:T(8,128)}, f32[768,768]{1,0:T(8,128)}) custom-call(s32[1]{0:T(128)} %bitcast.1.core_ref, bf16[1536,768]{1,0:T(8,128)(2,1)} %copy-done, bf16[1536,768]{1,0:T(8,128)(2,1)} %copy-done.3), custom_call_target="tpu_custom_call" | custom-call | bytes 14155776 | tf_op jit(solution)/shard_map/finish/pallas_call | solution.py:809
  (150 shorter events, 29.1 us)
Async XLA Ops:
  47.9 6.5 %collective-permute-start = (bf16[16,768]{1,0:T(8,128)(2,1)}, bf16[16,768]{1,0:T(8,128)(2,1)S(1)}, u32[]{:S(2)}, u32[]{:S(2)}) collective-permute-start(bf16[16,768]{1,0:T(8,128)(2,1)} %get-tuple-element.105.own_ref), channel_id=1, source_target_pairs={{0,8},{1,9},{2,10},{3,11},{4,12},{5,13},{6,14},{7,15},{8,0},{9,1},... | collective-permute-start | bytes 73736 | tf_op jit(solution)/shard_map/ppermute | solution.py:42
  51.0 5.3 %collective-permute-start.1 = (bf16[16,768]{1,0:T(8,128)(2,1)}, bf16[16,768]{1,0:T(8,128)(2,1)S(1)}, u32[]{:S(2)}, u32[]{:S(2)}) collective-permute-start(bf16[16,768]{1,0:T(8,128)(2,1)} %get-tuple-element.105.own_ref), channel_id=1, source_target_pairs={{0,16},{1,17},{2,18},{3,19},{4,20},{5,21},{6,22},{7,23},{8,24},{9,... | collective-permute-start | bytes 73736 | tf_op jit(solution)/shard_map/ppermute | solution.py:42
  53.6 5.8 %collective-permute-start.2 = (bf16[16,768]{1,0:T(8,128)(2,1)}, bf16[16,768]{1,0:T(8,128)(2,1)S(1)}, u32[]{:S(2)}, u32[]{:S(2)}) collective-permute-start(bf16[16,768]{1,0:T(8,128)(2,1)} %get-tuple-element.105.own_ref), channel_id=1, source_target_pairs={{0,24},{1,25},{2,26},{3,27},{4,28},{5,29},{6,30},{7,31},{8,16},{9,... | collective-permute-start | bytes 73736 | tf_op jit(solution)/shard_map/ppermute | solution.py:42
  59.4 5.3 %collective-permute-start.3 = (bf16[64,768]{1,0:T(8,128)(2,1)S(1)}, bf16[64,768]{1,0:T(8,128)(2,1)S(1)}, u32[]{:S(2)}, u32[]{:S(2)}) collective-permute-start(bf16[64,768]{1,0:T(8,128)(2,1)S(1)} %get-tuple-element.257), channel_id=1, source_target_pairs={{0,2},{1,3},{2,0},{3,1},{4,6},{5,7},{6,4},{7,5},{8,10},{9,11},{10,... | collective-permute-start | bytes 294920 | tf_op jit(solution)/shard_map/ppermute | solution.py:42
  60.9 5.0 %collective-permute-start.4 = (bf16[64,768]{1,0:T(8,128)(2,1)S(1)}, bf16[64,768]{1,0:T(8,128)(2,1)S(1)}, u32[]{:S(2)}, u32[]{:S(2)}) collective-permute-start(bf16[64,768]{1,0:T(8,128)(2,1)S(1)} %get-tuple-element.257), channel_id=1, source_target_pairs={{0,4},{1,5},{2,6},{3,7},{4,0},{5,1},{6,2},{7,3},{8,12},{9,13},{10,... | collective-permute-start | bytes 294920 | tf_op jit(solution)/shard_map/ppermute | solution.py:42
  62.5 5.5 %collective-permute-start.5 = (bf16[64,768]{1,0:T(8,128)(2,1)S(1)}, bf16[64,768]{1,0:T(8,128)(2,1)S(1)}, u32[]{:S(2)}, u32[]{:S(2)}) collective-permute-start(bf16[64,768]{1,0:T(8,128)(2,1)S(1)} %get-tuple-element.257), channel_id=1, source_target_pairs={{0,6},{1,7},{2,4},{3,5},{4,2},{5,3},{6,0},{7,1},{8,14},{9,15},{10,... | collective-permute-start | bytes 294920 | tf_op jit(solution)/shard_map/ppermute | solution.py:42
  68.0 1.8 collective-permute-start.6
  88.3 4.8 %collective-permute-start.7 = (bf16[1536,768]{1,0:T(8,128)(2,1)}, bf16[1536,768]{1,0:T(8,128)(2,1)S(1)}, u32[]{:S(2)}, u32[]{:S(2)}) collective-permute-start(bf16[1536,768]{1,0:T(8,128)(2,1)} %get-tuple-element.114), channel_id=1, source_target_pairs={{0,1},{1,0},{2,3},{3,2},{4,5},{5,4},{6,7},{7,6},{8,9},{9,8},{10,11... | collective-permute-start | bytes 7077896 | tf_op jit(solution)/shard_map/ppermute | solution.py:42
  95.3 29.4 %collective-permute-start.8 = (bf16[768,768]{1,0:T(8,128)(2,1)S(1)}, bf16[768,768]{1,0:T(8,128)(2,1)}, u32[]{:S(2)}, u32[]{:S(2)}) collective-permute-start(bf16[768,768]{1,0:T(8,128)(2,1)S(1)} %get-tuple-element.227), channel_id=1, source_target_pairs={{0,2},{1,5},{2,0},{3,7},{4,6},{5,1},{6,4},{7,3},{8,10},{9,13},{10,... | collective-permute-start | bytes 3538952 | tf_op jit(solution)/shard_map/ppermute | solution.py:42
  124.7 7.3 %copy-start.4 = (bf16[2304,512]{1,0:T(8,128)(2,1)S(1)}, bf16[2304,512]{1,0:T(8,128)(2,1)}, u32[]{:S(2)}) copy-start(bf16[2304,512]{1,0:T(8,128)(2,1)} %get-tuple-element.123) | copy-start | bytes 7077892
  127.2 4.9 %collective-permute-start.9 = (bf16[2304,512]{1,0:T(8,128)(2,1)}, bf16[2304,512]{1,0:T(8,128)(2,1)}, u32[]{:S(2)}, u32[]{:S(2)}) collective-permute-start(bf16[2304,512]{1,0:T(8,128)(2,1)} %get-tuple-element.127), channel_id=1, source_target_pairs={{0,1},{1,0},{2,3},{3,2},{4,5},{5,4},{6,7},{7,6},{8,9},{9,8},{10,11... | collective-permute-start | bytes 7077896 | tf_op jit(solution)/shard_map/ppermute | solution.py:42
  127.2 10.2 %collective-permute-start.11 = (bf16[384,768]{1,0:T(8,128)(2,1)}, bf16[384,768]{1,0:T(8,128)(2,1)}, u32[]{:S(2)}, u32[]{:S(2)}) collective-permute-start(bf16[384,768]{1,0:T(8,128)(2,1)} %get-tuple-element.233), channel_id=1, source_target_pairs={{0,4},{1,3},{2,6},{3,1},{4,0},{5,7},{6,2},{7,5},{8,12},{9,11},{10,... | collective-permute-start | bytes 1769480 | tf_op jit(solution)/shard_map/ppermute | solution.py:42
  135.3 35.8 %collective-permute-start.10 = (bf16[1152,512]{1,0:T(8,128)(2,1)}, bf16[1152,512]{1,0:T(8,128)(2,1)S(1)}, u32[]{:S(2)}, u32[]{:S(2)}) collective-permute-start(bf16[1152,512]{1,0:T(8,128)(2,1)} %get-tuple-element.224), channel_id=1, source_target_pairs={{0,2},{1,5},{2,0},{3,7},{4,6},{5,1},{6,4},{7,3},{8,10},{9,13},{10,... | collective-permute-start | bytes 3538952 | tf_op jit(solution)/shard_map/ppermute | solution.py:42
  138.5 31.6 %collective-permute-start.12 = (bf16[96,768]{1,0:T(8,128)(2,1)S(1)}, bf16[96,768]{1,0:T(8,128)(2,1)S(1)}, u32[]{:S(2)}, u32[]{:S(2)}) collective-permute-start(bf16[96,768]{1,0:T(8,128)(2,1)S(1)} %get-tuple-element.242), channel_id=1, source_target_pairs={{0,8},{1,9},{2,10},{3,11},{4,12},{5,13},{6,14},{7,15},{8,0},{9,1},... | collective-permute-start | bytes 442376 | tf_op jit(solution)/shard_map/ppermute | solution.py:42
  138.6 31.5 %collective-permute-start.13 = (bf16[96,768]{1,0:T(8,128)(2,1)S(1)}, bf16[96,768]{1,0:T(8,128)(2,1)S(1)}, u32[]{:S(2)}, u32[]{:S(2)}) collective-permute-start(bf16[96,768]{1,0:T(8,128)(2,1)S(1)} %get-tuple-element.240), channel_id=1, source_target_pairs={{0,16},{1,17},{2,18},{3,19},{4,20},{5,21},{6,22},{7,23},{8,24},{9,... | collective-permute-start | bytes 442376 | tf_op jit(solution)/shard_map/ppermute | solution.py:42
  139.4 30.7 %collective-permute-start.14 = (bf16[96,768]{1,0:T(8,128)(2,1)S(1)}, bf16[96,768]{1,0:T(8,128)(2,1)S(1)}, u32[]{:S(2)}, u32[]{:S(2)}) collective-permute-start(bf16[96,768]{1,0:T(8,128)(2,1)S(1)} %get-tuple-element.241), channel_id=1, source_target_pairs={{0,24},{1,25},{2,26},{3,27},{4,28},{5,29},{6,30},{7,31},{8,16},{9,... | collective-permute-start | bytes 442376 | tf_op jit(solution)/shard_map/ppermute | solution.py:42
  172.4 16.1 %collective-permute-start.16 = (bf16[1536,768]{1,0:T(8,128)(2,1)}, bf16[1536,768]{1,0:T(8,128)(2,1)}, u32[]{:S(2)}, u32[]{:S(2)}) collective-permute-start(bf16[1536,768]{1,0:T(8,128)(2,1)} %bitcast.4), channel_id=1, source_target_pairs={{0,1},{1,0},{2,3},{3,2},{4,5},{5,4},{6,7},{7,6},{8,9},{9,8},{10,11... | collective-permute-start | bytes 7077896 | tf_op jit(solution)/shard_map/ppermute | solution.py:42
  172.4 7.5 %collective-permute-start.19 = (bf16[96,768]{1,0:T(8,128)(2,1)S(1)}, bf16[96,768]{1,0:T(8,128)(2,1)S(1)}, u32[]{:S(2)}, u32[]{:S(2)}) collective-permute-start(bf16[96,768]{1,0:T(8,128)(2,1)S(1)} %add_convert_fusion.14), channel_id=1, source_target_pairs={{0,8},{1,9},{2,10},{3,11},{4,12},{5,13},{6,14},{7,15},{8,0},{9,1},... | collective-permute-start | bytes 442376 | tf_op jit(solution)/shard_map/ppermute | solution.py:42
  172.4 13.9 %collective-permute-start.18 = (bf16[96,768]{1,0:T(8,128)(2,1)S(1)}, bf16[96,768]{1,0:T(8,128)(2,1)S(1)}, u32[]{:S(2)}, u32[]{:S(2)}) collective-permute-start(bf16[96,768]{1,0:T(8,128)(2,1)S(1)} %add_convert_fusion.14), channel_id=1, source_target_pairs={{0,16},{1,17},{2,18},{3,19},{4,20},{5,21},{6,22},{7,23},{8,24},{9,... | collective-permute-start | bytes 442376 | tf_op jit(solution)/shard_map/ppermute | solution.py:42
  173.2 13.1 %collective-permute-start.17 = (bf16[96,768]{1,0:T(8,128)(2,1)S(1)}, bf16[96,768]{1,0:T(8,128)(2,1)S(1)}, u32[]{:S(2)}, u32[]{:S(2)}) collective-permute-start(bf16[96,768]{1,0:T(8,128)(2,1)S(1)} %add_convert_fusion.14), channel_id=1, source_target_pairs={{0,24},{1,25},{2,26},{3,27},{4,28},{5,29},{6,30},{7,31},{8,16},{9,... | collective-permute-start | bytes 442376 | tf_op jit(solution)/shard_map/ppermute | solution.py:42
  176.7 15.3 %collective-permute-start.15 = (bf16[576,512]{1,0:T(8,128)(2,1)}, bf16[576,512]{1,0:T(8,128)(2,1)}, u32[]{:S(2)}, u32[]{:S(2)}) collective-permute-start(bf16[576,512]{1,0:T(8,128)(2,1)} %get-tuple-element.230), channel_id=1, source_target_pairs={{0,4},{1,3},{2,6},{3,1},{4,0},{5,7},{6,2},{7,5},{8,12},{9,11},{10,... | collective-permute-start | bytes 1769480 | tf_op jit(solution)/shard_map/ppermute | solution.py:42
  186.5 4.8 %copy-start.12 = (bf16[96,768]{1,0:T(8,128)(2,1)}, bf16[96,768]{1,0:T(8,128)(2,1)S(1)}, u32[]{:S(2)}) copy-start(bf16[96,768]{1,0:T(8,128)(2,1)S(1)} %get-tuple-element.217) | copy-start | bytes 442372
  186.6 4.7 %copy-start.14 = (bf16[96,768]{1,0:T(8,128)(2,1)}, bf16[96,768]{1,0:T(8,128)(2,1)S(1)}, u32[]{:S(2)}) copy-start(bf16[96,768]{1,0:T(8,128)(2,1)S(1)} %get-tuple-element.215) | copy-start | bytes 442372
  187.1 13.7 %collective-permute-start.22 = (bf16[384,768]{1,0:T(8,128)(2,1)S(1)}, bf16[384,768]{1,0:T(8,128)(2,1)}, u32[]{:S(2)}, u32[]{:S(2)}) collective-permute-start(bf16[384,768]{1,0:T(8,128)(2,1)S(1)} %pad_maximum_fusion), channel_id=1, source_target_pairs={{0,4},{1,3},{2,6},{3,1},{4,0},{5,7},{6,2},{7,5},{8,12},{9,11},{10,... | collective-permute-start | bytes 1769480 | tf_op jit(solution)/shard_map/ppermute | solution.py:42
  191.3 21.0 %collective-permute-start.21 = (bf16[768,768]{1,0:T(8,128)(2,1)S(1)}, bf16[768,768]{1,0:T(8,128)(2,1)S(1)}, u32[]{:S(2)}, u32[]{:S(2)}) collective-permute-start(bf16[768,768]{1,0:T(8,128)(2,1)S(1)} %get-tuple-element.223), channel_id=1, source_target_pairs={{0,2},{1,5},{2,0},{3,7},{4,6},{5,1},{6,4},{7,3},{8,10},{9,13},{10,... | collective-permute-start | bytes 3538952 | tf_op jit(solution)/shard_map/ppermute | solution.py:42
  193.9 8.2 %copy-start.9 = (bf16[96,768]{1,0:T(8,128)(2,1)S(1)}, bf16[96,768]{1,0:T(8,128)(2,1)}, u32[]{:S(2)}) copy-start(bf16[96,768]{1,0:T(8,128)(2,1)} %copy-done.8) | copy-start | bytes 442372
  193.9 8.2 %copy-start.11 = (bf16[96,768]{1,0:T(8,128)(2,1)S(1)}, bf16[96,768]{1,0:T(8,128)(2,1)}, u32[]{:S(2)}) copy-start(bf16[96,768]{1,0:T(8,128)(2,1)} %copy-done.10) | copy-start | bytes 442372
  204.5 23.1 %collective-permute-start.27 = (bf16[768,768]{1,0:T(8,128)(2,1)S(1)}, bf16[768,768]{1,0:T(8,128)(2,1)}, u32[]{:S(2)}, u32[]{:S(2)}) collective-permute-start(bf16[768,768]{1,0:T(8,128)(2,1)S(1)} %broadcast_select_fusion.1), channel_id=1, source_target_pairs={{0,2},{1,5},{2,0},{3,7},{4,6},{5,1},{6,4},{7,3},{8,10},{9,13},{10,... | collective-permute-start | bytes 3538952 | tf_op jit(solution)/shard_map/ppermute | solution.py:42
  207.0 8.4 %collective-permute-start.20 = (bf16[144,512]{1,0:T(8,128)(2,1)}, bf16[144,512]{1,0:T(8,128)(2,1)}, u32[]{:S(2)}, u32[]{:S(2)}) collective-permute-start(bf16[144,512]{1,0:T(8,128)(2,1)} %get-tuple-element.239), channel_id=1, source_target_pairs={{0,8},{1,9},{2,10},{3,11},{4,12},{5,13},{6,14},{7,15},{8,0},{9,1},... | collective-permute-start | bytes 442376 | tf_op jit(solution)/shard_map/ppermute | solution.py:42
  209.9 10.2 %collective-permute-start.23 = (bf16[144,512]{1,0:T(8,128)(2,1)}, bf16[144,512]{1,0:T(8,128)(2,1)}, u32[]{:S(2)}, u32[]{:S(2)}) collective-permute-start(bf16[144,512]{1,0:T(8,128)(2,1)} %get-tuple-element.237), channel_id=1, source_target_pairs={{0,16},{1,17},{2,18},{3,19},{4,20},{5,21},{6,22},{7,23},{8,24},{9,... | collective-permute-start | bytes 442376 | tf_op jit(solution)/shard_map/ppermute | solution.py:42
  209.9 10.2 %collective-permute-start.24 = (bf16[144,512]{1,0:T(8,128)(2,1)}, bf16[144,512]{1,0:T(8,128)(2,1)}, u32[]{:S(2)}, u32[]{:S(2)}) collective-permute-start(bf16[144,512]{1,0:T(8,128)(2,1)} %get-tuple-element.238), channel_id=1, source_target_pairs={{0,24},{1,25},{2,26},{3,27},{4,28},{5,29},{6,30},{7,31},{8,16},{9,... | collective-permute-start | bytes 442376 | tf_op jit(solution)/shard_map/ppermute | solution.py:42
  213.4 16.1 %collective-permute-start.26 = (bf16[384,768]{1,0:T(8,128)(2,1)}, bf16[384,768]{1,0:T(8,128)(2,1)}, u32[]{:S(2)}, u32[]{:S(2)}) collective-permute-start(bf16[384,768]{1,0:T(8,128)(2,1)} %get-tuple-element.229), channel_id=1, source_target_pairs={{0,4},{1,3},{2,6},{3,1},{4,0},{5,7},{6,2},{7,5},{8,12},{9,11},{10,... | collective-permute-start | bytes 1769480 | tf_op jit(solution)/shard_map/ppermute | solution.py:42
  221.3 9.9 %collective-permute-start.29 = (bf16[144,512]{1,0:T(8,128)(2,1)S(1)}, bf16[144,512]{1,0:T(8,128)(2,1)S(1)}, u32[]{:S(2)}, u32[]{:S(2)}) collective-permute-start(bf16[144,512]{1,0:T(8,128)(2,1)S(1)} %add_convert_fusion.10), channel_id=1, source_target_pairs={{0,8},{1,9},{2,10},{3,11},{4,12},{5,13},{6,14},{7,15},{8,0},{9,1},... | collective-permute-start | bytes 442376 | tf_op jit(solution)/shard_map/ppermute | solution.py:42
  223.5 11.4 %collective-permute-start.28 = (bf16[144,512]{1,0:T(8,128)(2,1)S(1)}, bf16[144,512]{1,0:T(8,128)(2,1)S(1)}, u32[]{:S(2)}, u32[]{:S(2)}) collective-permute-start(bf16[144,512]{1,0:T(8,128)(2,1)S(1)} %add_convert_fusion.10), channel_id=1, source_target_pairs={{0,16},{1,17},{2,18},{3,19},{4,20},{5,21},{6,22},{7,23},{8,24},{9,... | collective-permute-start | bytes 442376 | tf_op jit(solution)/shard_map/ppermute | solution.py:42
  223.6 11.4 %collective-permute-start.25 = (bf16[144,512]{1,0:T(8,128)(2,1)S(1)}, bf16[144,512]{1,0:T(8,128)(2,1)S(1)}, u32[]{:S(2)}, u32[]{:S(2)}) collective-permute-start(bf16[144,512]{1,0:T(8,128)(2,1)S(1)} %add_convert_fusion.10), channel_id=1, source_target_pairs={{0,24},{1,25},{2,26},{3,27},{4,28},{5,29},{6,30},{7,31},{8,16},{9,... | collective-permute-start | bytes 442376 | tf_op jit(solution)/shard_map/ppermute | solution.py:42
  229.5 46.7 %copy-start.1 = (bf16[1536,768]{1,0:T(8,128)(2,1)}, bf16[1536,768]{1,0:T(8,128)(2,1)S(1)}, u32[]{:S(2)}) copy-start(bf16[1536,768]{1,0:T(8,128)(2,1)S(1)} %maximum_select_fusion.kept_ref) | copy-start | bytes 7077892
  235.2 6.7 %copy-start.16 = (f32[1,3072]{1,0:T(1,128)S(1)}, f32[1,3072]{1,0:T(1,128)}, u32[]{:S(2)}) copy-start(f32[1,3072]{1,0:T(1,128)} %get-tuple-element.170) | copy-start | bytes 36868
  235.2 6.7 %copy-start.17 = (f32[1,3072]{1,0:T(1,128)S(1)}, f32[1,3072]{1,0:T(1,128)}, u32[]{:S(2)}) copy-start(f32[1,3072]{1,0:T(1,128)} %get-tuple-element.171) | copy-start | bytes 36868
  235.2 6.7 %copy-start.18 = (f32[1,3072]{1,0:T(1,128)S(1)}, f32[1,3072]{1,0:T(1,128)}, u32[]{:S(2)}) copy-start(f32[1,3072]{1,0:T(1,128)} %get-tuple-element.172) | copy-start | bytes 36868
  235.3 6.7 %copy-start.19 = (f32[1,3072]{1,0:T(1,128)S(1)}, f32[1,3072]{1,0:T(1,128)}, u32[]{:S(2)}) copy-start(f32[1,3072]{1,0:T(1,128)} %get-tuple-element.173) | copy-start | bytes 36868
  235.4 21.8 %collective-permute-start.30 = (bf16[576,512]{1,0:T(8,128)(2,1)S(1)}, bf16[576,512]{1,0:T(8,128)(2,1)S(1)}, u32[]{:S(2)}, u32[]{:S(2)}) collective-permute-start(bf16[576,512]{1,0:T(8,128)(2,1)S(1)} %pad_maximum_fusion.1), channel_id=1, source_target_pairs={{0,4},{1,3},{2,6},{3,1},{4,0},{5,7},{6,2},{7,5},{8,12},{9,11},{10,... | collective-permute-start | bytes 1769480 | tf_op jit(solution)/shard_map/ppermute | solution.py:42
  236.7 7.1 %collective-permute-start.31 = (bf16[96,768]{1,0:T(8,128)(2,1)S(1)}, bf16[96,768]{1,0:T(8,128)(2,1)S(1)}, u32[]{:S(2)}, u32[]{:S(2)}) collective-permute-start(bf16[96,768]{1,0:T(8,128)(2,1)S(1)} %get-tuple-element.236), channel_id=1, source_target_pairs={{0,8},{1,9},{2,10},{3,11},{4,12},{5,13},{6,14},{7,15},{8,0},{9,1},... | collective-permute-start | bytes 442376 | tf_op jit(solution)/shard_map/ppermute | solution.py:42
  239.6 11.9 %collective-permute-start.32 = (bf16[96,768]{1,0:T(8,128)(2,1)S(1)}, bf16[96,768]{1,0:T(8,128)(2,1)S(1)}, u32[]{:S(2)}, u32[]{:S(2)}) collective-permute-start(bf16[96,768]{1,0:T(8,128)(2,1)S(1)} %get-tuple-element.235), channel_id=1, source_target_pairs={{0,16},{1,17},{2,18},{3,19},{4,20},{5,21},{6,22},{7,23},{8,24},{9,... | collective-permute-start | bytes 442376 | tf_op jit(solution)/shard_map/ppermute | solution.py:42
  239.6 11.9 %collective-permute-start.33 = (bf16[96,768]{1,0:T(8,128)(2,1)S(1)}, bf16[96,768]{1,0:T(8,128)(2,1)S(1)}, u32[]{:S(2)}, u32[]{:S(2)}) collective-permute-start(bf16[96,768]{1,0:T(8,128)(2,1)S(1)} %get-tuple-element.234), channel_id=1, source_target_pairs={{0,24},{1,25},{2,26},{3,27},{4,28},{5,29},{6,30},{7,31},{8,16},{9,... | collective-permute-start | bytes 442376 | tf_op jit(solution)/shard_map/ppermute | solution.py:42
  252.5 14.9 %collective-permute-start.36 = (bf16[96,768]{1,0:T(8,128)(2,1)S(1)}, bf16[96,768]{1,0:T(8,128)(2,1)S(1)}, u32[]{:S(2)}, u32[]{:S(2)}) collective-permute-start(bf16[96,768]{1,0:T(8,128)(2,1)S(1)} %add_convert_fusion.6), channel_id=1, source_target_pairs={{0,8},{1,9},{2,10},{3,11},{4,12},{5,13},{6,14},{7,15},{8,0},{9,1},... | collective-permute-start | bytes 442376 | tf_op jit(solution)/shard_map/ppermute | solution.py:42
  254.8 12.7 %collective-permute-start.35 = (bf16[96,768]{1,0:T(8,128)(2,1)S(1)}, bf16[96,768]{1,0:T(8,128)(2,1)S(1)}, u32[]{:S(2)}, u32[]{:S(2)}) collective-permute-start(bf16[96,768]{1,0:T(8,128)(2,1)S(1)} %add_convert_fusion.6), channel_id=1, source_target_pairs={{0,16},{1,17},{2,18},{3,19},{4,20},{5,21},{6,22},{7,23},{8,24},{9,... | collective-permute-start | bytes 442376 | tf_op jit(solution)/shard_map/ppermute | solution.py:42
  255.0 12.4 %collective-permute-start.34 = (bf16[96,768]{1,0:T(8,128)(2,1)S(1)}, bf16[96,768]{1,0:T(8,128)(2,1)S(1)}, u32[]{:S(2)}, u32[]{:S(2)}) collective-permute-start(bf16[96,768]{1,0:T(8,128)(2,1)S(1)} %add_convert_fusion.6), channel_id=1, source_target_pairs={{0,24},{1,25},{2,26},{3,27},{4,28},{5,29},{6,30},{7,31},{8,16},{9,... | collective-permute-start | bytes 442376 | tf_op jit(solution)/shard_map/ppermute | solution.py:42
  257.5 16.3 %collective-permute-start.38 = (bf16[1152,512]{1,0:T(8,128)(2,1)S(1)}, bf16[1152,512]{1,0:T(8,128)(2,1)S(1)}, u32[]{:S(2)}, u32[]{:S(2)}) collective-permute-start(bf16[1152,512]{1,0:T(8,128)(2,1)S(1)} %broadcast_select_fusion.2), channel_id=1, source_target_pairs={{0,2},{1,5},{2,0},{3,7},{4,6},{5,1},{6,4},{7,3},{8,10},{9,13},{10,... | collective-permute-start | bytes 3538952 | tf_op jit(solution)/shard_map/ppermute | solution.py:42
  274.5 10.2 %copy-start.2 = (bf16[2304,512]{1,0:T(8,128)(2,1)}, bf16[2304,512]{1,0:T(8,128)(2,1)S(1)}, u32[]{:S(2)}) copy-start(bf16[2304,512]{1,0:T(8,128)(2,1)S(1)} %maximum_select_fusion.1.kept_ref) | copy-start | bytes 7077892
  274.5 15.0 %collective-permute-start.43 = (bf16[2304,512]{1,0:T(8,128)(2,1)S(1)}, bf16[2304,512]{1,0:T(8,128)(2,1)S(1)}, u32[]{:S(2)}, u32[]{:S(2)}) collective-permute-start(bf16[2304,512]{1,0:T(8,128)(2,1)S(1)} %maximum_select_fusion.1.kept_ref), channel_id=1, source_target_pairs={{0,1},{1,0},{2,3},{3,2},{4,5},{5,4},{6,7},{7,6},{8,9},{9,8},{10,11... | collective-permute-start | bytes 7077896 | tf_op jit(solution)/shard_map/ppermute | solution.py:42
  274.6 9.9 %collective-permute-start.37 = (bf16[384,768]{1,0:T(8,128)(2,1)S(1)}, bf16[384,768]{1,0:T(8,128)(2,1)S(1)}, u32[]{:S(2)}, u32[]{:S(2)}) collective-permute-start(bf16[384,768]{1,0:T(8,128)(2,1)S(1)} %pad_maximum_fusion.2), channel_id=1, source_target_pairs={{0,4},{1,3},{2,6},{3,1},{4,0},{5,7},{6,2},{7,5},{8,12},{9,11},{10,... | collective-permute-start | bytes 1769480 | tf_op jit(solution)/shard_map/ppermute | solution.py:42
  276.2 23.4 %collective-permute-start.40 = (bf16[1536,768]{1,0:T(8,128)(2,1)S(1)}, bf16[1536,768]{1,0:T(8,128)(2,1)S(1)}, u32[]{:S(2)}, u32[]{:S(2)}) collective-permute-start(bf16[1536,768]{1,0:T(8,128)(2,1)S(1)} %maximum_select_fusion.kept_ref), channel_id=1, source_target_pairs={{0,1},{1,0},{2,3},{3,2},{4,5},{5,4},{6,7},{7,6},{8,9},{9,8},{10,11... | collective-permute-start | bytes 7077896 | tf_op jit(solution)/shard_map/ppermute | solution.py:42
  284.9 22.3 %collective-permute-start.39 = (bf16[768,768]{1,0:T(8,128)(2,1)S(1)}, bf16[768,768]{1,0:T(8,128)(2,1)}, u32[]{:S(2)}, u32[]{:S(2)}) collective-permute-start(bf16[768,768]{1,0:T(8,128)(2,1)S(1)} %broadcast_select_fusion), channel_id=1, source_target_pairs={{0,2},{1,5},{2,0},{3,7},{4,6},{5,1},{6,4},{7,3},{8,10},{9,13},{10,... | collective-permute-start | bytes 3538952 | tf_op jit(solution)/shard_map/ppermute | solution.py:42
  286.2 1.2 collective-permute-start.41
  287.5 12.0 %collective-permute-start.42 = (f32[4,3072]{1,0:T(4,128)S(1)}, f32[4,3072]{1,0:T(4,128)S(1)}, u32[]{:S(2)}, u32[]{:S(2)}) collective-permute-start(f32[4,3072]{1,0:T(4,128)S(1)} %add.315), channel_id=1, source_target_pairs={{0,8},{1,9},{2,10},{3,11},{4,12},{5,13},{6,14},{7,15},{8,0},{9,1},... | collective-permute-start | bytes 147464 | tf_op jit(solution)/shard_map/ppermute | solution.py:42
  288.6 10.9 %collective-permute-start.44 = (f32[4,3072]{1,0:T(4,128)S(1)}, f32[4,3072]{1,0:T(4,128)S(1)}, u32[]{:S(2)}, u32[]{:S(2)}) collective-permute-start(f32[4,3072]{1,0:T(4,128)S(1)} %add.315), channel_id=1, source_target_pairs={{0,16},{1,17},{2,18},{3,19},{4,20},{5,21},{6,22},{7,23},{8,24},{9,... | collective-permute-start | bytes 147464 | tf_op jit(solution)/shard_map/ppermute | solution.py:42
  290.9 8.6 %collective-permute-start.45 = (f32[4,3072]{1,0:T(4,128)S(1)}, f32[4,3072]{1,0:T(4,128)S(1)}, u32[]{:S(2)}, u32[]{:S(2)}) collective-permute-start(f32[4,3072]{1,0:T(4,128)S(1)} %add.315), channel_id=1, source_target_pairs={{0,24},{1,25},{2,26},{3,27},{4,28},{5,29},{6,30},{7,31},{8,16},{9,... | collective-permute-start | bytes 147464 | tf_op jit(solution)/shard_map/ppermute | solution.py:42
  299.6 1.4 copy-start.5
  309.1 8.7 %copy-start = (bf16[1536,768]{1,0:T(8,128)(2,1)}, bf16[1536,768]{1,0:T(8,128)(2,1)S(1)}, u32[]{:S(2)}) copy-start(bf16[1536,768]{1,0:T(8,128)(2,1)S(1)} %maximum_select_fusion.2.kept_ref) | copy-start | bytes 7077892
  309.1 8.7 %collective-permute-start.46 = (bf16[1536,768]{1,0:T(8,128)(2,1)S(1)}, bf16[1536,768]{1,0:T(8,128)(2,1)S(1)}, u32[]{:S(2)}, u32[]{:S(2)}) collective-permute-start(bf16[1536,768]{1,0:T(8,128)(2,1)S(1)} %maximum_select_fusion.2.kept_ref), channel_id=1, source_target_pairs={{0,1},{1,0},{2,3},{3,2},{4,5},{5,4},{6,7},{7,6},{8,9},{9,8},{10,11... | collective-permute-start | bytes 7077896 | tf_op jit(solution)/shard_map/ppermute | solution.py:42
  309.2 4.2 %collective-permute-start.47 = (f32[4,3072]{1,0:T(4,128)S(1)}, f32[4,3072]{1,0:T(4,128)S(1)}, u32[]{:S(2)}, u32[]{:S(2)}) collective-permute-start(f32[4,3072]{1,0:T(4,128)S(1)} %add_add_fusion.1), channel_id=1, source_target_pairs={{0,2},{1,3},{2,0},{3,1},{4,6},{5,7},{6,4},{7,5},{8,10},{9,11},{10,... | collective-permute-start | bytes 147464 | tf_op jit(solution)/shard_map/ppermute | solution.py:42
  310.3 4.1 %collective-permute-start.48 = (f32[4,3072]{1,0:T(4,128)S(1)}, f32[4,3072]{1,0:T(4,128)S(1)}, u32[]{:S(2)}, u32[]{:S(2)}) collective-permute-start(f32[4,3072]{1,0:T(4,128)S(1)} %add_add_fusion.1), channel_id=1, source_target_pairs={{0,4},{1,5},{2,6},{3,7},{4,0},{5,1},{6,2},{7,3},{8,12},{9,13},{10,... | collective-permute-start | bytes 147464 | tf_op jit(solution)/shard_map/ppermute | solution.py:42
  311.5 5.0 %collective-permute-start.49 = (f32[4,3072]{1,0:T(4,128)S(1)}, f32[4,3072]{1,0:T(4,128)S(1)}, u32[]{:S(2)}, u32[]{:S(2)}) collective-permute-start(f32[4,3072]{1,0:T(4,128)S(1)} %add_add_fusion.1), channel_id=1, source_target_pairs={{0,6},{1,7},{2,4},{3,5},{4,2},{5,3},{6,0},{7,1},{8,14},{9,15},{10,... | collective-permute-start | bytes 147464 | tf_op jit(solution)/shard_map/ppermute | solution.py:42
  317.8 1.4 copy-start.3
  (7 other events, 7.2 us)
where the time goes:
time: 332 us; the launch traced here: 326 us
  Pallas kernels  148 us (45%)
  waiting for transfers between devices  75.1 us (23%)
  starting transfers between devices  61.2 us (18%)
  other arithmetic  28.9 us (9%)
  local copies, waits for them, and re-layouts  10.2 us (3%)
    ppermute x50, waiting for transfers between devices, exchange(): return lax.ppermute(value, BOTH, pairs)  75.1 us
    ppermute x50, starting transfers between devices, exchange(): return lax.ppermute(value, BOTH, pairs)  61.2 us
    pallas_call x1, Pallas kernels, inner_back(): kernel_call(partial(inner_back_kernel, rows), 'inner_back', 6 * tokens *...  28.8 us
    pallas_call x1, Pallas kernels, feed(): kernel_call(partial(feed_kernel, 1024), 'feed', 4 * tokens * width * hidd...  27.2 us
    pallas_call x1, Pallas kernels, attend_back(): kernel_call(partial(attend_back_kernel, HEADS // 2), 'attend_back', 10 *...  27.1 us
    pallas_call x1, Pallas kernels, attend(): kernel_call(attend_kernel, 'attend', 2 * tokens * width * width * 4 + 4 *...  20.1 us
    pallas_call x3, Pallas kernels, finish(): kernel_call(partial(finish_kernel, plan), 'finish', 0, half * cols * 12,...  18.5 us
    pallas_call x1, Pallas kernels, outer_back(): kernel_call(partial(outer_back_kernel, min(count, 256), masks), 'outer_ba...  17.6 us
  transfers between devices with their start and end apart: 50, of which 24 were waited for; matrix products, arithmetic and copies ran while one was open for 7% of the time, Pallas kernels for 24%

commit v1 on v0

--- a/solution.py
+++ b/solution.py
@@ -230,13 +230,11 @@
     "C", "B", "C", "B", "X", "C", "S0", "B", "C", "S", "A", "BF", "S", "AF", "C", "SF", "C", "CF",
 )
 
-VMEM_LIMIT = 58 * 1024 * 1024
-
-
-def kernel_call(body, name, flops, nbytes, **options):
+
+def kernel_call(body, name, flops, nbytes, limit=58, **options):
     return pl.pallas_call(
         body,
-        compiler_params=pltpu.CompilerParams(vmem_limit_bytes=VMEM_LIMIT),
+        compiler_params=pltpu.CompilerParams(vmem_limit_bytes=limit << 20),
         cost_estimate=pl.CostEstimate(flops=flops, bytes_accessed=nbytes, transcendentals=0),
         name=name,
         **options,
@@ -642,7 +640,7 @@
     line = jax.ShapeDtypeStruct((1, hidden), F32)
     part = jax.ShapeDtypeStruct((half * width, chunk), BF)
     return kernel_call(
-        partial(inner_back_kernel, rows), "inner_back", 6 * tokens * hidden * width, 40 << 20,
+        partial(inner_back_kernel, rows), "inner_back", 6 * tokens * hidden * width, 40 << 20, limit=46,
         grid_spec=pltpu.PrefetchScalarGridSpec(
             num_scalar_prefetch=1,
             grid=(steps,),
@@ -744,7 +742,7 @@
     half = jax.ShapeDtypeStruct((2, width, width), BF)
     return kernel_call(
         partial(attend_back_kernel, HEADS // 2), "attend_back",
-        10 * tokens * 384 * width * 2 + 6 * tokens * width * width, 30 << 20,
+        10 * tokens * 384 * width * 2 + 6 * tokens * width * width, 30 << 20, limit=40,
         grid_spec=pltpu.PrefetchScalarGridSpec(
             num_scalar_prefetch=1,
             grid=(rows,),
@@ -807,7 +805,7 @@
     half, cols = kept.shape
     hbm = pl.BlockSpec(memory_space=pl.ANY)
     result = kernel_call(
-        partial(finish_kernel, plan), "finish", 0, half * cols * 12,
+        partial(finish_kernel, plan), "finish", 0, half * cols * 12, limit=24,
         in_specs=[pl.BlockSpec(memory_space=pltpu.SMEM)] + [pl.BlockSpec(memory_space=pltpu.VMEM)] * 2,
         out_specs=[hbm] * len(shapes),
         out_shape=[jax.ShapeDtypeStruct(shape, F32) for shape in shapes],

time: 332 us -> 311 us (0.937)
  Pallas kernels: 148 us -> 136 us
  other arithmetic: 28.9 us -> 23.2 us
  waiting for transfers between devices: 75.1 us -> 79.7 us
  local copies, waits for them, and re-layouts: 10.2 us -> 5.85 us
    pallas_call x3, Pallas kernels: 18.5 us -> 11.4 us  [finish(): kernel_call(partial(finish_kernel, plan), 'finish', 0, half * cols * 12,...]
    ppermute x50, waiting for transfers between devices: 75.1 us -> 79.7 us  [exchange(): return lax.ppermute(value, BOTH, pairs)]
    unnamed x60 -> x58, local copies, waits for them, and re-layouts: 8.83 us -> 4.51 us
    pallas_call x1, Pallas kernels: 27.1 us -> 23.7 us  [attend_back(): kernel_call(partial(attend_back_kernel, HEADS // 2), 'attend_back', 10 *...]
  transfers between devices with their start and end apart: 50 -> 50, of which waited for: 24 -> 25; matrix products, arithmetic and copies ran while one was open for 7% -> 6% of each run, Pallas kernels for 24% -> 22%
where the time goes in v1:
time: 311 us; the launch traced here: 306 us
  Pallas kernels  136 us (44%)
  waiting for transfers between devices  79.7 us (26%)
  starting transfers between devices  59.3 us (19%)
  other arithmetic  23.2 us (7%)
  local copies, waits for them, and re-layouts  5.85 us (2%)
    ppermute x50, waiting for transfers between devices, exchange(): return lax.ppermute(value, BOTH, pairs)  79.7 us
    ppermute x50, starting transfers between devices, exchange(): return lax.ppermute(value, BOTH, pairs)  59.3 us
    pallas_call x1, Pallas kernels, feed(): kernel_call(partial(feed_kernel, 1024), 'feed', 4 * tokens * width * hidd...  27.2 us
    pallas_call x1, Pallas kernels, inner_back(): kernel_call(partial(inner_back_kernel, rows), 'inner_back', 6 * tokens *...  26.9 us
    pallas_call x1, Pallas kernels, attend_back(): kernel_call(partial(attend_back_kernel, HEADS // 2), 'attend_back', 10 *...  23.7 us
    pallas_call x1, Pallas kernels, attend(): kernel_call(attend_kernel, 'attend', 2 * tokens * width * width * 4 + 4 *...  20.1 us
    pallas_call x1, Pallas kernels, outer_back(): kernel_call(partial(outer_back_kernel, min(count, 256), masks), 'outer_ba...  17.6 us
    pallas_call x3, Pallas kernels, finish(): kernel_call(partial(finish_kernel, plan), 'finish', 0, half * cols * 12,...  11.4 us
  transfers between devices with their start and end apart: 50, of which 25 were waited for; matrix products, arithmetic and copies ran while one was open for 6% of the time, Pallas kernels for 22%

profile of v1, /device:TPU:0, one launch (start us, length us, event | category | flops | bytes accessed | tf_op | source)
XLA Modules:
  0.0 305.8 jit_solution(12918719947370854206)
XLA Ops:
  0.6 20.1 %attend.1 = (bf16[1024,768]{1,0:T(8,128)(2,1)}, bf16[1024,768]{1,0:T(8,128)(2,1)}, bf16[1024,768]{1,0:T(8,128)(2,1)}, bf16[768,1024]{1,0:T(8,128)(2,1)}, f32[6,4...) custom-call(bf16[1024,768]{1,0:T(8,128)(2,1)} %x_ref.1, ...), custom_call_target="tpu_custom_call" | custom-call | flops 7247757312 | bytes 20971520 | tf_op jit(solution)/shard_map/attend/pallas_call | solution.py:339
  20.7 27.2 %feed.1 = (bf16[3072,1024]{1,0:T(8,128)(2,1)}, bf16[1024,3072]{1,0:T(8,128)(2,1)}, f32[1024,768]{1,0:T(8,128)}, f32[1024,1]{1,0:T(8,128)}, bf16[1024,768]{1,0:T(8,128)(2,1)}, /*index=5*/bf16[16,768]{1,0:T(8,128)(2,1)}) custom-call(f32[1024,768]{1,0:T(8,128)} %get-tuple-element.103.hat_ref.hat_hbm, bf16[1024,768]{1,0:T(8,128)(2,1)} %get-tuple-element.104.low_ref, ...), custom_call_target="tpu_custom_call" | custom-call | flops 9663676416 | bytes 31457280 | tf_op jit(solution)/shard_map/feed/pallas_call | solution.py:427
  47.9 3.1 %collective-permute-start = (bf16[16,768]{1,0:T(8,128)(2,1)}, bf16[16,768]{1,0:T(8,128)(2,1)S(1)}, u32[]{:S(2)}, u32[]{:S(2)}) collective-permute-start(bf16[16,768]{1,0:T(8,128)(2,1)} %get-tuple-element.105.own_ref), channel_id=1, source_target_pairs={{0,8},{1,9},{2,10},{3,11},{4,12},{5,13},{6,14},{7,15},{8,0},{9,1},... | collective-permute-start | bytes 73736 | tf_op jit(solution)/shard_map/ppermute | solution.py:42
  51.0 2.6 collective-permute-start.1
  54.4 1.9 collective-permute-done.1
  56.3 3.1 %collective-permute-done.2 = bf16[16,768]{1,0:T(8,128)(2,1)S(1)} collective-permute-done((bf16[16,768]{1,0:T(8,128)(2,1)}, bf16[16,768]{1,0:T(8,128)(2,1)S(1)}, u32[]{:S(2)}, u32[]{:S(2)}) %collective-permute-start.2) | collective-permute-done | bytes 24608 | tf_op jit(solution)/shard_map/ppermute | solution.py:42
  59.4 1.5 collective-permute-start.3
  60.9 1.5 collective-permute-start.4
  62.9 1.8 collective-permute-done.3
  64.7 1.2 collective-permute-done.4
  66.0 2.0 collective-permute-done.5
  70.7 17.6 %outer_back.1 = (f32[1,1]{1,0:T(1,128)}, f32[1,3072]{1,0:T(1,128)}, bf16[1536,768]{1,0:T(8,128)(2,1)}, bf16[1536,768]{1,0:T(8,128)(2,1)}, f32[1024,768]{1,0:T(8,128)}, /*index=5*/bf16[1024,768]{1,0:T(8,128)(2,1)}) custom-call(s32[2]{0:T(128)} %pad_add_fusion.info_ref, s32[512]{0:T(512)} %partner_ref.1, f32[1]{0:T(128)S(6)} %copy.73.cool_ref, ...), custom_call_target="tpu_custom_call" | custom-call | flops 4831838208 | bytes 20971520 | tf_op jit(solution)/shard_map/outer_back/pallas_call | solution.py:543
  88.5 4.6 %collective-permute-done.7 = bf16[1536,768]{1,0:T(8,128)(2,1)S(1)} collective-permute-done((bf16[1536,768]{1,0:T(8,128)(2,1)}, bf16[1536,768]{1,0:T(8,128)(2,1)S(1)}, u32[]{:S(2)}, u32[]{:S(2)}) %collective-permute-start.7) | collective-permute-done | bytes 2359328 | tf_op jit(solution)/shard_map/ppermute | solution.py:42
  93.2 2.3 convert_add_fusion.2
  96.2 26.9 %inner_back.1 = (bf16[2304,512]{1,0:T(8,128)(2,1)}, bf16[2304,512]{1,0:T(8,128)(2,1)}, f32[1,3072]{1,0:T(1,128)S(1)}, bf16[1024,768]{1,0:T(8,128)(2,1)S(1)}, bf1...) custom-call(s32[2]{0:T(128)S(1)} %copy-done.6, bf16[1024,768]{1,0:T(8,128)(2,1)S(1)} %copy-done.7, ...), custom_call_target="tpu_custom_call" | custom-call | flops 14495514624 | bytes 41943040 | tf_op jit(solution)/shard_map/inner_back/pallas_call | solution.py:642
  123.1 1.4 convert_add_fusion.5
  124.7 1.1 collective-permute-start.11
  125.8 3.6 %collective-permute-done.9 = bf16[2304,512]{1,0:T(8,128)(2,1)} collective-permute-done((bf16[2304,512]{1,0:T(8,128)(2,1)}, bf16[2304,512]{1,0:T(8,128)(2,1)}, u32[]{:S(2)}, u32[]{:S(2)}) %collective-permute-start.9) | collective-permute-done | bytes 2359328 | tf_op jit(solution)/shard_map/ppermute | solution.py:42
  129.4 3.2 %add_convert_fusion.1 = (bf16[1152,512]{1,0:T(8,128)(2,1)S(1)}, f32[1152,512]{1,0:T(8,128)S(1)}) fusion(bf16[2304,512]{1,0:T(8,128)(2,1)} %collective-permute-done.9, s32[]{:T(128)S(6)} %select_n.445, bf16[2304,512]{1,0:T(8,128)(2,1)} %get-tuple-element.123, s32[]{:T(128)S(6)} %select_n.441), kind=kLoop, calls=%fused_computation.5 | loop fusion | flops 4128768 | bytes 8257544 | tf_op jit(solution)/shard_map/convert_element_type | solution.py:88
  132.7 1.4 collective-permute-start.10
  135.8 3.6 %collective-permute-start.14 = (bf16[96,768]{1,0:T(8,128)(2,1)S(1)}, bf16[96,768]{1,0:T(8,128)(2,1)S(1)}, u32[]{:S(2)}, u32[]{:S(2)}) collective-permute-start(bf16[96,768]{1,0:T(8,128)(2,1)S(1)} %get-tuple-element.241), channel_id=1, source_target_pairs={{0,24},{1,25},{2,26},{3,27},{4,28},{5,29},{6,30},{7,31},{8,16},{9,... | collective-permute-start | bytes 442376 | tf_op jit(solution)/shard_map/ppermute | solution.py:42
  139.4 23.7 %attend_back.1 = (bf16[1024,768]{1,0:T(8,128)(2,1)S(1)}, bf16[1024,768]{1,0:T(8,128)(2,1)S(1)}, bf16[1024,768]{1,0:T(8,128)(2,1)S(1)}, bf16[2,768,768]{2,1,0:T(8...) custom-call(s32[1]{0:T(128)} %bitcast.1.core_ref, bf16[768,1024]{1,0:T(8,128)(2,1)S(1)} %copy-done.11, ...), custom_call_target="tpu_custom_call" | custom-call | flops 9663676416 | bytes 31457280 | tf_op jit(solution)/shard_map/attend_back/pallas_call | solution.py:743
  163.3 1.8 add_convert_fusion.4
  166.3 3.6 %collective-permute-start.17 = (bf16[96,768]{1,0:T(8,128)(2,1)S(1)}, bf16[96,768]{1,0:T(8,128)(2,1)S(1)}, u32[]{:S(2)}, u32[]{:S(2)}) collective-permute-start(bf16[96,768]{1,0:T(8,128)(2,1)S(1)} %add_convert_fusion.14), channel_id=1, source_target_pairs={{0,24},{1,25},{2,26},{3,27},{4,28},{5,29},{6,30},{7,31},{8,16},{9,... | collective-permute-start | bytes 442376 | tf_op jit(solution)/shard_map/ppermute | solution.py:42
  171.0 2.0 collective-permute-done.19
  173.0 6.4 %collective-permute-done.18 = bf16[96,768]{1,0:T(8,128)(2,1)S(1)} collective-permute-done((bf16[96,768]{1,0:T(8,128)(2,1)S(1)}, bf16[96,768]{1,0:T(8,128)(2,1)S(1)}, u32[]{:S(2)}, u32[]{:S(2)}) %collective-permute-start.18) | collective-permute-done | bytes 147488 | tf_op jit(solution)/shard_map/ppermute | solution.py:42
  180.5 1.2 collective-permute-start.22
  181.6 2.8 convert_add_fusion
  185.2 1.9 add_convert_fusion.12
  187.0 7.5 %collective-permute-done.22 = bf16[384,768]{1,0:T(8,128)(2,1)} collective-permute-done((bf16[384,768]{1,0:T(8,128)(2,1)S(1)}, bf16[384,768]{1,0:T(8,128)(2,1)}, u32[]{:S(2)}, u32[]{:S(2)}) %collective-permute-start.22) | collective-permute-done | bytes 589856 | tf_op jit(solution)/shard_map/ppermute | solution.py:42
  194.5 1.2 constant_dynamic-update-slice_fusion.28
  195.8 1.2 broadcast_select_fusion.1
  197.0 1.7 collective-permute-start.27
  198.7 2.9 collective-permute-start.20
  201.6 2.4 collective-permute-start.24
  204.0 1.1 convert_add_fusion.3
  205.1 1.8 collective-permute-done.20
  207.0 4.7 %collective-permute-done.23 = bf16[144,512]{1,0:T(8,128)(2,1)S(1)} collective-permute-done((bf16[144,512]{1,0:T(8,128)(2,1)}, bf16[144,512]{1,0:T(8,128)(2,1)S(1)}, u32[]{:S(2)}, u32[]{:S(2)}) %collective-permute-start.23) | collective-permute-done | bytes 147488 | tf_op jit(solution)/shard_map/ppermute | solution.py:42
  212.7 2.2 collective-permute-start.29
  215.0 2.4 collective-permute-start.25
  217.3 3.2 %collective-permute-done.27 = bf16[768,768]{1,0:T(8,128)(2,1)} collective-permute-done((bf16[768,768]{1,0:T(8,128)(2,1)}, bf16[768,768]{1,0:T(8,128)(2,1)}, u32[]{:S(2)}, u32[]{:S(2)}) %collective-permute-start.27) | collective-permute-done | bytes 1179680 | tf_op jit(solution)/shard_map/ppermute | solution.py:42
  220.5 2.6 maximum_select_fusion.kept_ref
  223.2 3.2 %collective-permute-done.28 = bf16[144,512]{1,0:T(8,128)(2,1)S(1)} collective-permute-done((bf16[144,512]{1,0:T(8,128)(2,1)S(1)}, bf16[144,512]{1,0:T(8,128)(2,1)S(1)}, u32[]{:S(2)}, u32[]{:S(2)}) %collective-permute-start.28) | collective-permute-done | bytes 147488 | tf_op jit(solution)/shard_map/ppermute | solution.py:42
  226.8 1.6 collective-permute-start.30
  228.5 2.5 collective-permute-start.31
  231.0 2.3 collective-permute-start.33
  233.4 1.9 collective-permute-done.31
  235.3 8.0 %collective-permute-done.32 = bf16[96,768]{1,0:T(8,128)(2,1)S(1)} collective-permute-done((bf16[96,768]{1,0:T(8,128)(2,1)S(1)}, bf16[96,768]{1,0:T(8,128)(2,1)S(1)}, u32[]{:S(2)}, u32[]{:S(2)}) %collective-permute-start.32) | collective-permute-done | bytes 147488 | tf_op jit(solution)/shard_map/ppermute | solution.py:42
  243.4 2.6 collective-permute-start.36
  246.2 2.3 collective-permute-start.34
  249.7 8.7 %input_back.1 = f32[1024,768]{1,0:T(8,128)} custom-call(f32[1024,768]{1,0:T(8,128)} %get-tuple-element.163.first_ref, bf16[1024,768]{1,0:T(8,128)(2,1)} %copy-done, bf16[1024,768]{1,0:T(8,128)(2,1)} %copy-done.1, bf16[1024,768]{1,0:T(8,128)(2,1)} %copy-done.2, bf16[768,2304]{1,0:T(8,128)(2,1)} %refs_3_.1), custom_call_target="tpu_custom_call" | custom-call | flops 3623878656 | bytes 15728640 | tf_op jit(solution)/shard_map/input_back/pallas_call | solution.py:776
  258.8 6.3 %collective-permute-done.38 = bf16[1152,512]{1,0:T(8,128)(2,1)S(1)} collective-permute-done((bf16[1152,512]{1,0:T(8,128)(2,1)S(1)}, bf16[1152,512]{1,0:T(8,128)(2,1)S(1)}, u32[]{:S(2)}, u32[]{:S(2)}) %collective-permute-start.38) | collective-permute-done | bytes 1179680 | tf_op jit(solution)/shard_map/ppermute | solution.py:42
  265.9 1.6 collective-permute-start.37
  267.5 8.4 %collective-permute-done.37 = bf16[384,768]{1,0:T(8,128)(2,1)S(1)} collective-permute-done((bf16[384,768]{1,0:T(8,128)(2,1)S(1)}, bf16[384,768]{1,0:T(8,128)(2,1)S(1)}, u32[]{:S(2)}, u32[]{:S(2)}) %collective-permute-start.37) | collective-permute-done | bytes 589856 | tf_op jit(solution)/shard_map/ppermute | solution.py:42
  277.0 1.2 collective-permute-done.41
  278.3 1.1 collective-permute-start.42
  280.3 2.4 collective-permute-start.45
  282.7 3.8 %finish.3 = f32[768,3072]{1,0:T(8,128)} custom-call(s32[1]{0:T(128)} %bitcast.1.core_ref, bf16[2304,512]{1,0:T(8,128)(2,1)S(1)} %maximum_select_fusion.1.kept_ref, bf16[2304,512]{1,0:T(8,128)(2,1)S(1)} %collective-permute-done.43.got_ref), custom_call_target="tpu_custom_call" | custom-call | bytes 14155776 | tf_op jit(solution)/shard_map/finish/pallas_call | solution.py:807
  286.6 3.8 %finish.4 = f32[3072,768]{1,0:T(8,128)} custom-call(s32[1]{0:T(128)} %bitcast.1.core_ref, bf16[1536,768]{1,0:T(8,128)(2,1)S(1)} %maximum_select_fusion.kept_ref, bf16[1536,768]{1,0:T(8,128)(2,1)S(1)} %collective-permute-done.40.got_ref), custom_call_target="tpu_custom_call" | custom-call | bytes 14155776 | tf_op jit(solution)/shard_map/finish/pallas_call | solution.py:807
  290.4 2.0 collective-permute-done.39
  294.0 1.4 collective-permute-start.48
  295.4 1.3 collective-permute-start.49
  298.1 2.3 collective-permute-done.49
  301.7 3.9 %finish.5 = (f32[768,2304]{1,0:T(8,128)}, f32[768,768]{1,0:T(8,128)}) custom-call(s32[1]{0:T(128)} %bitcast.1.core_ref, bf16[1536,768]{1,0:T(8,128)(2,1)S(1)} %maximum_select_fusion.2.kept_ref, bf16[1536,768]{1,0:T(8,128)(2,1)S(1)} %collective-permute-done.46.got_ref), custom_call_target="tpu_custom_call" | custom-call | bytes 14155776 | tf_op jit(solution)/shard_map/finish/pallas_call | solution.py:807
  (148 shorter events, 21.1 us)
Async XLA Ops:
  47.9 6.5 %collective-permute-start = (bf16[16,768]{1,0:T(8,128)(2,1)}, bf16[16,768]{1,0:T(8,128)(2,1)S(1)}, u32[]{:S(2)}, u32[]{:S(2)}) collective-permute-start(bf16[16,768]{1,0:T(8,128)(2,1)} %get-tuple-element.105.own_ref), channel_id=1, source_target_pairs={{0,8},{1,9},{2,10},{3,11},{4,12},{5,13},{6,14},{7,15},{8,0},{9,1},... | collective-permute-start | bytes 73736 | tf_op jit(solution)/shard_map/ppermute | solution.py:42
  51.0 5.3 %collective-permute-start.1 = (bf16[16,768]{1,0:T(8,128)(2,1)}, bf16[16,768]{1,0:T(8,128)(2,1)S(1)}, u32[]{:S(2)}, u32[]{:S(2)}) collective-permute-start(bf16[16,768]{1,0:T(8,128)(2,1)} %get-tuple-element.105.own_ref), channel_id=1, source_target_pairs={{0,16},{1,17},{2,18},{3,19},{4,20},{5,21},{6,22},{7,23},{8,24},{9,... | collective-permute-start | bytes 73736 | tf_op jit(solution)/shard_map/ppermute | solution.py:42
  53.6 5.8 %collective-permute-start.2 = (bf16[16,768]{1,0:T(8,128)(2,1)}, bf16[16,768]{1,0:T(8,128)(2,1)S(1)}, u32[]{:S(2)}, u32[]{:S(2)}) collective-permute-start(bf16[16,768]{1,0:T(8,128)(2,1)} %get-tuple-element.105.own_ref), channel_id=1, source_target_pairs={{0,24},{1,25},{2,26},{3,27},{4,28},{5,29},{6,30},{7,31},{8,16},{9,... | collective-permute-start | bytes 73736 | tf_op jit(solution)/shard_map/ppermute | solution.py:42
  59.4 5.3 %collective-permute-start.3 = (bf16[64,768]{1,0:T(8,128)(2,1)S(1)}, bf16[64,768]{1,0:T(8,128)(2,1)S(1)}, u32[]{:S(2)}, u32[]{:S(2)}) collective-permute-start(bf16[64,768]{1,0:T(8,128)(2,1)S(1)} %get-tuple-element.257), channel_id=1, source_target_pairs={{0,2},{1,3},{2,0},{3,1},{4,6},{5,7},{6,4},{7,5},{8,10},{9,11},{10,... | collective-permute-start | bytes 294920 | tf_op jit(solution)/shard_map/ppermute | solution.py:42
  60.9 5.0 %collective-permute-start.4 = (bf16[64,768]{1,0:T(8,128)(2,1)S(1)}, bf16[64,768]{1,0:T(8,128)(2,1)S(1)}, u32[]{:S(2)}, u32[]{:S(2)}) collective-permute-start(bf16[64,768]{1,0:T(8,128)(2,1)S(1)} %get-tuple-element.257), channel_id=1, source_target_pairs={{0,4},{1,5},{2,6},{3,7},{4,0},{5,1},{6,2},{7,3},{8,12},{9,13},{10,... | collective-permute-start | bytes 294920 | tf_op jit(solution)/shard_map/ppermute | solution.py:42
  62.5 5.5 %collective-permute-start.5 = (bf16[64,768]{1,0:T(8,128)(2,1)S(1)}, bf16[64,768]{1,0:T(8,128)(2,1)S(1)}, u32[]{:S(2)}, u32[]{:S(2)}) collective-permute-start(bf16[64,768]{1,0:T(8,128)(2,1)S(1)} %get-tuple-element.257), channel_id=1, source_target_pairs={{0,6},{1,7},{2,4},{3,5},{4,2},{5,3},{6,0},{7,1},{8,14},{9,15},{10,... | collective-permute-start | bytes 294920 | tf_op jit(solution)/shard_map/ppermute | solution.py:42
  68.0 1.8 collective-permute-start.6
  88.3 4.8 %collective-permute-start.7 = (bf16[1536,768]{1,0:T(8,128)(2,1)}, bf16[1536,768]{1,0:T(8,128)(2,1)S(1)}, u32[]{:S(2)}, u32[]{:S(2)}) collective-permute-start(bf16[1536,768]{1,0:T(8,128)(2,1)} %get-tuple-element.114), channel_id=1, source_target_pairs={{0,1},{1,0},{2,3},{3,2},{4,5},{5,4},{6,7},{7,6},{8,9},{9,8},{10,11... | collective-permute-start | bytes 7077896 | tf_op jit(solution)/shard_map/ppermute | solution.py:42
  93.2 2.9 copy-start.3
  93.2 2.9 copy-start.4
  93.2 2.9 copy-start.6
  93.2 2.9 copy-start.7
  93.2 3.0 copy-start.12
  93.2 3.1 %copy-start.13 = (f32[1024,1]{1,0:T(8,128)S(1)}, f32[1024,1]{1,0:T(8,128)}, u32[]{:S(2)}) copy-start(f32[1024,1]{1,0:T(8,128)} %get-tuple-element.119.rstd_ref) | copy-start | bytes 12292
  95.5 27.6 %collective-permute-start.8 = (bf16[768,768]{1,0:T(8,128)(2,1)S(1)}, bf16[768,768]{1,0:T(8,128)(2,1)S(1)}, u32[]{:S(2)}, u32[]{:S(2)}) collective-permute-start(bf16[768,768]{1,0:T(8,128)(2,1)S(1)} %get-tuple-element.227), channel_id=1, source_target_pairs={{0,2},{1,5},{2,0},{3,7},{4,6},{5,1},{6,4},{7,3},{8,10},{9,13},{10,... | collective-permute-start | bytes 3538952 | tf_op jit(solution)/shard_map/ppermute | solution.py:42
  124.5 4.9 %collective-permute-start.9 = (bf16[2304,512]{1,0:T(8,128)(2,1)}, bf16[2304,512]{1,0:T(8,128)(2,1)}, u32[]{:S(2)}, u32[]{:S(2)}) collective-permute-start(bf16[2304,512]{1,0:T(8,128)(2,1)} %get-tuple-element.127), channel_id=1, source_target_pairs={{0,1},{1,0},{2,3},{3,2},{4,5},{5,4},{6,7},{7,6},{8,9},{9,8},{10,11... | collective-permute-start | bytes 7077896 | tf_op jit(solution)/shard_map/ppermute | solution.py:42
  124.7 10.1 %collective-permute-start.11 = (bf16[384,768]{1,0:T(8,128)(2,1)}, bf16[384,768]{1,0:T(8,128)(2,1)S(1)}, u32[]{:S(2)}, u32[]{:S(2)}) collective-permute-start(bf16[384,768]{1,0:T(8,128)(2,1)} %get-tuple-element.233), channel_id=1, source_target_pairs={{0,4},{1,3},{2,6},{3,1},{4,0},{5,7},{6,2},{7,5},{8,12},{9,11},{10,... | collective-permute-start | bytes 1769480 | tf_op jit(solution)/shard_map/ppermute | solution.py:42
  129.4 5.4 %copy-start.15 = (f32[384,768]{1,0:T(8,128)S(1)}, f32[384,768]{1,0:T(8,128)}, u32[]{:S(2)}) copy-start(f32[384,768]{1,0:T(8,128)} %get-tuple-element.232) | copy-start | bytes 3538948
  129.4 9.9 %copy-start.9 = (bf16[1024,768]{1,0:T(8,128)(2,1)S(1)}, bf16[1024,768]{1,0:T(8,128)(2,1)}, u32[]{:S(2)}) copy-start(bf16[1024,768]{1,0:T(8,128)(2,1)} %get-tuple-element.134.k_ref) | copy-start | bytes 4718596
  129.4 9.9 %copy-start.10 = (bf16[1024,768]{1,0:T(8,128)(2,1)S(1)}, bf16[1024,768]{1,0:T(8,128)(2,1)}, u32[]{:S(2)}) copy-start(bf16[1024,768]{1,0:T(8,128)(2,1)} %get-tuple-element.135.v_ref) | copy-start | bytes 4718596
  129.4 9.9 %copy-start.11 = (bf16[768,1024]{1,0:T(8,128)(2,1)S(1)}, bf16[768,1024]{1,0:T(8,128)(2,1)}, u32[]{:S(2)}) copy-start(bf16[768,1024]{1,0:T(8,128)(2,1)} %get-tuple-element.130.x_t_ref) | copy-start | bytes 4718596
  132.7 6.7 %copy-start.5 = (s32[2,512]{1,0:T(2,128)S(1)}, s32[2,512]{1,0:T(2,128)}, u32[]{:S(2)}) copy-start(s32[2,512]{1,0:T(2,128)} %seg_ref.7) | copy-start | bytes 12292
  132.7 6.7 %copy-start.8 = (bf16[1024,768]{1,0:T(8,128)(2,1)S(1)}, bf16[1024,768]{1,0:T(8,128)(2,1)}, u32[]{:S(2)}) copy-start(bf16[1024,768]{1,0:T(8,128)(2,1)} %get-tuple-element.133.q_ref) | copy-start | bytes 4718596
  132.7 6.7 %copy-start.14 = (f32[6,4,512]{2,1,0:T(4,128)S(1)}, f32[6,4,512]{2,1,0:T(4,128)}, u32[]{:S(2)}) copy-start(f32[6,4,512]{2,1,0:T(4,128)} %get-tuple-element.132.lse_ref) | copy-start | bytes 147460
  132.7 30.6 %collective-permute-start.10 = (bf16[1152,512]{1,0:T(8,128)(2,1)S(1)}, bf16[1152,512]{1,0:T(8,128)(2,1)S(1)}, u32[]{:S(2)}, u32[]{:S(2)}) collective-permute-start(bf16[1152,512]{1,0:T(8,128)(2,1)S(1)} %get-tuple-element.224), channel_id=1, source_target_pairs={{0,2},{1,5},{2,0},{3,7},{4,6},{5,1},{6,4},{7,3},{8,10},{9,13},{10,... | collective-permute-start | bytes 3538952 | tf_op jit(solution)/shard_map/ppermute | solution.py:42
  134.9 28.3 %collective-permute-start.12 = (bf16[96,768]{1,0:T(8,128)(2,1)S(1)}, bf16[96,768]{1,0:T(8,128)(2,1)S(1)}, u32[]{:S(2)}, u32[]{:S(2)}) collective-permute-start(bf16[96,768]{1,0:T(8,128)(2,1)S(1)} %get-tuple-element.242), channel_id=1, source_target_pairs={{0,8},{1,9},{2,10},{3,11},{4,12},{5,13},{6,14},{7,15},{8,0},{9,1},... | collective-permute-start | bytes 442376 | tf_op jit(solution)/shard_map/ppermute | solution.py:42
  135.0 28.2 %collective-permute-start.13 = (bf16[96,768]{1,0:T(8,128)(2,1)S(1)}, bf16[96,768]{1,0:T(8,128)(2,1)S(1)}, u32[]{:S(2)}, u32[]{:S(2)}) collective-permute-start(bf16[96,768]{1,0:T(8,128)(2,1)S(1)} %get-tuple-element.240), channel_id=1, source_target_pairs={{0,16},{1,17},{2,18},{3,19},{4,20},{5,21},{6,22},{7,23},{8,24},{9,... | collective-permute-start | bytes 442376 | tf_op jit(solution)/shard_map/ppermute | solution.py:42
  135.8 27.4 %collective-permute-start.14 = (bf16[96,768]{1,0:T(8,128)(2,1)S(1)}, bf16[96,768]{1,0:T(8,128)(2,1)S(1)}, u32[]{:S(2)}, u32[]{:S(2)}) collective-permute-start(bf16[96,768]{1,0:T(8,128)(2,1)S(1)} %get-tuple-element.241), channel_id=1, source_target_pairs={{0,24},{1,25},{2,26},{3,27},{4,28},{5,29},{6,30},{7,31},{8,16},{9,... | collective-permute-start | bytes 442376 | tf_op jit(solution)/shard_map/ppermute | solution.py:42
  165.5 16.1 %collective-permute-start.16 = (bf16[1536,768]{1,0:T(8,128)(2,1)}, bf16[1536,768]{1,0:T(8,128)(2,1)}, u32[]{:S(2)}, u32[]{:S(2)}) collective-permute-start(bf16[1536,768]{1,0:T(8,128)(2,1)} %bitcast.4), channel_id=1, source_target_pairs={{0,1},{1,0},{2,3},{3,2},{4,5},{5,4},{6,7},{7,6},{8,9},{9,8},{10,11... | collective-permute-start | bytes 7077896 | tf_op jit(solution)/shard_map/ppermute | solution.py:42
  165.5 7.5 %collective-permute-start.19 = (bf16[96,768]{1,0:T(8,128)(2,1)S(1)}, bf16[96,768]{1,0:T(8,128)(2,1)S(1)}, u32[]{:S(2)}, u32[]{:S(2)}) collective-permute-start(bf16[96,768]{1,0:T(8,128)(2,1)S(1)} %add_convert_fusion.14), channel_id=1, source_target_pairs={{0,8},{1,9},{2,10},{3,11},{4,12},{5,13},{6,14},{7,15},{8,0},{9,1},... | collective-permute-start | bytes 442376 | tf_op jit(solution)/shard_map/ppermute | solution.py:42
  165.5 13.9 %collective-permute-start.18 = (bf16[96,768]{1,0:T(8,128)(2,1)S(1)}, bf16[96,768]{1,0:T(8,128)(2,1)S(1)}, u32[]{:S(2)}, u32[]{:S(2)}) collective-permute-start(bf16[96,768]{1,0:T(8,128)(2,1)S(1)} %add_convert_fusion.14), channel_id=1, source_target_pairs={{0,16},{1,17},{2,18},{3,19},{4,20},{5,21},{6,22},{7,23},{8,24},{9,... | collective-permute-start | bytes 442376 | tf_op jit(solution)/shard_map/ppermute | solution.py:42
  166.3 13.1 %collective-permute-start.17 = (bf16[96,768]{1,0:T(8,128)(2,1)S(1)}, bf16[96,768]{1,0:T(8,128)(2,1)S(1)}, u32[]{:S(2)}, u32[]{:S(2)}) collective-permute-start(bf16[96,768]{1,0:T(8,128)(2,1)S(1)} %add_convert_fusion.14), channel_id=1, source_target_pairs={{0,24},{1,25},{2,26},{3,27},{4,28},{5,29},{6,30},{7,31},{8,16},{9,... | collective-permute-start | bytes 442376 | tf_op jit(solution)/shard_map/ppermute | solution.py:42
  169.9 15.3 %collective-permute-start.15 = (bf16[576,512]{1,0:T(8,128)(2,1)}, bf16[576,512]{1,0:T(8,128)(2,1)}, u32[]{:S(2)}, u32[]{:S(2)}) collective-permute-start(bf16[576,512]{1,0:T(8,128)(2,1)} %get-tuple-element.230), channel_id=1, source_target_pairs={{0,4},{1,3},{2,6},{3,1},{4,0},{5,7},{6,2},{7,5},{8,12},{9,11},{10,... | collective-permute-start | bytes 1769480 | tf_op jit(solution)/shard_map/ppermute | solution.py:42
  180.5 14.1 %collective-permute-start.22 = (bf16[384,768]{1,0:T(8,128)(2,1)S(1)}, bf16[384,768]{1,0:T(8,128)(2,1)}, u32[]{:S(2)}, u32[]{:S(2)}) collective-permute-start(bf16[384,768]{1,0:T(8,128)(2,1)S(1)} %pad_maximum_fusion), channel_id=1, source_target_pairs={{0,4},{1,3},{2,6},{3,1},{4,0},{5,7},{6,2},{7,5},{8,12},{9,11},{10,... | collective-permute-start | bytes 1769480 | tf_op jit(solution)/shard_map/ppermute | solution.py:42
  184.5 19.5 %collective-permute-start.21 = (bf16[768,768]{1,0:T(8,128)(2,1)S(1)}, bf16[768,768]{1,0:T(8,128)(2,1)S(1)}, u32[]{:S(2)}, u32[]{:S(2)}) collective-permute-start(bf16[768,768]{1,0:T(8,128)(2,1)S(1)} %get-tuple-element.223), channel_id=1, source_target_pairs={{0,2},{1,5},{2,0},{3,7},{4,6},{5,1},{6,4},{7,3},{8,10},{9,13},{10,... | collective-permute-start | bytes 3538952 | tf_op jit(solution)/shard_map/ppermute | solution.py:42
  197.0 23.5 %collective-permute-start.27 = (bf16[768,768]{1,0:T(8,128)(2,1)}, bf16[768,768]{1,0:T(8,128)(2,1)}, u32[]{:S(2)}, u32[]{:S(2)}) collective-permute-start(bf16[768,768]{1,0:T(8,128)(2,1)} %broadcast_select_fusion.1), channel_id=1, source_target_pairs={{0,2},{1,5},{2,0},{3,7},{4,6},{5,1},{6,4},{7,3},{8,10},{9,13},{10,... | collective-permute-start | bytes 3538952 | tf_op jit(solution)/shard_map/ppermute | solution.py:42
  198.7 8.3 %collective-permute-start.20 = (bf16[144,512]{1,0:T(8,128)(2,1)}, bf16[144,512]{1,0:T(8,128)(2,1)S(1)}, u32[]{:S(2)}, u32[]{:S(2)}) collective-permute-start(bf16[144,512]{1,0:T(8,128)(2,1)} %get-tuple-element.239), channel_id=1, source_target_pairs={{0,8},{1,9},{2,10},{3,11},{4,12},{5,13},{6,14},{7,15},{8,0},{9,1},... | collective-permute-start | bytes 442376 | tf_op jit(solution)/shard_map/ppermute | solution.py:42
  201.6 10.0 %collective-permute-start.23 = (bf16[144,512]{1,0:T(8,128)(2,1)}, bf16[144,512]{1,0:T(8,128)(2,1)S(1)}, u32[]{:S(2)}, u32[]{:S(2)}) collective-permute-start(bf16[144,512]{1,0:T(8,128)(2,1)} %get-tuple-element.237), channel_id=1, source_target_pairs={{0,16},{1,17},{2,18},{3,19},{4,20},{5,21},{6,22},{7,23},{8,24},{9,... | collective-permute-start | bytes 442376 | tf_op jit(solution)/shard_map/ppermute | solution.py:42
  201.6 10.0 %collective-permute-start.24 = (bf16[144,512]{1,0:T(8,128)(2,1)}, bf16[144,512]{1,0:T(8,128)(2,1)S(1)}, u32[]{:S(2)}, u32[]{:S(2)}) collective-permute-start(bf16[144,512]{1,0:T(8,128)(2,1)} %get-tuple-element.238), channel_id=1, source_target_pairs={{0,24},{1,25},{2,26},{3,27},{4,28},{5,29},{6,30},{7,31},{8,16},{9,... | collective-permute-start | bytes 442376 | tf_op jit(solution)/shard_map/ppermute | solution.py:42
  205.1 18.0 %collective-permute-start.26 = (bf16[384,768]{1,0:T(8,128)(2,1)}, bf16[384,768]{1,0:T(8,128)(2,1)S(1)}, u32[]{:S(2)}, u32[]{:S(2)}) collective-permute-start(bf16[384,768]{1,0:T(8,128)(2,1)} %get-tuple-element.229), channel_id=1, source_target_pairs={{0,4},{1,3},{2,6},{3,1},{4,0},{5,7},{6,2},{7,5},{8,12},{9,11},{10,... | collective-permute-start | bytes 1769480 | tf_op jit(solution)/shard_map/ppermute | solution.py:42
  212.7 10.5 %collective-permute-start.29 = (bf16[144,512]{1,0:T(8,128)(2,1)S(1)}, bf16[144,512]{1,0:T(8,128)(2,1)S(1)}, u32[]{:S(2)}, u32[]{:S(2)}) collective-permute-start(bf16[144,512]{1,0:T(8,128)(2,1)S(1)} %add_convert_fusion.10), channel_id=1, source_target_pairs={{0,8},{1,9},{2,10},{3,11},{4,12},{5,13},{6,14},{7,15},{8,0},{9,1},... | collective-permute-start | bytes 442376 | tf_op jit(solution)/shard_map/ppermute | solution.py:42
  214.9 11.5 %collective-permute-start.28 = (bf16[144,512]{1,0:T(8,128)(2,1)S(1)}, bf16[144,512]{1,0:T(8,128)(2,1)S(1)}, u32[]{:S(2)}, u32[]{:S(2)}) collective-permute-start(bf16[144,512]{1,0:T(8,128)(2,1)S(1)} %add_convert_fusion.10), channel_id=1, source_target_pairs={{0,16},{1,17},{2,18},{3,19},{4,20},{5,21},{6,22},{7,23},{8,24},{9,... | collective-permute-start | bytes 442376 | tf_op jit(solution)/shard_map/ppermute | solution.py:42
  215.0 11.4 %collective-permute-start.25 = (bf16[144,512]{1,0:T(8,128)(2,1)S(1)}, bf16[144,512]{1,0:T(8,128)(2,1)S(1)}, u32[]{:S(2)}, u32[]{:S(2)}) collective-permute-start(bf16[144,512]{1,0:T(8,128)(2,1)S(1)} %add_convert_fusion.10), channel_id=1, source_target_pairs={{0,24},{1,25},{2,26},{3,27},{4,28},{5,29},{6,30},{7,31},{8,16},{9,... | collective-permute-start | bytes 442376 | tf_op jit(solution)/shard_map/ppermute | solution.py:42
  226.7 6.7 %copy-start.18 = (f32[1,3072]{1,0:T(1,128)S(1)}, f32[1,3072]{1,0:T(1,128)}, u32[]{:S(2)}) copy-start(f32[1,3072]{1,0:T(1,128)} %get-tuple-element.170) | copy-start | bytes 36868
  226.8 21.7 %collective-permute-start.30 = (bf16[576,512]{1,0:T(8,128)(2,1)S(1)}, bf16[576,512]{1,0:T(8,128)(2,1)S(1)}, u32[]{:S(2)}, u32[]{:S(2)}) collective-permute-start(bf16[576,512]{1,0:T(8,128)(2,1)S(1)} %pad_maximum_fusion.1), channel_id=1, source_target_pairs={{0,4},{1,3},{2,6},{3,1},{4,0},{5,7},{6,2},{7,5},{8,12},{9,11},{10,... | collective-permute-start | bytes 1769480 | tf_op jit(solution)/shard_map/ppermute | solution.py:42
  228.5 6.9 %collective-permute-start.31 = (bf16[96,768]{1,0:T(8,128)(2,1)S(1)}, bf16[96,768]{1,0:T(8,128)(2,1)S(1)}, u32[]{:S(2)}, u32[]{:S(2)}) collective-permute-start(bf16[96,768]{1,0:T(8,128)(2,1)S(1)} %get-tuple-element.236), channel_id=1, source_target_pairs={{0,8},{1,9},{2,10},{3,11},{4,12},{5,13},{6,14},{7,15},{8,0},{9,1},... | collective-permute-start | bytes 442376 | tf_op jit(solution)/shard_map/ppermute | solution.py:42
  231.0 12.3 %collective-permute-start.32 = (bf16[96,768]{1,0:T(8,128)(2,1)S(1)}, bf16[96,768]{1,0:T(8,128)(2,1)S(1)}, u32[]{:S(2)}, u32[]{:S(2)}) collective-permute-start(bf16[96,768]{1,0:T(8,128)(2,1)S(1)} %get-tuple-element.235), channel_id=1, source_target_pairs={{0,16},{1,17},{2,18},{3,19},{4,20},{5,21},{6,22},{7,23},{8,24},{9,... | collective-permute-start | bytes 442376 | tf_op jit(solution)/shard_map/ppermute | solution.py:42
  231.0 12.3 %collective-permute-start.33 = (bf16[96,768]{1,0:T(8,128)(2,1)S(1)}, bf16[96,768]{1,0:T(8,128)(2,1)S(1)}, u32[]{:S(2)}, u32[]{:S(2)}) collective-permute-start(bf16[96,768]{1,0:T(8,128)(2,1)S(1)} %get-tuple-element.234), channel_id=1, source_target_pairs={{0,24},{1,25},{2,26},{3,27},{4,28},{5,29},{6,30},{7,31},{8,16},{9,... | collective-permute-start | bytes 442376 | tf_op jit(solution)/shard_map/ppermute | solution.py:42
  243.4 15.0 %collective-permute-start.36 = (bf16[96,768]{1,0:T(8,128)(2,1)S(1)}, bf16[96,768]{1,0:T(8,128)(2,1)S(1)}, u32[]{:S(2)}, u32[]{:S(2)}) collective-permute-start(bf16[96,768]{1,0:T(8,128)(2,1)S(1)} %add_convert_fusion.6), channel_id=1, source_target_pairs={{0,8},{1,9},{2,10},{3,11},{4,12},{5,13},{6,14},{7,15},{8,0},{9,1},... | collective-permute-start | bytes 442376 | tf_op jit(solution)/shard_map/ppermute | solution.py:42
  246.1 12.3 %collective-permute-start.35 = (bf16[96,768]{1,0:T(8,128)(2,1)S(1)}, bf16[96,768]{1,0:T(8,128)(2,1)S(1)}, u32[]{:S(2)}, u32[]{:S(2)}) collective-permute-start(bf16[96,768]{1,0:T(8,128)(2,1)S(1)} %add_convert_fusion.6), channel_id=1, source_target_pairs={{0,16},{1,17},{2,18},{3,19},{4,20},{5,21},{6,22},{7,23},{8,24},{9,... | collective-permute-start | bytes 442376 | tf_op jit(solution)/shard_map/ppermute | solution.py:42
  246.2 12.2 %collective-permute-start.34 = (bf16[96,768]{1,0:T(8,128)(2,1)S(1)}, bf16[96,768]{1,0:T(8,128)(2,1)S(1)}, u32[]{:S(2)}, u32[]{:S(2)}) collective-permute-start(bf16[96,768]{1,0:T(8,128)(2,1)S(1)} %add_convert_fusion.6), channel_id=1, source_target_pairs={{0,24},{1,25},{2,26},{3,27},{4,28},{5,29},{6,30},{7,31},{8,16},{9,... | collective-permute-start | bytes 442376 | tf_op jit(solution)/shard_map/ppermute | solution.py:42
  248.8 16.3 %collective-permute-start.38 = (bf16[1152,512]{1,0:T(8,128)(2,1)S(1)}, bf16[1152,512]{1,0:T(8,128)(2,1)S(1)}, u32[]{:S(2)}, u32[]{:S(2)}) collective-permute-start(bf16[1152,512]{1,0:T(8,128)(2,1)S(1)} %broadcast_select_fusion.2), channel_id=1, source_target_pairs={{0,2},{1,5},{2,0},{3,7},{4,6},{5,1},{6,4},{7,3},{8,10},{9,13},{10,... | collective-permute-start | bytes 3538952 | tf_op jit(solution)/shard_map/ppermute | solution.py:42
  265.8 14.5 %collective-permute-start.43 = (bf16[2304,512]{1,0:T(8,128)(2,1)S(1)}, bf16[2304,512]{1,0:T(8,128)(2,1)S(1)}, u32[]{:S(2)}, u32[]{:S(2)}) collective-permute-start(bf16[2304,512]{1,0:T(8,128)(2,1)S(1)} %maximum_select_fusion.1.kept_ref), channel_id=1, source_target_pairs={{0,1},{1,0},{2,3},{3,2},{4,5},{5,4},{6,7},{7,6},{8,9},{9,8},{10,11... | collective-permute-start | bytes 7077896 | tf_op jit(solution)/shard_map/ppermute | solution.py:42
  265.9 9.9 %collective-permute-start.37 = (bf16[384,768]{1,0:T(8,128)(2,1)S(1)}, bf16[384,768]{1,0:T(8,128)(2,1)S(1)}, u32[]{:S(2)}, u32[]{:S(2)}) collective-permute-start(bf16[384,768]{1,0:T(8,128)(2,1)S(1)} %pad_maximum_fusion.2), channel_id=1, source_target_pairs={{0,4},{1,3},{2,6},{3,1},{4,0},{5,7},{6,2},{7,5},{8,12},{9,11},{10,... | collective-permute-start | bytes 1769480 | tf_op jit(solution)/shard_map/ppermute | solution.py:42
  267.5 19.1 %collective-permute-start.40 = (bf16[1536,768]{1,0:T(8,128)(2,1)S(1)}, bf16[1536,768]{1,0:T(8,128)(2,1)S(1)}, u32[]{:S(2)}, u32[]{:S(2)}) collective-permute-start(bf16[1536,768]{1,0:T(8,128)(2,1)S(1)} %maximum_select_fusion.kept_ref), channel_id=1, source_target_pairs={{0,1},{1,0},{2,3},{3,2},{4,5},{5,4},{6,7},{7,6},{8,9},{9,8},{10,11... | collective-permute-start | bytes 7077896 | tf_op jit(solution)/shard_map/ppermute | solution.py:42
  276.1 16.3 %collective-permute-start.39 = (bf16[768,768]{1,0:T(8,128)(2,1)S(1)}, bf16[768,768]{1,0:T(8,128)(2,1)S(1)}, u32[]{:S(2)}, u32[]{:S(2)}) collective-permute-start(bf16[768,768]{1,0:T(8,128)(2,1)S(1)} %broadcast_select_fusion), channel_id=1, source_target_pairs={{0,2},{1,5},{2,0},{3,7},{4,6},{5,1},{6,4},{7,3},{8,10},{9,13},{10,... | collective-permute-start | bytes 3538952 | tf_op jit(solution)/shard_map/ppermute | solution.py:42
  277.0 1.2 collective-permute-start.41
  278.3 8.3 %collective-permute-start.42 = (f32[4,3072]{1,0:T(4,128)S(1)}, f32[4,3072]{1,0:T(4,128)S(1)}, u32[]{:S(2)}, u32[]{:S(2)}) collective-permute-start(f32[4,3072]{1,0:T(4,128)S(1)} %add.315), channel_id=1, source_target_pairs={{0,8},{1,9},{2,10},{3,11},{4,12},{5,13},{6,14},{7,15},{8,0},{9,1},... | collective-permute-start | bytes 147464 | tf_op jit(solution)/shard_map/ppermute | solution.py:42
  279.4 7.2 %collective-permute-start.44 = (f32[4,3072]{1,0:T(4,128)S(1)}, f32[4,3072]{1,0:T(4,128)S(1)}, u32[]{:S(2)}, u32[]{:S(2)}) collective-permute-start(f32[4,3072]{1,0:T(4,128)S(1)} %add.315), channel_id=1, source_target_pairs={{0,16},{1,17},{2,18},{3,19},{4,20},{5,21},{6,22},{7,23},{8,24},{9,... | collective-permute-start | bytes 147464 | tf_op jit(solution)/shard_map/ppermute | solution.py:42
  280.3 6.2 %collective-permute-start.45 = (f32[4,3072]{1,0:T(4,128)S(1)}, f32[4,3072]{1,0:T(4,128)S(1)}, u32[]{:S(2)}, u32[]{:S(2)}) collective-permute-start(f32[4,3072]{1,0:T(4,128)S(1)} %add.315), channel_id=1, source_target_pairs={{0,24},{1,25},{2,26},{3,27},{4,28},{5,29},{6,30},{7,31},{8,16},{9,... | collective-permute-start | bytes 147464 | tf_op jit(solution)/shard_map/ppermute | solution.py:42
  293.1 8.6 %collective-permute-start.46 = (bf16[1536,768]{1,0:T(8,128)(2,1)S(1)}, bf16[1536,768]{1,0:T(8,128)(2,1)S(1)}, u32[]{:S(2)}, u32[]{:S(2)}) collective-permute-start(bf16[1536,768]{1,0:T(8,128)(2,1)S(1)} %maximum_select_fusion.2.kept_ref), channel_id=1, source_target_pairs={{0,1},{1,0},{2,3},{3,2},{4,5},{5,4},{6,7},{7,6},{8,9},{9,8},{10,11... | collective-permute-start | bytes 7077896 | tf_op jit(solution)/shard_map/ppermute | solution.py:42
  293.1 4.2 %collective-permute-start.47 = (f32[4,3072]{1,0:T(4,128)S(1)}, f32[4,3072]{1,0:T(4,128)S(1)}, u32[]{:S(2)}, u32[]{:S(2)}) collective-permute-start(f32[4,3072]{1,0:T(4,128)S(1)} %add_add_fusion.1), channel_id=1, source_target_pairs={{0,2},{1,3},{2,0},{3,1},{4,6},{5,7},{6,4},{7,5},{8,10},{9,11},{10,... | collective-permute-start | bytes 147464 | tf_op jit(solution)/shard_map/ppermute | solution.py:42
  294.0 4.1 %collective-permute-start.48 = (f32[4,3072]{1,0:T(4,128)S(1)}, f32[4,3072]{1,0:T(4,128)S(1)}, u32[]{:S(2)}, u32[]{:S(2)}) collective-permute-start(f32[4,3072]{1,0:T(4,128)S(1)} %add_add_fusion.1), channel_id=1, source_target_pairs={{0,4},{1,5},{2,6},{3,7},{4,0},{5,1},{6,2},{7,3},{8,12},{9,13},{10,... | collective-permute-start | bytes 147464 | tf_op jit(solution)/shard_map/ppermute | solution.py:42
  295.4 5.0 %collective-permute-start.49 = (f32[4,3072]{1,0:T(4,128)S(1)}, f32[4,3072]{1,0:T(4,128)S(1)}, u32[]{:S(2)}, u32[]{:S(2)}) collective-permute-start(f32[4,3072]{1,0:T(4,128)S(1)} %add_add_fusion.1), channel_id=1, source_target_pairs={{0,6},{1,7},{2,4},{3,5},{4,2},{5,3},{6,0},{7,1},{8,14},{9,15},{10,... | collective-permute-start | bytes 147464 | tf_op jit(solution)/shard_map/ppermute | solution.py:42
  (6 other events, 9.1 us)

commit v2 on v1

--- a/solution.py
+++ b/solution.py
@@ -226,8 +226,9 @@
 
 
 SEQUENCE = (
-    "A0", "A", "I", "A", "B0", "B", "A", "T", "A", "B", "C0", "A", "C", "B", "A", "C", "B", "A",
-    "C", "B", "C", "B", "X", "C", "S0", "B", "C", "S", "A", "BF", "S", "AF", "C", "SF", "C", "CF",
+    "A0", "A", "I", "A", "B0", "B", "A", "T", "A", "B", "C0", "A", "C", "B",
+    "A", "C", "B", "A", "C", "B", "C", "B", "X", "C", "S0", "B", "C", "A",
+    "S", "BF", "C", "S", "AF", "SF", "C", "CF",
 )
 
 

time: 311 us -> 315 us (1.013)
  transfers between devices with their start and end apart: 50 -> 50, of which waited for: 25 -> 23; matrix products, arithmetic and copies ran while one was open for 6% -> 7% of each run, Pallas kernels for 22% -> 22%
where the time goes in v2:
time: 315 us; the launch traced here: 309 us
  Pallas kernels  136 us (43%)
  waiting for transfers between devices  81.4 us (26%)
  starting transfers between devices  61.3 us (19%)
  other arithmetic  23.2 us (7%)
  local copies, waits for them, and re-layouts  5.86 us (2%)
    ppermute x50, waiting for transfers between devices, exchange(): return lax.ppermute(value, BOTH, pairs)  81.4 us
    ppermute x50, starting transfers between devices, exchange(): return lax.ppermute(value, BOTH, pairs)  61.3 us
    pallas_call x1, Pallas kernels, feed(): kernel_call(partial(feed_kernel, 1024), 'feed', 4 * tokens * width * hidd...  27.2 us
    pallas_call x1, Pallas kernels, inner_back(): kernel_call(partial(inner_back_kernel, rows), 'inner_back', 6 * tokens *...  26.9 us
    pallas_call x1, Pallas kernels, attend_back(): kernel_call(partial(attend_back_kernel, HEADS // 2), 'attend_back', 10 *...  23.7 us
    pallas_call x1, Pallas kernels, attend(): kernel_call(attend_kernel, 'attend', 2 * tokens * width * width * 4 + 4 *...  20.1 us
    pallas_call x1, Pallas kernels, outer_back(): kernel_call(partial(outer_back_kernel, min(count, 256), masks), 'outer_ba...  17.6 us
    pallas_call x3, Pallas kernels, finish(): kernel_call(partial(finish_kernel, plan), 'finish', 0, half * cols * 12,...  11.4 us
  transfers between devices with their start and end apart: 50, of which 23 were waited for; matrix products, arithmetic and copies ran while one was open for 7% of the time, Pallas kernels for 22%

profile of v2, /device:TPU:0, one launch (start us, length us, event | category | flops | bytes accessed | tf_op | source)
XLA Modules:
  0.0 309.5 jit_solution(1308805235507455904)
XLA Ops:
  0.6 20.1 %attend.1 = (bf16[1024,768]{1,0:T(8,128)(2,1)}, bf16[1024,768]{1,0:T(8,128)(2,1)}, bf16[1024,768]{1,0:T(8,128)(2,1)}, bf16[768,1024]{1,0:T(8,128)(2,1)}, f32[6,4...) custom-call(bf16[1024,768]{1,0:T(8,128)(2,1)} %x_ref.1, ...), custom_call_target="tpu_custom_call" | custom-call | flops 7247757312 | bytes 20971520 | tf_op jit(solution)/shard_map/attend/pallas_call | solution.py:340
  20.7 27.2 %feed.1 = (bf16[3072,1024]{1,0:T(8,128)(2,1)}, bf16[1024,3072]{1,0:T(8,128)(2,1)}, f32[1024,768]{1,0:T(8,128)}, f32[1024,1]{1,0:T(8,128)}, bf16[1024,768]{1,0:T(8,128)(2,1)}, /*index=5*/bf16[16,768]{1,0:T(8,128)(2,1)}) custom-call(f32[1024,768]{1,0:T(8,128)} %get-tuple-element.103.hat_ref.hat_hbm, bf16[1024,768]{1,0:T(8,128)(2,1)} %get-tuple-element.104.low_ref, ...), custom_call_target="tpu_custom_call" | custom-call | flops 9663676416 | bytes 31457280 | tf_op jit(solution)/shard_map/feed/pallas_call | solution.py:428
  47.9 3.1 collective-permute-start
  51.0 2.6 collective-permute-start.1
  54.4 1.9 collective-permute-done.1
  56.3 3.1 %collective-permute-done.2 = bf16[16,768]{1,0:T(8,128)(2,1)S(1)} collective-permute-done((bf16[16,768]{1,0:T(8,128)(2,1)}, bf16[16,768]{1,0:T(8,128)(2,1)S(1)}, u32[]{:S(2)}, u32[]{:S(2)}) %collective-permute-start.2) | collective-permute-done | bytes 24608 | tf_op jit(solution)/shard_map/ppermute | solution.py:42
  59.4 1.5 collective-permute-start.3
  60.9 1.5 collective-permute-start.4
  62.9 1.8 collective-permute-done.3
  64.7 1.2 collective-permute-done.4
  66.0 2.0 collective-permute-done.5
  70.7 17.6 %outer_back.1 = (f32[1,1]{1,0:T(1,128)}, f32[1,3072]{1,0:T(1,128)}, bf16[1536,768]{1,0:T(8,128)(2,1)}, bf16[1536,768]{1,0:T(8,128)(2,1)}, f32[1024,768]{1,0:T(8,128)}, /*index=5*/bf16[1024,768]{1,0:T(8,128)(2,1)}) custom-call(s32[2]{0:T(128)} %pad_add_fusion.info_ref, s32[512]{0:T(512)} %partner_ref.1, f32[1]{0:T(128)S(6)} %copy.73.cool_ref, ...), custom_call_target="tpu_custom_call" | custom-call | flops 4831838208 | bytes 20971520 | tf_op jit(solution)/shard_map/outer_back/pallas_call | solution.py:544
  88.5 4.6 %collective-permute-done.7 = bf16[1536,768]{1,0:T(8,128)(2,1)S(1)} collective-permute-done((bf16[1536,768]{1,0:T(8,128)(2,1)}, bf16[1536,768]{1,0:T(8,128)(2,1)S(1)}, u32[]{:S(2)}, u32[]{:S(2)}) %collective-permute-start.7) | collective-permute-done | bytes 2359328 | tf_op jit(solution)/shard_map/ppermute | solution.py:42
  93.2 2.3 convert_add_fusion.2
  96.2 26.9 %inner_back.1 = (bf16[2304,512]{1,0:T(8,128)(2,1)}, bf16[2304,512]{1,0:T(8,128)(2,1)}, f32[1,3072]{1,0:T(1,128)S(1)}, bf16[1024,768]{1,0:T(8,128)(2,1)S(1)}, bf1...) custom-call(s32[2]{0:T(128)S(1)} %copy-done.6, bf16[1024,768]{1,0:T(8,128)(2,1)S(1)} %copy-done.7, ...), custom_call_target="tpu_custom_call" | custom-call | flops 14495514624 | bytes 41943040 | tf_op jit(solution)/shard_map/inner_back/pallas_call | solution.py:643
  123.1 1.4 convert_add_fusion.5
  125.8 3.6 %collective-permute-done.9 = bf16[2304,512]{1,0:T(8,128)(2,1)} collective-permute-done((bf16[2304,512]{1,0:T(8,128)(2,1)}, bf16[2304,512]{1,0:T(8,128)(2,1)}, u32[]{:S(2)}, u32[]{:S(2)}) %collective-permute-start.9) | collective-permute-done | bytes 2359328 | tf_op jit(solution)/shard_map/ppermute | solution.py:42
  129.4 3.2 %add_convert_fusion.1 = (bf16[1152,512]{1,0:T(8,128)(2,1)S(1)}, f32[1152,512]{1,0:T(8,128)S(1)}) fusion(bf16[2304,512]{1,0:T(8,128)(2,1)} %collective-permute-done.9, s32[]{:T(128)S(6)} %select_n.445, bf16[2304,512]{1,0:T(8,128)(2,1)} %get-tuple-element.123, s32[]{:T(128)S(6)} %select_n.441), kind=kLoop, calls=%fused_computation.5 | loop fusion | flops 4128768 | bytes 8257544 | tf_op jit(solution)/shard_map/convert_element_type | solution.py:88
  132.7 1.4 collective-permute-start.10
  135.8 3.6 %collective-permute-start.14 = (bf16[96,768]{1,0:T(8,128)(2,1)S(1)}, bf16[96,768]{1,0:T(8,128)(2,1)S(1)}, u32[]{:S(2)}, u32[]{:S(2)}) collective-permute-start(bf16[96,768]{1,0:T(8,128)(2,1)S(1)} %get-tuple-element.241), channel_id=1, source_target_pairs={{0,24},{1,25},{2,26},{3,27},{4,28},{5,29},{6,30},{7,31},{8,16},{9,... | collective-permute-start | bytes 442376 | tf_op jit(solution)/shard_map/ppermute | solution.py:42
  139.4 23.7 %attend_back.1 = (bf16[1024,768]{1,0:T(8,128)(2,1)S(1)}, bf16[1024,768]{1,0:T(8,128)(2,1)S(1)}, bf16[1024,768]{1,0:T(8,128)(2,1)S(1)}, bf16[2,768,768]{2,1,0:T(8...) custom-call(s32[1]{0:T(128)} %bitcast.1.core_ref, bf16[768,1024]{1,0:T(8,128)(2,1)S(1)} %copy-done.11, ...), custom_call_target="tpu_custom_call" | custom-call | flops 9663676416 | bytes 31457280 | tf_op jit(solution)/shard_map/attend_back/pallas_call | solution.py:744
  163.3 1.8 add_convert_fusion.4
  166.3 3.6 %collective-permute-start.17 = (bf16[96,768]{1,0:T(8,128)(2,1)S(1)}, bf16[96,768]{1,0:T(8,128)(2,1)S(1)}, u32[]{:S(2)}, u32[]{:S(2)}) collective-permute-start(bf16[96,768]{1,0:T(8,128)(2,1)S(1)} %add_convert_fusion.14), channel_id=1, source_target_pairs={{0,24},{1,25},{2,26},{3,27},{4,28},{5,29},{6,30},{7,31},{8,16},{9,... | collective-permute-start | bytes 442376 | tf_op jit(solution)/shard_map/ppermute | solution.py:42
  171.0 2.0 collective-permute-done.19
  173.0 6.4 %collective-permute-done.18 = bf16[96,768]{1,0:T(8,128)(2,1)S(1)} collective-permute-done((bf16[96,768]{1,0:T(8,128)(2,1)S(1)}, bf16[96,768]{1,0:T(8,128)(2,1)S(1)}, u32[]{:S(2)}, u32[]{:S(2)}) %collective-permute-start.18) | collective-permute-done | bytes 147488 | tf_op jit(solution)/shard_map/ppermute | solution.py:42
  180.5 1.2 collective-permute-start.22
  181.6 2.8 convert_add_fusion
  185.2 1.9 add_convert_fusion.12
  187.0 7.5 %collective-permute-done.22 = bf16[384,768]{1,0:T(8,128)(2,1)} collective-permute-done((bf16[384,768]{1,0:T(8,128)(2,1)S(1)}, bf16[384,768]{1,0:T(8,128)(2,1)}, u32[]{:S(2)}, u32[]{:S(2)}) %collective-permute-start.22) | collective-permute-done | bytes 589856 | tf_op jit(solution)/shard_map/ppermute | solution.py:42
  194.5 1.2 constant_dynamic-update-slice_fusion.28
  195.8 1.2 broadcast_select_fusion.1
  197.0 1.7 collective-permute-start.27
  198.7 2.9 collective-permute-start.20
  201.6 2.4 collective-permute-start.24
  204.0 1.1 convert_add_fusion.3
  205.1 1.8 collective-permute-done.20
  207.0 4.7 %collective-permute-done.23 = bf16[144,512]{1,0:T(8,128)(2,1)S(1)} collective-permute-done((bf16[144,512]{1,0:T(8,128)(2,1)}, bf16[144,512]{1,0:T(8,128)(2,1)S(1)}, u32[]{:S(2)}, u32[]{:S(2)}) %collective-permute-start.23) | collective-permute-done | bytes 147488 | tf_op jit(solution)/shard_map/ppermute | solution.py:42
  212.7 2.2 collective-permute-start.29
  215.0 2.4 collective-permute-start.25
  217.3 3.2 %collective-permute-done.27 = bf16[768,768]{1,0:T(8,128)(2,1)} collective-permute-done((bf16[768,768]{1,0:T(8,128)(2,1)}, bf16[768,768]{1,0:T(8,128)(2,1)}, u32[]{:S(2)}, u32[]{:S(2)}) %collective-permute-start.27) | collective-permute-done | bytes 1179680 | tf_op jit(solution)/shard_map/ppermute | solution.py:42
  220.5 2.6 maximum_select_fusion.kept_ref
  223.2 3.2 %collective-permute-done.28 = bf16[144,512]{1,0:T(8,128)(2,1)S(1)} collective-permute-done((bf16[144,512]{1,0:T(8,128)(2,1)S(1)}, bf16[144,512]{1,0:T(8,128)(2,1)S(1)}, u32[]{:S(2)}, u32[]{:S(2)}) %collective-permute-start.28) | collective-permute-done | bytes 147488 | tf_op jit(solution)/shard_map/ppermute | solution.py:42
  226.8 1.6 collective-permute-start.30
  228.5 2.5 collective-permute-start.31
  231.0 2.3 collective-permute-start.33
  233.4 1.9 collective-permute-done.31
  235.3 8.0 %collective-permute-done.32 = bf16[96,768]{1,0:T(8,128)(2,1)S(1)} collective-permute-done((bf16[96,768]{1,0:T(8,128)(2,1)S(1)}, bf16[96,768]{1,0:T(8,128)(2,1)S(1)}, u32[]{:S(2)}, u32[]{:S(2)}) %collective-permute-start.32) | collective-permute-done | bytes 147488 | tf_op jit(solution)/shard_map/ppermute | solution.py:42
  243.4 2.6 collective-permute-start.36
  246.2 2.3 collective-permute-start.34
  249.7 8.7 %input_back.1 = f32[1024,768]{1,0:T(8,128)} custom-call(f32[1024,768]{1,0:T(8,128)} %get-tuple-element.163.first_ref, bf16[1024,768]{1,0:T(8,128)(2,1)} %copy-done, bf16[1024,768]{1,0:T(8,128)(2,1)} %copy-done.1, bf16[1024,768]{1,0:T(8,128)(2,1)} %copy-done.2, bf16[768,2304]{1,0:T(8,128)(2,1)} %refs_3_.1), custom_call_target="tpu_custom_call" | custom-call | flops 3623878656 | bytes 15728640 | tf_op jit(solution)/shard_map/input_back/pallas_call | solution.py:777
  258.8 1.9 collective-permute-start.37
  260.8 8.7 %collective-permute-done.38 = bf16[1152,512]{1,0:T(8,128)(2,1)S(1)} collective-permute-done((bf16[1152,512]{1,0:T(8,128)(2,1)S(1)}, bf16[1152,512]{1,0:T(8,128)(2,1)S(1)}, u32[]{:S(2)}, u32[]{:S(2)}) %collective-permute-start.38) | collective-permute-done | bytes 1179680 | tf_op jit(solution)/shard_map/ppermute | solution.py:42
  270.6 1.1 collective-permute-start.39
  271.7 1.2 collective-permute-start.47
  272.9 5.4 %collective-permute-done.41 = f32[4,3072]{1,0:T(4,128)S(1)} collective-permute-done((f32[4,3072]{1,0:T(4,128)S(1)}, f32[4,3072]{1,0:T(4,128)S(1)}, u32[]{:S(2)}, u32[]{:S(2)}) %collective-permute-start.41) | collective-permute-done | bytes 49184 | tf_op jit(solution)/shard_map/ppermute | solution.py:42
  278.3 3.8 %finish.3 = f32[768,3072]{1,0:T(8,128)} custom-call(s32[1]{0:T(128)} %bitcast.1.core_ref, bf16[2304,512]{1,0:T(8,128)(2,1)S(1)} %maximum_select_fusion.1.kept_ref, bf16[2304,512]{1,0:T(8,128)(2,1)S(1)} %collective-permute-done.40.got_ref), custom_call_target="tpu_custom_call" | custom-call | bytes 14155776 | tf_op jit(solution)/shard_map/finish/pallas_call | solution.py:808
  282.1 4.8 %collective-permute-done.39 = bf16[768,768]{1,0:T(8,128)(2,1)S(1)} collective-permute-done((bf16[768,768]{1,0:T(8,128)(2,1)S(1)}, bf16[768,768]{1,0:T(8,128)(2,1)S(1)}, u32[]{:S(2)}, u32[]{:S(2)}) %collective-permute-start.39) | collective-permute-done | bytes 1179680 | tf_op jit(solution)/shard_map/ppermute | solution.py:42
  287.7 1.3 collective-permute-start.43
  289.9 2.1 collective-permute-start.45
  292.0 4.0 %collective-permute-done.44 = f32[4,3072]{1,0:T(4,128)S(1)} collective-permute-done((f32[4,3072]{1,0:T(4,128)S(1)}, f32[4,3072]{1,0:T(4,128)S(1)}, u32[]{:S(2)}, u32[]{:S(2)}) %collective-permute-start.44) | collective-permute-done | bytes 49184 | tf_op jit(solution)/shard_map/ppermute | solution.py:42
  296.1 1.1 collective-permute-start.46
  297.2 2.0 collective-permute-start.48
  299.9 3.8 %finish.4 = f32[3072,768]{1,0:T(8,128)} custom-call(s32[1]{0:T(128)} %bitcast.1.core_ref, bf16[1536,768]{1,0:T(8,128)(2,1)S(1)} %maximum_select_fusion.kept_ref, bf16[1536,768]{1,0:T(8,128)(2,1)S(1)} %collective-permute-done.47.got_ref), custom_call_target="tpu_custom_call" | custom-call | bytes 14155776 | tf_op jit(solution)/shard_map/finish/pallas_call | solution.py:808
  305.4 3.9 %finish.5 = (f32[768,2304]{1,0:T(8,128)}, f32[768,768]{1,0:T(8,128)}) custom-call(s32[1]{0:T(128)} %bitcast.1.core_ref, bf16[1536,768]{1,0:T(8,128)(2,1)S(1)} %maximum_select_fusion.2.kept_ref, bf16[1536,768]{1,0:T(8,128)(2,1)S(1)} %collective-permute-done.42.got_ref), custom_call_target="tpu_custom_call" | custom-call | bytes 14155776 | tf_op jit(solution)/shard_map/finish/pallas_call | solution.py:808
  (148 shorter events, 20.3 us)
Async XLA Ops:
  47.9 6.5 %collective-permute-start = (bf16[16,768]{1,0:T(8,128)(2,1)}, bf16[16,768]{1,0:T(8,128)(2,1)S(1)}, u32[]{:S(2)}, u32[]{:S(2)}) collective-permute-start(bf16[16,768]{1,0:T(8,128)(2,1)} %get-tuple-element.105.own_ref), channel_id=1, source_target_pairs={{0,8},{1,9},{2,10},{3,11},{4,12},{5,13},{6,14},{7,15},{8,0},{9,1},... | collective-permute-start | bytes 73736 | tf_op jit(solution)/shard_map/ppermute | solution.py:42
  51.0 5.3 %collective-permute-start.1 = (bf16[16,768]{1,0:T(8,128)(2,1)}, bf16[16,768]{1,0:T(8,128)(2,1)S(1)}, u32[]{:S(2)}, u32[]{:S(2)}) collective-permute-start(bf16[16,768]{1,0:T(8,128)(2,1)} %get-tuple-element.105.own_ref), channel_id=1, source_target_pairs={{0,16},{1,17},{2,18},{3,19},{4,20},{5,21},{6,22},{7,23},{8,24},{9,... | collective-permute-start | bytes 73736 | tf_op jit(solution)/shard_map/ppermute | solution.py:42
  53.6 5.8 %collective-permute-start.2 = (bf16[16,768]{1,0:T(8,128)(2,1)}, bf16[16,768]{1,0:T(8,128)(2,1)S(1)}, u32[]{:S(2)}, u32[]{:S(2)}) collective-permute-start(bf16[16,768]{1,0:T(8,128)(2,1)} %get-tuple-element.105.own_ref), channel_id=1, source_target_pairs={{0,24},{1,25},{2,26},{3,27},{4,28},{5,29},{6,30},{7,31},{8,16},{9,... | collective-permute-start | bytes 73736 | tf_op jit(solution)/shard_map/ppermute | solution.py:42
  59.4 5.3 %collective-permute-start.3 = (bf16[64,768]{1,0:T(8,128)(2,1)S(1)}, bf16[64,768]{1,0:T(8,128)(2,1)S(1)}, u32[]{:S(2)}, u32[]{:S(2)}) collective-permute-start(bf16[64,768]{1,0:T(8,128)(2,1)S(1)} %get-tuple-element.257), channel_id=1, source_target_pairs={{0,2},{1,3},{2,0},{3,1},{4,6},{5,7},{6,4},{7,5},{8,10},{9,11},{10,... | collective-permute-start | bytes 294920 | tf_op jit(solution)/shard_map/ppermute | solution.py:42
  60.9 5.0 %collective-permute-start.4 = (bf16[64,768]{1,0:T(8,128)(2,1)S(1)}, bf16[64,768]{1,0:T(8,128)(2,1)S(1)}, u32[]{:S(2)}, u32[]{:S(2)}) collective-permute-start(bf16[64,768]{1,0:T(8,128)(2,1)S(1)} %get-tuple-element.257), channel_id=1, source_target_pairs={{0,4},{1,5},{2,6},{3,7},{4,0},{5,1},{6,2},{7,3},{8,12},{9,13},{10,... | collective-permute-start | bytes 294920 | tf_op jit(solution)/shard_map/ppermute | solution.py:42
  62.5 5.5 %collective-permute-start.5 = (bf16[64,768]{1,0:T(8,128)(2,1)S(1)}, bf16[64,768]{1,0:T(8,128)(2,1)S(1)}, u32[]{:S(2)}, u32[]{:S(2)}) collective-permute-start(bf16[64,768]{1,0:T(8,128)(2,1)S(1)} %get-tuple-element.257), channel_id=1, source_target_pairs={{0,6},{1,7},{2,4},{3,5},{4,2},{5,3},{6,0},{7,1},{8,14},{9,15},{10,... | collective-permute-start | bytes 294920 | tf_op jit(solution)/shard_map/ppermute | solution.py:42
  68.0 1.8 collective-permute-start.6
  88.3 4.8 %collective-permute-start.7 = (bf16[1536,768]{1,0:T(8,128)(2,1)}, bf16[1536,768]{1,0:T(8,128)(2,1)S(1)}, u32[]{:S(2)}, u32[]{:S(2)}) collective-permute-start(bf16[1536,768]{1,0:T(8,128)(2,1)} %get-tuple-element.114), channel_id=1, source_target_pairs={{0,1},{1,0},{2,3},{3,2},{4,5},{5,4},{6,7},{7,6},{8,9},{9,8},{10,11... | collective-permute-start | bytes 7077896 | tf_op jit(solution)/shard_map/ppermute | solution.py:42
  93.2 2.9 copy-start.3
  93.2 2.9 copy-start.4
  93.2 2.9 copy-start.6
  93.2 2.9 copy-start.7
  93.2 3.0 copy-start.12
  93.2 3.1 copy-start.13
  95.5 27.6 %collective-permute-start.8 = (bf16[768,768]{1,0:T(8,128)(2,1)S(1)}, bf16[768,768]{1,0:T(8,128)(2,1)S(1)}, u32[]{:S(2)}, u32[]{:S(2)}) collective-permute-start(bf16[768,768]{1,0:T(8,128)(2,1)S(1)} %get-tuple-element.227), channel_id=1, source_target_pairs={{0,2},{1,5},{2,0},{3,7},{4,6},{5,1},{6,4},{7,3},{8,10},{9,13},{10,... | collective-permute-start | bytes 3538952 | tf_op jit(solution)/shard_map/ppermute | solution.py:42
  124.5 4.9 %collective-permute-start.9 = (bf16[2304,512]{1,0:T(8,128)(2,1)}, bf16[2304,512]{1,0:T(8,128)(2,1)}, u32[]{:S(2)}, u32[]{:S(2)}) collective-permute-start(bf16[2304,512]{1,0:T(8,128)(2,1)} %get-tuple-element.127), channel_id=1, source_target_pairs={{0,1},{1,0},{2,3},{3,2},{4,5},{5,4},{6,7},{7,6},{8,9},{9,8},{10,11... | collective-permute-start | bytes 7077896 | tf_op jit(solution)/shard_map/ppermute | solution.py:42
  124.7 10.1 %collective-permute-start.11 = (bf16[384,768]{1,0:T(8,128)(2,1)}, bf16[384,768]{1,0:T(8,128)(2,1)S(1)}, u32[]{:S(2)}, u32[]{:S(2)}) collective-permute-start(bf16[384,768]{1,0:T(8,128)(2,1)} %get-tuple-element.233), channel_id=1, source_target_pairs={{0,4},{1,3},{2,6},{3,1},{4,0},{5,7},{6,2},{7,5},{8,12},{9,11},{10,... | collective-permute-start | bytes 1769480 | tf_op jit(solution)/shard_map/ppermute | solution.py:42
  129.4 5.4 %copy-start.15 = (f32[384,768]{1,0:T(8,128)S(1)}, f32[384,768]{1,0:T(8,128)}, u32[]{:S(2)}) copy-start(f32[384,768]{1,0:T(8,128)} %get-tuple-element.232) | copy-start | bytes 3538948
  129.4 9.9 %copy-start.9 = (bf16[1024,768]{1,0:T(8,128)(2,1)S(1)}, bf16[1024,768]{1,0:T(8,128)(2,1)}, u32[]{:S(2)}) copy-start(bf16[1024,768]{1,0:T(8,128)(2,1)} %get-tuple-element.134.k_ref) | copy-start | bytes 4718596
  129.4 9.9 %copy-start.10 = (bf16[1024,768]{1,0:T(8,128)(2,1)S(1)}, bf16[1024,768]{1,0:T(8,128)(2,1)}, u32[]{:S(2)}) copy-start(bf16[1024,768]{1,0:T(8,128)(2,1)} %get-tuple-element.135.v_ref) | copy-start | bytes 4718596
  129.4 9.9 %copy-start.11 = (bf16[768,1024]{1,0:T(8,128)(2,1)S(1)}, bf16[768,1024]{1,0:T(8,128)(2,1)}, u32[]{:S(2)}) copy-start(bf16[768,1024]{1,0:T(8,128)(2,1)} %get-tuple-element.130.x_t_ref) | copy-start | bytes 4718596
  132.7 6.7 %copy-start.5 = (s32[2,512]{1,0:T(2,128)S(1)}, s32[2,512]{1,0:T(2,128)}, u32[]{:S(2)}) copy-start(s32[2,512]{1,0:T(2,128)} %seg_ref.7) | copy-start | bytes 12292
  132.7 6.7 %copy-start.8 = (bf16[1024,768]{1,0:T(8,128)(2,1)S(1)}, bf16[1024,768]{1,0:T(8,128)(2,1)}, u32[]{:S(2)}) copy-start(bf16[1024,768]{1,0:T(8,128)(2,1)} %get-tuple-element.133.q_ref) | copy-start | bytes 4718596
  132.7 6.7 %copy-start.14 = (f32[6,4,512]{2,1,0:T(4,128)S(1)}, f32[6,4,512]{2,1,0:T(4,128)}, u32[]{:S(2)}) copy-start(f32[6,4,512]{2,1,0:T(4,128)} %get-tuple-element.132.lse_ref) | copy-start | bytes 147460
  132.7 30.6 %collective-permute-start.10 = (bf16[1152,512]{1,0:T(8,128)(2,1)S(1)}, bf16[1152,512]{1,0:T(8,128)(2,1)S(1)}, u32[]{:S(2)}, u32[]{:S(2)}) collective-permute-start(bf16[1152,512]{1,0:T(8,128)(2,1)S(1)} %get-tuple-element.224), channel_id=1, source_target_pairs={{0,2},{1,5},{2,0},{3,7},{4,6},{5,1},{6,4},{7,3},{8,10},{9,13},{10,... | collective-permute-start | bytes 3538952 | tf_op jit(solution)/shard_map/ppermute | solution.py:42
  134.9 28.3 %collective-permute-start.12 = (bf16[96,768]{1,0:T(8,128)(2,1)S(1)}, bf16[96,768]{1,0:T(8,128)(2,1)S(1)}, u32[]{:S(2)}, u32[]{:S(2)}) collective-permute-start(bf16[96,768]{1,0:T(8,128)(2,1)S(1)} %get-tuple-element.242), channel_id=1, source_target_pairs={{0,8},{1,9},{2,10},{3,11},{4,12},{5,13},{6,14},{7,15},{8,0},{9,1},... | collective-permute-start | bytes 442376 | tf_op jit(solution)/shard_map/ppermute | solution.py:42
  135.0 28.2 %collective-permute-start.13 = (bf16[96,768]{1,0:T(8,128)(2,1)S(1)}, bf16[96,768]{1,0:T(8,128)(2,1)S(1)}, u32[]{:S(2)}, u32[]{:S(2)}) collective-permute-start(bf16[96,768]{1,0:T(8,128)(2,1)S(1)} %get-tuple-element.240), channel_id=1, source_target_pairs={{0,16},{1,17},{2,18},{3,19},{4,20},{5,21},{6,22},{7,23},{8,24},{9,... | collective-permute-start | bytes 442376 | tf_op jit(solution)/shard_map/ppermute | solution.py:42
  135.8 27.4 %collective-permute-start.14 = (bf16[96,768]{1,0:T(8,128)(2,1)S(1)}, bf16[96,768]{1,0:T(8,128)(2,1)S(1)}, u32[]{:S(2)}, u32[]{:S(2)}) collective-permute-start(bf16[96,768]{1,0:T(8,128)(2,1)S(1)} %get-tuple-element.241), channel_id=1, source_target_pairs={{0,24},{1,25},{2,26},{3,27},{4,28},{5,29},{6,30},{7,31},{8,16},{9,... | collective-permute-start | bytes 442376 | tf_op jit(solution)/shard_map/ppermute | solution.py:42
  165.5 16.1 %collective-permute-start.16 = (bf16[1536,768]{1,0:T(8,128)(2,1)}, bf16[1536,768]{1,0:T(8,128)(2,1)}, u32[]{:S(2)}, u32[]{:S(2)}) collective-permute-start(bf16[1536,768]{1,0:T(8,128)(2,1)} %bitcast.4), channel_id=1, source_target_pairs={{0,1},{1,0},{2,3},{3,2},{4,5},{5,4},{6,7},{7,6},{8,9},{9,8},{10,11... | collective-permute-start | bytes 7077896 | tf_op jit(solution)/shard_map/ppermute | solution.py:42
  165.5 7.5 %collective-permute-start.19 = (bf16[96,768]{1,0:T(8,128)(2,1)S(1)}, bf16[96,768]{1,0:T(8,128)(2,1)S(1)}, u32[]{:S(2)}, u32[]{:S(2)}) collective-permute-start(bf16[96,768]{1,0:T(8,128)(2,1)S(1)} %add_convert_fusion.14), channel_id=1, source_target_pairs={{0,8},{1,9},{2,10},{3,11},{4,12},{5,13},{6,14},{7,15},{8,0},{9,1},... | collective-permute-start | bytes 442376 | tf_op jit(solution)/shard_map/ppermute | solution.py:42
  165.5 13.9 %collective-permute-start.18 = (bf16[96,768]{1,0:T(8,128)(2,1)S(1)}, bf16[96,768]{1,0:T(8,128)(2,1)S(1)}, u32[]{:S(2)}, u32[]{:S(2)}) collective-permute-start(bf16[96,768]{1,0:T(8,128)(2,1)S(1)} %add_convert_fusion.14), channel_id=1, source_target_pairs={{0,16},{1,17},{2,18},{3,19},{4,20},{5,21},{6,22},{7,23},{8,24},{9,... | collective-permute-start | bytes 442376 | tf_op jit(solution)/shard_map/ppermute | solution.py:42
  166.3 13.1 %collective-permute-start.17 = (bf16[96,768]{1,0:T(8,128)(2,1)S(1)}, bf16[96,768]{1,0:T(8,128)(2,1)S(1)}, u32[]{:S(2)}, u32[]{:S(2)}) collective-permute-start(bf16[96,768]{1,0:T(8,128)(2,1)S(1)} %add_convert_fusion.14), channel_id=1, source_target_pairs={{0,24},{1,25},{2,26},{3,27},{4,28},{5,29},{6,30},{7,31},{8,16},{9,... | collective-permute-start | bytes 442376 | tf_op jit(solution)/shard_map/ppermute | solution.py:42
  169.9 15.3 %collective-permute-start.15 = (bf16[576,512]{1,0:T(8,128)(2,1)}, bf16[576,512]{1,0:T(8,128)(2,1)}, u32[]{:S(2)}, u32[]{:S(2)}) collective-permute-start(bf16[576,512]{1,0:T(8,128)(2,1)} %get-tuple-element.230), channel_id=1, source_target_pairs={{0,4},{1,3},{2,6},{3,1},{4,0},{5,7},{6,2},{7,5},{8,12},{9,11},{10,... | collective-permute-start | bytes 1769480 | tf_op jit(solution)/shard_map/ppermute | solution.py:42
  180.5 14.1 %collective-permute-start.22 = (bf16[384,768]{1,0:T(8,128)(2,1)S(1)}, bf16[384,768]{1,0:T(8,128)(2,1)}, u32[]{:S(2)}, u32[]{:S(2)}) collective-permute-start(bf16[384,768]{1,0:T(8,128)(2,1)S(1)} %pad_maximum_fusion), channel_id=1, source_target_pairs={{0,4},{1,3},{2,6},{3,1},{4,0},{5,7},{6,2},{7,5},{8,12},{9,11},{10,... | collective-permute-start | bytes 1769480 | tf_op jit(solution)/shard_map/ppermute | solution.py:42
  184.5 19.5 %collective-permute-start.21 = (bf16[768,768]{1,0:T(8,128)(2,1)S(1)}, bf16[768,768]{1,0:T(8,128)(2,1)S(1)}, u32[]{:S(2)}, u32[]{:S(2)}) collective-permute-start(bf16[768,768]{1,0:T(8,128)(2,1)S(1)} %get-tuple-element.223), channel_id=1, source_target_pairs={{0,2},{1,5},{2,0},{3,7},{4,6},{5,1},{6,4},{7,3},{8,10},{9,13},{10,... | collective-permute-start | bytes 3538952 | tf_op jit(solution)/shard_map/ppermute | solution.py:42
  197.0 23.5 %collective-permute-start.27 = (bf16[768,768]{1,0:T(8,128)(2,1)}, bf16[768,768]{1,0:T(8,128)(2,1)}, u32[]{:S(2)}, u32[]{:S(2)}) collective-permute-start(bf16[768,768]{1,0:T(8,128)(2,1)} %broadcast_select_fusion.1), channel_id=1, source_target_pairs={{0,2},{1,5},{2,0},{3,7},{4,6},{5,1},{6,4},{7,3},{8,10},{9,13},{10,... | collective-permute-start | bytes 3538952 | tf_op jit(solution)/shard_map/ppermute | solution.py:42
  198.7 8.3 %collective-permute-start.20 = (bf16[144,512]{1,0:T(8,128)(2,1)}, bf16[144,512]{1,0:T(8,128)(2,1)S(1)}, u32[]{:S(2)}, u32[]{:S(2)}) collective-permute-start(bf16[144,512]{1,0:T(8,128)(2,1)} %get-tuple-element.239), channel_id=1, source_target_pairs={{0,8},{1,9},{2,10},{3,11},{4,12},{5,13},{6,14},{7,15},{8,0},{9,1},... | collective-permute-start | bytes 442376 | tf_op jit(solution)/shard_map/ppermute | solution.py:42
  201.6 10.0 %collective-permute-start.23 = (bf16[144,512]{1,0:T(8,128)(2,1)}, bf16[144,512]{1,0:T(8,128)(2,1)S(1)}, u32[]{:S(2)}, u32[]{:S(2)}) collective-permute-start(bf16[144,512]{1,0:T(8,128)(2,1)} %get-tuple-element.237), channel_id=1, source_target_pairs={{0,16},{1,17},{2,18},{3,19},{4,20},{5,21},{6,22},{7,23},{8,24},{9,... | collective-permute-start | bytes 442376 | tf_op jit(solution)/shard_map/ppermute | solution.py:42
  201.6 10.0 %collective-permute-start.24 = (bf16[144,512]{1,0:T(8,128)(2,1)}, bf16[144,512]{1,0:T(8,128)(2,1)S(1)}, u32[]{:S(2)}, u32[]{:S(2)}) collective-permute-start(bf16[144,512]{1,0:T(8,128)(2,1)} %get-tuple-element.238), channel_id=1, source_target_pairs={{0,24},{1,25},{2,26},{3,27},{4,28},{5,29},{6,30},{7,31},{8,16},{9,... | collective-permute-start | bytes 442376 | tf_op jit(solution)/shard_map/ppermute | solution.py:42
  205.1 18.0 %collective-permute-start.26 = (bf16[384,768]{1,0:T(8,128)(2,1)}, bf16[384,768]{1,0:T(8,128)(2,1)S(1)}, u32[]{:S(2)}, u32[]{:S(2)}) collective-permute-start(bf16[384,768]{1,0:T(8,128)(2,1)} %get-tuple-element.229), channel_id=1, source_target_pairs={{0,4},{1,3},{2,6},{3,1},{4,0},{5,7},{6,2},{7,5},{8,12},{9,11},{10,... | collective-permute-start | bytes 1769480 | tf_op jit(solution)/shard_map/ppermute | solution.py:42
  212.7 10.5 %collective-permute-start.29 = (bf16[144,512]{1,0:T(8,128)(2,1)S(1)}, bf16[144,512]{1,0:T(8,128)(2,1)S(1)}, u32[]{:S(2)}, u32[]{:S(2)}) collective-permute-start(bf16[144,512]{1,0:T(8,128)(2,1)S(1)} %add_convert_fusion.10), channel_id=1, source_target_pairs={{0,8},{1,9},{2,10},{3,11},{4,12},{5,13},{6,14},{7,15},{8,0},{9,1},... | collective-permute-start | bytes 442376 | tf_op jit(solution)/shard_map/ppermute | solution.py:42
  214.9 11.5 %collective-permute-start.28 = (bf16[144,512]{1,0:T(8,128)(2,1)S(1)}, bf16[144,512]{1,0:T(8,128)(2,1)S(1)}, u32[]{:S(2)}, u32[]{:S(2)}) collective-permute-start(bf16[144,512]{1,0:T(8,128)(2,1)S(1)} %add_convert_fusion.10), channel_id=1, source_target_pairs={{0,16},{1,17},{2,18},{3,19},{4,20},{5,21},{6,22},{7,23},{8,24},{9,... | collective-permute-start | bytes 442376 | tf_op jit(solution)/shard_map/ppermute | solution.py:42
  215.0 11.4 %collective-permute-start.25 = (bf16[144,512]{1,0:T(8,128)(2,1)S(1)}, bf16[144,512]{1,0:T(8,128)(2,1)S(1)}, u32[]{:S(2)}, u32[]{:S(2)}) collective-permute-start(bf16[144,512]{1,0:T(8,128)(2,1)S(1)} %add_convert_fusion.10), channel_id=1, source_target_pairs={{0,24},{1,25},{2,26},{3,27},{4,28},{5,29},{6,30},{7,31},{8,16},{9,... | collective-permute-start | bytes 442376 | tf_op jit(solution)/shard_map/ppermute | solution.py:42
  226.7 6.7 %copy-start.18 = (f32[1,3072]{1,0:T(1,128)S(1)}, f32[1,3072]{1,0:T(1,128)}, u32[]{:S(2)}) copy-start(f32[1,3072]{1,0:T(1,128)} %get-tuple-element.170) | copy-start | bytes 36868
  226.8 21.7 %collective-permute-start.30 = (bf16[576,512]{1,0:T(8,128)(2,1)S(1)}, bf16[576,512]{1,0:T(8,128)(2,1)S(1)}, u32[]{:S(2)}, u32[]{:S(2)}) collective-permute-start(bf16[576,512]{1,0:T(8,128)(2,1)S(1)} %pad_maximum_fusion.1), channel_id=1, source_target_pairs={{0,4},{1,3},{2,6},{3,1},{4,0},{5,7},{6,2},{7,5},{8,12},{9,11},{10,... | collective-permute-start | bytes 1769480 | tf_op jit(solution)/shard_map/ppermute | solution.py:42
  228.5 6.9 %collective-permute-start.31 = (bf16[96,768]{1,0:T(8,128)(2,1)S(1)}, bf16[96,768]{1,0:T(8,128)(2,1)S(1)}, u32[]{:S(2)}, u32[]{:S(2)}) collective-permute-start(bf16[96,768]{1,0:T(8,128)(2,1)S(1)} %get-tuple-element.236), channel_id=1, source_target_pairs={{0,8},{1,9},{2,10},{3,11},{4,12},{5,13},{6,14},{7,15},{8,0},{9,1},... | collective-permute-start | bytes 442376 | tf_op jit(solution)/shard_map/ppermute | solution.py:42
  231.0 12.3 %collective-permute-start.32 = (bf16[96,768]{1,0:T(8,128)(2,1)S(1)}, bf16[96,768]{1,0:T(8,128)(2,1)S(1)}, u32[]{:S(2)}, u32[]{:S(2)}) collective-permute-start(bf16[96,768]{1,0:T(8,128)(2,1)S(1)} %get-tuple-element.235), channel_id=1, source_target_pairs={{0,16},{1,17},{2,18},{3,19},{4,20},{5,21},{6,22},{7,23},{8,24},{9,... | collective-permute-start | bytes 442376 | tf_op jit(solution)/shard_map/ppermute | solution.py:42
  231.0 12.3 %collective-permute-start.33 = (bf16[96,768]{1,0:T(8,128)(2,1)S(1)}, bf16[96,768]{1,0:T(8,128)(2,1)S(1)}, u32[]{:S(2)}, u32[]{:S(2)}) collective-permute-start(bf16[96,768]{1,0:T(8,128)(2,1)S(1)} %get-tuple-element.234), channel_id=1, source_target_pairs={{0,24},{1,25},{2,26},{3,27},{4,28},{5,29},{6,30},{7,31},{8,16},{9,... | collective-permute-start | bytes 442376 | tf_op jit(solution)/shard_map/ppermute | solution.py:42
  243.4 15.0 %collective-permute-start.36 = (bf16[96,768]{1,0:T(8,128)(2,1)S(1)}, bf16[96,768]{1,0:T(8,128)(2,1)S(1)}, u32[]{:S(2)}, u32[]{:S(2)}) collective-permute-start(bf16[96,768]{1,0:T(8,128)(2,1)S(1)} %add_convert_fusion.6), channel_id=1, source_target_pairs={{0,8},{1,9},{2,10},{3,11},{4,12},{5,13},{6,14},{7,15},{8,0},{9,1},... | collective-permute-start | bytes 442376 | tf_op jit(solution)/shard_map/ppermute | solution.py:42
  246.1 12.3 %collective-permute-start.35 = (bf16[96,768]{1,0:T(8,128)(2,1)S(1)}, bf16[96,768]{1,0:T(8,128)(2,1)S(1)}, u32[]{:S(2)}, u32[]{:S(2)}) collective-permute-start(bf16[96,768]{1,0:T(8,128)(2,1)S(1)} %add_convert_fusion.6), channel_id=1, source_target_pairs={{0,16},{1,17},{2,18},{3,19},{4,20},{5,21},{6,22},{7,23},{8,24},{9,... | collective-permute-start | bytes 442376 | tf_op jit(solution)/shard_map/ppermute | solution.py:42
  246.2 12.2 %collective-permute-start.34 = (bf16[96,768]{1,0:T(8,128)(2,1)S(1)}, bf16[96,768]{1,0:T(8,128)(2,1)S(1)}, u32[]{:S(2)}, u32[]{:S(2)}) collective-permute-start(bf16[96,768]{1,0:T(8,128)(2,1)S(1)} %add_convert_fusion.6), channel_id=1, source_target_pairs={{0,24},{1,25},{2,26},{3,27},{4,28},{5,29},{6,30},{7,31},{8,16},{9,... | collective-permute-start | bytes 442376 | tf_op jit(solution)/shard_map/ppermute | solution.py:42
  248.8 20.6 %collective-permute-start.38 = (bf16[1152,512]{1,0:T(8,128)(2,1)S(1)}, bf16[1152,512]{1,0:T(8,128)(2,1)S(1)}, u32[]{:S(2)}, u32[]{:S(2)}) collective-permute-start(bf16[1152,512]{1,0:T(8,128)(2,1)S(1)} %broadcast_select_fusion.2), channel_id=1, source_target_pairs={{0,2},{1,5},{2,0},{3,7},{4,6},{5,1},{6,4},{7,3},{8,10},{9,13},{10,... | collective-permute-start | bytes 3538952 | tf_op jit(solution)/shard_map/ppermute | solution.py:42
  258.8 11.5 %collective-permute-start.37 = (bf16[384,768]{1,0:T(8,128)(2,1)S(1)}, bf16[384,768]{1,0:T(8,128)(2,1)S(1)}, u32[]{:S(2)}, u32[]{:S(2)}) collective-permute-start(bf16[384,768]{1,0:T(8,128)(2,1)S(1)} %pad_maximum_fusion.2), channel_id=1, source_target_pairs={{0,4},{1,3},{2,6},{3,1},{4,0},{5,7},{6,2},{7,5},{8,12},{9,11},{10,... | collective-permute-start | bytes 1769480 | tf_op jit(solution)/shard_map/ppermute | solution.py:42
  270.2 8.1 %collective-permute-start.40 = (bf16[2304,512]{1,0:T(8,128)(2,1)S(1)}, bf16[2304,512]{1,0:T(8,128)(2,1)S(1)}, u32[]{:S(2)}, u32[]{:S(2)}) collective-permute-start(bf16[2304,512]{1,0:T(8,128)(2,1)S(1)} %maximum_select_fusion.1.kept_ref), channel_id=1, source_target_pairs={{0,1},{1,0},{2,3},{3,2},{4,5},{5,4},{6,7},{7,6},{8,9},{9,8},{10,11... | collective-permute-start | bytes 7077896 | tf_op jit(solution)/shard_map/ppermute | solution.py:42
  270.6 16.3 %collective-permute-start.39 = (bf16[768,768]{1,0:T(8,128)(2,1)S(1)}, bf16[768,768]{1,0:T(8,128)(2,1)S(1)}, u32[]{:S(2)}, u32[]{:S(2)}) collective-permute-start(bf16[768,768]{1,0:T(8,128)(2,1)S(1)} %broadcast_select_fusion), channel_id=1, source_target_pairs={{0,2},{1,5},{2,0},{3,7},{4,6},{5,1},{6,4},{7,3},{8,10},{9,13},{10,... | collective-permute-start | bytes 3538952 | tf_op jit(solution)/shard_map/ppermute | solution.py:42
  271.7 28.2 %collective-permute-start.47 = (bf16[1536,768]{1,0:T(8,128)(2,1)S(1)}, bf16[1536,768]{1,0:T(8,128)(2,1)S(1)}, u32[]{:S(2)}, u32[]{:S(2)}) collective-permute-start(bf16[1536,768]{1,0:T(8,128)(2,1)S(1)} %maximum_select_fusion.kept_ref), channel_id=1, source_target_pairs={{0,1},{1,0},{2,3},{3,2},{4,5},{5,4},{6,7},{7,6},{8,9},{9,8},{10,11... | collective-permute-start | bytes 7077896 | tf_op jit(solution)/shard_map/ppermute | solution.py:42
  272.9 5.4 %collective-permute-start.41 = (f32[4,3072]{1,0:T(4,128)S(1)}, f32[4,3072]{1,0:T(4,128)S(1)}, u32[]{:S(2)}, u32[]{:S(2)}) collective-permute-start(f32[4,3072]{1,0:T(4,128)S(1)} %pad_maximum_fusion.3), channel_id=1, source_target_pairs={{0,1},{1,0},{2,3},{3,2},{4,5},{5,4},{6,7},{7,6},{8,9},{9,8},{10,11... | collective-permute-start | bytes 147464 | tf_op jit(solution)/shard_map/ppermute | solution.py:42
  287.5 17.9 %collective-permute-start.42 = (bf16[1536,768]{1,0:T(8,128)(2,1)S(1)}, bf16[1536,768]{1,0:T(8,128)(2,1)S(1)}, u32[]{:S(2)}, u32[]{:S(2)}) collective-permute-start(bf16[1536,768]{1,0:T(8,128)(2,1)S(1)} %maximum_select_fusion.2.kept_ref), channel_id=1, source_target_pairs={{0,1},{1,0},{2,3},{3,2},{4,5},{5,4},{6,7},{7,6},{8,9},{9,8},{10,11... | collective-permute-start | bytes 7077896 | tf_op jit(solution)/shard_map/ppermute | solution.py:42
  287.7 4.4 %collective-permute-start.43 = (f32[4,3072]{1,0:T(4,128)S(1)}, f32[4,3072]{1,0:T(4,128)S(1)}, u32[]{:S(2)}, u32[]{:S(2)}) collective-permute-start(f32[4,3072]{1,0:T(4,128)S(1)} %add.315), channel_id=1, source_target_pairs={{0,8},{1,9},{2,10},{3,11},{4,12},{5,13},{6,14},{7,15},{8,0},{9,1},... | collective-permute-start | bytes 147464 | tf_op jit(solution)/shard_map/ppermute | solution.py:42
  288.9 7.1 %collective-permute-start.44 = (f32[4,3072]{1,0:T(4,128)S(1)}, f32[4,3072]{1,0:T(4,128)S(1)}, u32[]{:S(2)}, u32[]{:S(2)}) collective-permute-start(f32[4,3072]{1,0:T(4,128)S(1)} %add.315), channel_id=1, source_target_pairs={{0,16},{1,17},{2,18},{3,19},{4,20},{5,21},{6,22},{7,23},{8,24},{9,... | collective-permute-start | bytes 147464 | tf_op jit(solution)/shard_map/ppermute | solution.py:42
  289.9 6.1 %collective-permute-start.45 = (f32[4,3072]{1,0:T(4,128)S(1)}, f32[4,3072]{1,0:T(4,128)S(1)}, u32[]{:S(2)}, u32[]{:S(2)}) collective-permute-start(f32[4,3072]{1,0:T(4,128)S(1)} %add.315), channel_id=1, source_target_pairs={{0,24},{1,25},{2,26},{3,27},{4,28},{5,29},{6,30},{7,31},{8,16},{9,... | collective-permute-start | bytes 147464 | tf_op jit(solution)/shard_map/ppermute | solution.py:42
  296.1 7.6 %collective-permute-start.46 = (f32[4,3072]{1,0:T(4,128)S(1)}, f32[4,3072]{1,0:T(4,128)S(1)}, u32[]{:S(2)}, u32[]{:S(2)}) collective-permute-start(f32[4,3072]{1,0:T(4,128)S(1)} %add_add_fusion.1), channel_id=1, source_target_pairs={{0,2},{1,3},{2,0},{3,1},{4,6},{5,7},{6,4},{7,5},{8,10},{9,11},{10,... | collective-permute-start | bytes 147464 | tf_op jit(solution)/shard_map/ppermute | solution.py:42
  297.2 6.5 %collective-permute-start.48 = (f32[4,3072]{1,0:T(4,128)S(1)}, f32[4,3072]{1,0:T(4,128)S(1)}, u32[]{:S(2)}, u32[]{:S(2)}) collective-permute-start(f32[4,3072]{1,0:T(4,128)S(1)} %add_add_fusion.1), channel_id=1, source_target_pairs={{0,4},{1,5},{2,6},{3,7},{4,0},{5,1},{6,2},{7,3},{8,12},{9,13},{10,... | collective-permute-start | bytes 147464 | tf_op jit(solution)/shard_map/ppermute | solution.py:42
  299.1 5.0 %collective-permute-start.49 = (f32[4,3072]{1,0:T(4,128)S(1)}, f32[4,3072]{1,0:T(4,128)S(1)}, u32[]{:S(2)}, u32[]{:S(2)}) collective-permute-start(f32[4,3072]{1,0:T(4,128)S(1)} %add_add_fusion.1), channel_id=1, source_target_pairs={{0,6},{1,7},{2,4},{3,5},{4,2},{5,3},{6,0},{7,1},{8,14},{9,15},{10,... | collective-permute-start | bytes 147464 | tf_op jit(solution)/shard_map/ppermute | solution.py:42
  (6 other events, 9.1 us)
